TPU v7x, 256 devices: a whole 4x4x8 slice. The times are simulated.
256 devices in a mesh: seq: 64 (over z, x, core), chan: 4 (over y).
Axes of the slice: x: 4, y: 4, z: 8, core: 2. Of those that a mesh axis runs over, the one named last changes fastest.
Arguments:
- q_in: bfloat16 [4096, 8192], P('chan', 'seq'), may hold values from -6 to 6
- k_in: bfloat16 [4096, 8192], P('chan', 'seq'), may hold values from -6 to 6
- v_in: bfloat16 [4096, 8192], P('chan', 'seq'), may hold values from -6 to 6
- cotangent: bfloat16 [4096, 8192], P('chan', 'seq'), may hold values from -6 to 6
- taps_short: float32 [4096, 7], P('chan'), may hold values from -2 to 2
- residues: float32 [1024, 16], replicated, may hold values from -1.5 to 1.5
- rates: float32 [1024, 16], replicated, may hold values from 3.0517578e-05 to 0.03
Outputs:
- grad_q: bfloat16 [4096, 8192], P('chan', 'seq')
- grad_k: bfloat16 [4096, 8192], P('chan', 'seq')
- grad_v: bfloat16 [4096, 8192], P('chan', 'seq')
- grad_short: float32 [4096, 7], P('chan')
- grad_residues: float32 [1024, 16], replicated
All inputs are finite; a program needn't handle non-finite values.
Results may differ from a plain program's by a relative error of at most 0.008.
Values may be sent and summed in bfloat16 or wider, within the bound.
No kernel may reach another device: no remote copies, remote signals or barrier semaphores. Data moves between devices by JAX's collectives and lax.ppermute only.
A program may use at most 128 MiB of HBM per device.

v0:
```python
import math

import jax
import jax.numpy as jnp
from jax import lax
from jax.sharding import PartitionSpec as P

HIGHEST = lax.Precision.HIGHEST


def from_behind(value, axis, steps):
    count = lax.axis_size(axis)
    initial, last = (max(0, -steps), min(count, count - steps))
    return lax.ppermute(value, axis, [(source, source + steps) for source in range(initial, last)])


def tables(rows, cols, modulus):
    left = lax.broadcasted_iota(jnp.int32, (rows, cols), 0)
    right = lax.broadcasted_iota(jnp.int32, (rows, cols), 1)
    angle = (left * right % modulus).astype(jnp.float32) * (2.0 * math.pi / modulus)
    return (jnp.cos(angle), jnp.sin(angle))


def twiddle_table(first, second, modulus):
    angle = (first[:, None] * second[None, :] % modulus).astype(jnp.float32) * (
        2.0 * math.pi / modulus
    )
    return (jnp.cos(angle), jnp.sin(angle))


def rotate(real_part, imag_part, cosine, sine, sign):
    return (
        real_part * cosine - sign * imag_part * sine,
        imag_part * cosine + sign * real_part * sine,
    )


def transform(form, real_part, imag_part, cosine, sine, sign):
    real_cos = jnp.einsum(form, real_part, cosine, precision=HIGHEST)
    imag_sin = jnp.einsum(form, imag_part, sine, precision=HIGHEST)
    imag_cos = jnp.einsum(form, imag_part, cosine, precision=HIGHEST)
    real_sin = jnp.einsum(form, real_part, sine, precision=HIGHEST)
    return (real_cos - sign * imag_sin, imag_cos + sign * real_sin)


def short_filter(padded_keys, taps_short, count):
    result = taps_short[:, 0:1] * padded_keys[:, 8 : 8 + count]
    for offset in range(1, 7):
        result = (
            result
            + taps_short[:, offset : offset + 1] * padded_keys[:, 8 - offset : 8 - offset + count]
        )
    return result


def forward_spectra(signals, shard_index, shard_count):
    count_sig, channels, seq_dev = signals.shape
    width_a = 2 * shard_count
    block = seq_dev // shard_count
    modulus = width_a * seq_dev
    first_len = min(128, seq_dev)
    second_len = seq_dev // first_len
    spread = lax.all_to_all(
        signals.reshape(count_sig, channels, 1, seq_dev),
        "seq",
        split_axis=3,
        concat_axis=2,
        tiled=True,
    )
    cos_a, sin_a = tables(shard_count, width_a, width_a)
    real_part = jnp.einsum("scab,ak->sckb", spread, cos_a, precision=HIGHEST)
    imag_part = -jnp.einsum("scab,ak->sckb", spread, sin_a, precision=HIGHEST)
    positions = shard_index * block + jnp.arange(block, dtype=jnp.int32)
    cos_t, sin_t = twiddle_table(jnp.arange(width_a, dtype=jnp.int32), positions, modulus)
    real_part, imag_part = rotate(real_part, imag_part, cos_t, sin_t, -1.0)
    real_part, imag_part = (
        lax.all_to_all(real_part, "seq", split_axis=2, concat_axis=3, tiled=True),
        lax.all_to_all(imag_part, "seq", split_axis=2, concat_axis=3, tiled=True),
    )
    real_part = real_part.reshape(count_sig, channels, 2, first_len, second_len)
    imag_part = imag_part.reshape(count_sig, channels, 2, first_len, second_len)
    cos_one, sin_one = tables(first_len, first_len, first_len)
    real_part, imag_part = transform(
        "scjab,ak->scjkb", real_part, imag_part, cos_one, sin_one, -1.0
    )
    cos_mid, sin_mid = twiddle_table(
        jnp.arange(first_len, dtype=jnp.int32), jnp.arange(second_len, dtype=jnp.int32), seq_dev
    )
    real_part, imag_part = rotate(real_part, imag_part, cos_mid, sin_mid, -1.0)
    cos_two, sin_two = tables(second_len, second_len, second_len)
    return transform("scjkb,bm->scjkm", real_part, imag_part, cos_two, sin_two, -1.0)


def inverse_partial(real_part, imag_part, shard_index, shard_count):
    count_sig, channels, pair, first_len, second_len = real_part.shape
    seq_dev = first_len * second_len
    width_a = 2 * shard_count
    block = seq_dev // shard_count
    modulus = width_a * seq_dev
    cos_two, sin_two = tables(second_len, second_len, second_len)
    real_part, imag_part = transform("scjkm,mb->scjkb", real_part, imag_part, cos_two, sin_two, 1.0)
    cos_mid, sin_mid = twiddle_table(
        jnp.arange(first_len, dtype=jnp.int32), jnp.arange(second_len, dtype=jnp.int32), seq_dev
    )
    real_part, imag_part = rotate(real_part, imag_part, cos_mid, sin_mid, 1.0)
    cos_one, sin_one = tables(first_len, first_len, first_len)
    real_part, imag_part = transform("scjkb,ka->scjab", real_part, imag_part, cos_one, sin_one, 1.0)
    real_part = real_part.reshape(count_sig, channels, 2, seq_dev)
    imag_part = imag_part.reshape(count_sig, channels, 2, seq_dev)
    real_part, imag_part = (
        lax.all_to_all(
            real_part.astype(jnp.bfloat16), "seq", split_axis=3, concat_axis=2, tiled=True
        ).astype(real_part.dtype),
        lax.all_to_all(
            imag_part.astype(jnp.bfloat16), "seq", split_axis=3, concat_axis=2, tiled=True
        ).astype(imag_part.dtype),
    )
    positions = shard_index * block + jnp.arange(block, dtype=jnp.int32)
    cos_t, sin_t = twiddle_table(jnp.arange(width_a, dtype=jnp.int32), positions, modulus)
    real_part, imag_part = rotate(real_part, imag_part, cos_t, sin_t, 1.0)
    cos_a, sin_a = tables(width_a, shard_count, width_a)
    return (real_part, imag_part, cos_a, sin_a)


def spectral_long(gated, grad_z, residues, rates, shard_index, shard_count):
    channels, seq_dev = gated.shape
    seq_len = seq_dev * shard_count
    modulus = 2 * seq_len
    width_a = 2 * shard_count
    first_len = min(128, seq_dev)
    second_len = seq_dev // first_len
    spec_real, spec_imag = forward_spectra(jnp.stack([gated, grad_z]), shard_index, shard_count)
    gated_r, grad_r = (spec_real[0], spec_real[1])
    gated_i, grad_i = (spec_imag[0], spec_imag[1])
    pair_idx = lax.broadcasted_iota(jnp.int32, (2, first_len, second_len), 0)
    low_idx = lax.broadcasted_iota(jnp.int32, (2, first_len, second_len), 1)
    high_idx = lax.broadcasted_iota(jnp.int32, (2, first_len, second_len), 2)
    freq = 2 * shard_index + pair_idx + width_a * (low_idx + first_len * high_idx)
    mirror = jnp.minimum(freq, modulus - freq)
    sign_flip = jnp.where(freq > modulus - freq, -1.0, 1.0)
    sine_freq = jnp.sin(mirror.astype(jnp.float32) * (2.0 * math.pi / modulus)) * sign_flip
    half_sine = jnp.sin(mirror.astype(jnp.float32) * (math.pi / modulus))
    half_square = 2.0 * half_sine * half_sine
    odd_freq = freq % 2 == 1
    cross_r = grad_r * gated_r + grad_i * gated_i
    cross_i = grad_i * gated_r - grad_r * gated_i
    rate_b = rates[:, :, None, None, None]
    decay_one = jnp.exp(-rate_b)
    weight_b = jnp.sqrt(-jnp.expm1(-2.0 * rate_b))
    numer = jnp.where(
        odd_freq[None, None], 1.0 + jnp.exp(-rate_b * seq_len), -jnp.expm1(-rate_b * seq_len)
    )
    denom_r = -jnp.expm1(-rate_b) + decay_one * half_square[None, None]
    denom_i = decay_one * sine_freq[None, None]
    denom_sq = denom_r * denom_r + denom_i * denom_i
    mode_r = numer * denom_r / denom_sq
    mode_i = -numer * denom_i / denom_sq
    scaled_b = residues[:, :, None, None, None] * weight_b
    kern_r = jnp.sum(scaled_b * mode_r, axis=1)
    kern_i = jnp.sum(scaled_b * mode_i, axis=1)
    weight_cp = jnp.sqrt(-jnp.expm1(-2.0 * rates))
    pole_part = (
        weight_cp
        * jnp.sum(cross_r[:, None] * mode_r + cross_i[:, None] * mode_i, axis=(2, 3, 4))
        / modulus
    )
    out_r = gated_r * kern_r - gated_i * kern_i
    out_i = gated_r * kern_i + gated_i * kern_r
    back_r = grad_r * kern_r + grad_i * kern_i
    back_i = grad_i * kern_r - grad_r * kern_i
    part_r, part_i, cos_a, sin_a = inverse_partial(
        jnp.stack([out_r, back_r]), jnp.stack([out_i, back_i]), shard_index, shard_count
    )
    finals = jnp.einsum("sckb,ka->scab", part_r, cos_a, precision=HIGHEST) - jnp.einsum(
        "sckb,ka->scab", part_i, sin_a, precision=HIGHEST
    )
    returned = lax.all_to_all(finals, "seq", split_axis=2, concat_axis=3, tiled=True).reshape(
        2, channels, seq_dev
    ) * (1.0 / modulus)
    return (returned[0], returned[1], pole_part)


def per_device(q_in, k_in, v_in, cotangent, taps_short, residues, rates):
    channels, seq_dev = q_in.shape
    shard_count = lax.axis_size("seq")
    shard_index = lax.axis_index("seq")
    seq_len = seq_dev * shard_count
    scale_grad = seq_len ** (-0.5)
    key_data = k_in.astype(jnp.float32)
    value_data = v_in.astype(jnp.float32)
    queries = q_in.astype(jnp.float32)
    grads_out = cotangent.astype(jnp.float32)
    key_rim = from_behind(k_in[:, -8:], "seq", 1).astype(jnp.float32)
    padded_keys = jnp.concatenate([key_rim, key_data], axis=1)
    gate = short_filter(padded_keys, taps_short, seq_dev)
    gated = gate * value_data
    grad_z = grads_out * queries
    long_out, long_grad, pole_part = spectral_long(
        gated, grad_z, residues, rates, shard_index, shard_count
    )
    grad_q = (grads_out * long_out).astype(jnp.bfloat16)
    grad_v = (long_grad * gate).astype(jnp.bfloat16)
    grad_gate = long_grad * value_data
    gate_head = from_behind(grad_gate[:, :8].astype(jnp.bfloat16), "seq", -1).astype(jnp.float32)
    gate_ext = jnp.concatenate([grad_gate, gate_head], axis=1)
    grad_k = taps_short[:, 0:1] * gate_ext[:, 0:seq_dev]
    for offset in range(1, 7):
        grad_k = (
            grad_k + taps_short[:, offset : offset + 1] * gate_ext[:, offset : offset + seq_dev]
        )
    grad_k = grad_k.astype(jnp.bfloat16)
    short_part = jnp.stack(
        [
            jnp.sum(grad_gate * padded_keys[:, 8 - offset : 8 - offset + seq_dev], axis=1)
            for offset in range(7)
        ],
        axis=1,
    )
    short_sum = lax.psum(short_part, "seq")
    pole_sum = lax.psum(pole_part, ("seq", "chan"))
    return (grad_q, grad_k, grad_v, short_sum * scale_grad, pole_sum * scale_grad)


def solution(mesh):
    in_specs = (
        P("chan", "seq"),
        P("chan", "seq"),
        P("chan", "seq"),
        P("chan", "seq"),
        P("chan", None),
        P(),
        P(),
    )
    out_specs = (P("chan", "seq"), P("chan", "seq"), P("chan", "seq"), P("chan", None), P())
    return jax.shard_map(
        per_device, mesh=mesh, in_specs=in_specs, out_specs=out_specs, check_vma=False
    )
```

profile of v0, /device:TPU:1, one launch (start us, length us, event | category | flops | bytes accessed | tf_op | source)
XLA Modules:
  0.0 855.8 jit_solution(3213359760369631879)
XLA Ops:
  8.3 4.5 collective-permute-start
  15.5 1.3 fusion.31
  17.0 1.8 copy.167
  18.8 11.7 %all-to-all-start = ((f32[2,1024,1,128]{1,0,2,3:T(2,128)}), f32[2,1024,1,128]{1,0,2,3:T(2,128)S(1)}, u32[]{:S(2)}, u32[]{:S(2)}) async-start(f32[2,1024,1,128]{1,0,2,3:T(2,128)} %copy.167), calls=%async_computation | async-start | bytes 2097152 | tf_op jit(solution)/shard_map/all_to_all | solution.py:63
  30.6 27.9 %all-to-all-done = f32[2,1024,1,128]{1,0,2,3:T(2,128)S(1)} async-done(((f32[2,1024,1,128]{1,0,2,3:T(2,128)}), f32[2,1024,1,128]{1,0,2,3:T(2,128)S(1)}, u32[]{:S(2)}, u32[]{:S(2)}) %all-to-all-start) | async-done | bytes 1048608 | tf_op jit(solution)/shard_map/all_to_all | solution.py:63
  58.5 2.4 fusion.23
  60.9 4.2 subtract_bitcast_fusion
  65.1 3.0 copy.170
  68.1 6.8 all-to-all-start.1
  74.9 4.5 copy.173
  79.4 45.0 %all-to-all-done.1 = f32[2,1024,128,2]{1,3,0,2:T(2,128)S(1)} async-done(((f32[2,1024,128,2]{1,3,0,2:T(2,128)}), f32[2,1024,128,2]{1,3,0,2:T(2,128)S(1)}, u32[]{:S(2)}, u32[]{:S(2)}) %all-to-all-start.1) | async-done | bytes 2097184 | tf_op jit(solution)/shard_map/all_to_all | solution.py:77
  124.4 7.2 all-to-all-start.2
  137.0 3.0 copy.171
  140.0 2.8 copy.172
  142.8 3.5 fusion.66
  146.2 35.0 %all-to-all-done.2 = f32[2,1024,128,2]{1,3,0,2:T(2,128)} async-done(((f32[2,1024,128,2]{1,3,0,2:T(2,128)}), f32[2,1024,128,2]{1,3,0,2:T(2,128)}, u32[]{:S(2)}, u32[]{:S(2)}) %all-to-all-start.2) | async-done | bytes 2097184 | tf_op jit(solution)/shard_map/all_to_all | solution.py:78
  181.2 4.5 copy.174
  185.8 3.2 copy.175
  189.0 2.1 fusion.64
  191.1 2.3 multiply_subtract_fusion.3
  193.4 2.8 fusion.3
  196.2 1.9 add_bitcast_fusion.1
  198.2 1.5 copy.202
  199.7 2.3 copy.203
  202.0 40.9 %multiply_reduce_fusion.1 = (f32[1024,2,128]{2,1,0:T(2,128)}, f32[1024,2,128]{2,1,0:T(2,128)}, f32[1024,16]{1,0:T(8,128)}) fusion(f32[1024,16]{1,0:T(8,128)} %copy.178, f32[2,128]{1,0:T(2,128)S(1)} %get-tuple-element.67, f32[2,128]{1,0:T(2,128)S(1)} %get-tuple-element.66, f32[1024,16]{1,0:T(8,128)} %copy.182, f32[1024,16]{1,0:T(8,128)} %copy.181, ...), kind=kLoop, calls=%fused_computation.9 | loop fusion | flops 83345408 | bytes 4589824 | tf_op jit(solution)/shard_map/reduce_sum | solution.py:159
  242.8 1.5 copy.183
  244.3 2.4 copy.185
  246.8 2.1 fusion.18
  250.5 2.1 fusion.27
  252.6 2.2 fusion.10
  254.8 2.1 copy.191
  256.9 7.0 all-to-all-start.3
  263.9 3.8 fusion.28
  267.8 2.2 fusion.11
  270.0 2.1 copy.196
  272.1 19.8 %all-to-all-done.3 = bf16[2,1024,2,128]{1,2,0,3:T(2,128)(2,1)S(1)} async-done(((bf16[2,1024,2,128]{1,2,0,3:T(2,128)(2,1)}), bf16[2,1024,2,128]{1,2,0,3:T(2,128)(2,1)S(1)}, u32[]{:S(2)}, u32[]{:S(2)}) %all-to-all-start.3) | async-done | bytes 1048608 | tf_op jit(solution)/shard_map/all_to_all | solution.py:111
  291.9 7.0 all-to-all-start.4
  300.6 26.0 %all-to-all-done.4 = bf16[2,1024,2,128]{1,2,0,3:T(2,128)(2,1)} async-done(((bf16[2,1024,2,128]{1,2,0,3:T(2,128)(2,1)}), bf16[2,1024,2,128]{1,2,0,3:T(2,128)(2,1)}, u32[]{:S(2)}, u32[]{:S(2)}) %all-to-all-start.4) | async-done | bytes 1048608 | tf_op jit(solution)/shard_map/all_to_all | solution.py:114
  326.6 2.0 copy.197
  328.7 2.2 multiply_subtract_fusion
  330.9 1.9 fusion.6
  332.8 1.9 fusion.15
  334.8 1.8 copy.201
  336.6 6.5 all-to-all-start.5
  344.0 245.9 %all-reduce.2.cloned.1.call-done = f32[1024,16]{0,1:T(8,128)} async-done(((f32[1024,16]{0,1:T(8,128)}), f32[1024,16]{0,1:T(8,128)}) %all-reduce.2.cloned.1.call-update) | async-done | bytes 65552 | tf_op jit(solution)/shard_map/psum | solution.py:220
  590.0 1.5 broadcast_multiply_fusion.1
  594.6 242.4 %psum.14 = f32[1024,7]{0,1:T(8,128)S(1)} all-reduce(f32[1024,7]{0,1:T(8,128)S(1)} %stack.55), channel_id=1, replica_groups=mesh['seq'=64,'chan'=4] {'seq'}, use_global_device_ids=true, to_apply=%region_9.10 | all-reduce | flops 7168 | bytes 57344 | tf_op jit(solution)/shard_map/psum | solution.py:219
  837.0 7.5 collective-permute-start.1
  (93 shorter events, 20.5 us)
Async XLA Ops:
  7.2 8.1 copy-start.22
  7.2 8.1 copy-start.20
  8.3 7.2 collective-permute-start
  13.9 1.3 copy-start.10
  15.3 1.6 copy-start.8
  15.5 3.3 copy-start.12
  18.8 39.7 %all-to-all-start = ((f32[2,1024,1,128]{1,0,2,3:T(2,128)}), f32[2,1024,1,128]{1,0,2,3:T(2,128)S(1)}, u32[]{:S(2)}, u32[]{:S(2)}) async-start(f32[2,1024,1,128]{1,0,2,3:T(2,128)} %copy.167), calls=%async_computation | async-start | bytes 2097152 | tf_op jit(solution)/shard_map/all_to_all | solution.py:63
  68.1 56.3 %all-to-all-start.1 = ((f32[2,1024,128,2]{1,3,0,2:T(2,128)}), f32[2,1024,128,2]{1,3,0,2:T(2,128)S(1)}, u32[]{:S(2)}, u32[]{:S(2)}) async-start(f32[2,1024,128,2]{1,3,0,2:T(2,128)} %copy.170), calls=%async_computation.1 | async-start | bytes 4194304 | tf_op jit(solution)/shard_map/all_to_all | solution.py:77
  79.4 52.2 %copy-start.18 = (f32[1024,16]{0,1:T(8,128)S(1)}, f32[1024,16]{0,1:T(8,128)}, u32[]{:S(2)}) copy-start(f32[1024,16]{0,1:T(8,128)} %param.13) | copy-start | bytes 196612
  79.4 52.2 %copy-start.21 = (f32[1024,16]{0,1:T(8,128)S(1)}, f32[1024,16]{0,1:T(8,128)}, u32[]{:S(2)}) copy-start(f32[1024,16]{0,1:T(8,128)} %param.12) | copy-start | bytes 196612
  124.4 56.8 %all-to-all-start.2 = ((f32[2,1024,128,2]{1,3,0,2:T(2,128)}), f32[2,1024,128,2]{1,3,0,2:T(2,128)}, u32[]{:S(2)}, u32[]{:S(2)}) async-start(f32[2,1024,128,2]{1,3,0,2:T(2,128)} %copy.173), calls=%async_computation.2 | async-start | bytes 4194304 | tf_op jit(solution)/shard_map/all_to_all | solution.py:78
  142.8 3.5 copy-start.4
  188.9 2.1 copy-start.7
  191.1 2.3 copy-start.5
  196.2 2.0 copy-start.2
  246.8 2.2 copy-start.3
  246.8 2.5 copy-start.6
  250.5 2.1 copy-start
  256.9 35.0 %all-to-all-start.3 = ((bf16[2,1024,2,128]{1,2,0,3:T(2,128)(2,1)}), bf16[2,1024,2,128]{1,2,0,3:T(2,128)(2,1)S(1)}, u32[]{:S(2)}, u32[]{:S(2)}) async-start(bf16[2,1024,2,128]{1,2,0,3:T(2,128)(2,1)} %copy.191), calls=%async_computation.3 | async-start | bytes 2097152 | tf_op jit(solution)/shard_map/all_to_all | solution.py:111
  263.9 3.9 copy-start.1
  291.9 34.8 %all-to-all-start.4 = ((bf16[2,1024,2,128]{1,2,0,3:T(2,128)(2,1)}), bf16[2,1024,2,128]{1,2,0,3:T(2,128)(2,1)}, u32[]{:S(2)}, u32[]{:S(2)}) async-start(bf16[2,1024,2,128]{1,2,0,3:T(2,128)(2,1)} %copy.196), calls=%async_computation.4 | async-start | bytes 2097152 | tf_op jit(solution)/shard_map/all_to_all | solution.py:114
  300.6 28.1 %copy-start.17 = (f32[128,2]{1,0:T(8,128)S(1)}, f32[128,2]{1,0:T(8,128)}, u32[]{:S(2)}) copy-start(f32[128,2]{1,0:T(8,128)} %copy.198) | copy-start | bytes 3076
  334.8 8.3 copy-start.15
  334.8 8.5 copy-start.19
  336.6 254.8 %all-to-all-start.5 = ((f32[2,1024,64,2]{1,3,0,2:T(2,128)}), f32[2,1024,64,2]{1,3,0,2:T(2,128)S(1)}, u32[]{:S(2)}, u32[]{:S(2)}) async-start(f32[2,1024,64,2]{1,3,0,2:T(2,128)} %copy.201), calls=%async_computation.5 | async-start | bytes 2097152 | tf_op jit(solution)/shard_map/all_to_all | solution.py:177
  343.1 246.9 %all-reduce.2.cloned.1.call-start = ((), (), s32[]{:S(2)}) async-start(), calls=%async_computation.6 | async-start | bytes 131072 | tf_op jit(solution)/shard_map/psum | solution.py:220
  592.0 1.0 copy-start.9
  592.0 1.1 copy-start.13
  592.0 1.3 copy-start.14
  592.5 252.4 %copy-start.11 = (bf16[1024,128]{0,1:T(8,128)(2,1)S(1)}, bf16[1024,128]{0,1:T(8,128)(2,1)}, u32[]{:S(2)}) copy-start(bf16[1024,128]{0,1:T(8,128)(2,1)} %copy-done.10) | copy-start | bytes 786436
  594.5 251.1 %copy-start.16 = (bf16[1024,128]{0,1:T(8,128)(2,1)S(1)}, bf16[1024,128]{0,1:T(8,128)(2,1)}, u32[]{:S(2)}) copy-start(bf16[1024,128]{0,1:T(8,128)(2,1)} %get-tuple-element.53) | copy-start | bytes 786436
  837.0 10.3 %collective-permute-start.1 = (bf16[1024,8]{0,1:T(8,128)(2,1)S(1)}, bf16[1024,8]{0,1:T(8,128)(2,1)S(1)}, u32[]{:S(2)}, u32[]{:S(2)}) collective-permute-start(bf16[1024,8]{0,1:T(8,128)(2,1)S(1)} %slice.303), channel_id=1, source_target_pairs={{4,0},{8,4},{12,8},{16,12},{20,16},{24,20},{28,24},{32,28},{36,32}... | collective-permute-start | bytes 49160 | tf_op jit(solution)/shard_map/ppermute | solution.py:14
Sparse Core Ops, SparseCore 0:
  350.0 239.9 all-reduce.1
where the time goes:
time: 865 us; the launch traced here: 856 us
  waiting for transfers between devices  400 us (46%)
  blocking collectives  242 us (28%)
  starting transfers between devices  58.4 us (7%)
  other arithmetic  55.4 us (6%)
  local copies, waits for them, and re-layouts  53.4 us (6%)
  matrix products  31.5 us (4%)
  between operations  15.1 us (2%)
    psum x1, waiting for transfers between devices, per_device(): pole_sum = lax.psum(pole_part, ('seq', 'chan'))  246 us
    psum x1, blocking collectives, per_device(): short_sum = lax.psum(short_part, 'seq')  242 us
    all_to_all x1, waiting for transfers between devices, forward_spectra(): lax.all_to_all(real_part, 'seq', split_axis=2, concat_axis=3, tiled=True)  45 us
    reduce_sum x1, other arithmetic, spectral_long(): kern_r = jnp.sum(scaled_b * mode_r, axis=1)  40.9 us
    all_to_all x1, waiting for transfers between devices, forward_spectra(): lax.all_to_all(imag_part, 'seq', split_axis=2, concat_axis=3, tiled=True)  35 us
    all_to_all x1, waiting for transfers between devices, forward_spectra(): lax.all_to_all(signals.reshape(count_sig, channels, 1, seq_dev), 'seq', s...  27.9 us
    all_to_all x1, waiting for transfers between devices, inverse_partial(): lax.all_to_all(imag_part.astype(jnp.bfloat16), 'seq', split_axis=3, conca...  26 us
    all_to_all x1, waiting for transfers between devices, inverse_partial(): lax.all_to_all(real_part.astype(jnp.bfloat16), 'seq', split_axis=3, conca...  19.8 us
  transfers between devices with their start and end apart: 9, of which 6 were waited for; matrix products, arithmetic and copies ran while one was open for 4% of the time, Pallas kernels for 0%

commit v1 on v0

v1 whole, which is shorter than its diff:
```python
import functools

import jax
import jax.numpy as jnp
from jax import lax
from jax.experimental import pallas as pl
from jax.experimental.pallas import tpu as pltpu
from jax.sharding import PartitionSpec as P

F32 = jnp.float32
BF16 = jnp.bfloat16
LANES = 128
SUB = 8
LEN = 128
POLES = 16
TAPS = 7
HALO = TAPS - 1
EDGE = 8
CARRY = 4 + TAPS
ROWS_OUT = 24
ROWS_BACK = 8
VMEM = 48 * 1024 * 1024


def one_minus_exp(x):
    series = 1.0 - x * (1.0 / 7.0)
    for order in (6.0, 5.0, 4.0, 3.0, 2.0):
        series = 1.0 - x * (1.0 / order) * series
    return x * series


def tile(index):
    if isinstance(index, int):
        return pl.ds(SUB * index, SUB)
    return pl.ds(pl.multiple_of(SUB * index, SUB), SUB)


def across(block):
    return pl.ds(block, LEN, stride=SUB)


def lane_group():
    return lax.broadcasted_iota(jnp.int32, (SUB, LANES), 1) // 16


def to_owner(x):
    y = pltpu.roll(x, 0, 1, stride=16, stride_axis=0)
    group = lane_group()
    for bit in (1, 2, 4):
        y = jnp.where((group & bit) != 0, pltpu.roll(y, SUB - bit, 0), y)
    return pltpu.roll(y, 0, 1, stride=16, stride_axis=0)


def skew_left(x):
    row = lax.broadcasted_iota(jnp.int32, (SUB, LANES), 0)
    for bit in (1, 2, 4):
        x = jnp.where((row & bit) != 0, pltpu.roll(x, LANES - 16 * bit, 1), x)
    return x


def from_owner(x):
    y = skew_left(x)
    group = lane_group()
    for bit in (1, 2, 4):
        y = jnp.where((group & bit) != 0, pltpu.roll(y, bit, 0), y)
    return skew_left(y)


def enter_kernel(q, k, v, cot, rates, residues, taps, kt, vt, zt, tail, head, par):
    for s in range(SUB):
        rows = slice(s * LANES, (s + 1) * LANES)
        kt[across(s), :] = k[rows, :].astype(F32).T
        vt[across(s), :] = v[rows, :].astype(F32).T
        zt[across(s), :] = (q[rows, :].astype(F32) * cot[rows, :].astype(F32)).T
        rate = rates[rows, :].T
        par[pl.ds(s, POLES, stride=SUB), :] = jnp.exp(-rate)
        par[pl.ds(SUB * POLES + s, POLES, stride=SUB), :] = residues[rows, :].T * jnp.sqrt(
            one_minus_exp(2.0 * rate)
        )
        par[pl.ds(2 * SUB * POLES + s, TAPS, stride=SUB), :] = taps[rows, :].T
    tail[...] = kt[SUB * (LEN - HALO) : SUB * LEN, :]
    head[0 : SUB * HALO, :] = zt[0 : SUB * HALO, :]
    head[SUB * HALO : 2 * SUB * HALO, :] = vt[0 : SUB * HALO, :]


def decay_of(par, r):
    return par[tile(r), :]


def coef_of(par, r):
    return par[tile(POLES + r), :]


def tap_of(par, j):
    return par[tile(2 * POLES + j), :]


def scan_down(par, z, gated, w, local, count, base, first, read, write, unroll):
    for pair in range(POLES // 2):
        modes = (2 * pair, 2 * pair + 1)
        decay = [decay_of(par, r) for r in modes]
        coef = [coef_of(par, r) for r in modes]
        final = pair == POLES // 2 - 1
        state = tuple(tuple(read(r, n) for n in range(CARRY)) for r in modes)
        sums = tuple(read(POLES, j) for j in range(TAPS)) if final else ()

        def step(i, carry, pair=pair, decay=decay, coef=coef, final=final):
            state, sums = carry
            t = count - 1 - i
            z_now = z[tile(t + base), :]
            g_now = gated[tile(t), :]
            w_now = [w[j, tile(t), :] for j in range(TAPS)]
            total = None if pair == 0 else local[tile(t), :]
            after = []
            for n in range(2):
                back, pole, ahead, power, *moments = state[n]
                back = back * decay[n] + z_now
                pole = pole + g_now * back
                ahead = ahead + power * g_now
                moments = [m + power * x for m, x in zip(moments, w_now)]
                power = power * decay[n]
                term = coef[n] * back
                total = term if total is None else total + term
                after.append((back, pole, ahead, power, *moments))
            local[tile(t), :] = total
            if final:
                sums = tuple(a + total * x for a, x in zip(sums, w_now))
            return tuple(after), sums

        state, sums = lax.fori_loop(0, count, step, (state, sums), unroll=unroll)
        for n, r in enumerate(modes):
            for m in range(CARRY):
                write(r, m, state[n][m])
        for j, value in enumerate(sums):
            write(POLES, j, value)


def inner_kernel(kt, vt, zt, par, gated, gate, local, carry, w):
    count = LEN - EDGE
    taps = [tap_of(par, j) for j in range(TAPS)]

    def prepare(i, before):
        keys = (kt[tile(i + EDGE), :], *before)
        now = taps[0] * keys[0]
        for j in range(1, TAPS):
            now = now + taps[j] * keys[j]
        value = vt[tile(i + EDGE), :]
        gate[tile(i), :] = now
        gated[tile(i), :] = now * value
        for j in range(TAPS):
            w[j, tile(i), :] = value * keys[j]
        return keys[:HALO]

    lax.fori_loop(0, count, prepare, tuple(kt[tile(EDGE - 1 - j), :] for j in range(HALO)), unroll=4)
    zero = jnp.zeros((SUB, LANES), F32)

    def read(r, n):
        return decay_of(par, r) if r < POLES and n == 3 else zero

    def write(r, n, value):
        carry[tile(r * CARRY + n), :] = value

    scan_down(par, zt, gated, w, local, count, EDGE, True, read, write, 4)


def edge_kernel(kt, tail, vt, zt, par, carry, gated, gate, local, out, w, gather, spread):
    keys = [tail[tile(n), :] for n in range(HALO)] + [kt[tile(n), :] for n in range(EDGE)]
    taps = [tap_of(par, j) for j in range(TAPS)]
    for t in range(EDGE):
        now = taps[0] * keys[t + HALO]
        for j in range(1, TAPS):
            now = now + taps[j] * keys[t + HALO - j]
        value = vt[tile(t), :]
        gate[tile(t), :] = now
        gated[tile(t), :] = now * value
        for j in range(TAPS):
            w[j, tile(t), :] = value * keys[t + HALO - j]

    def read(r, n):
        return carry[tile(r * CARRY + n), :]

    def write(r, n, value):
        if r == POLES:
            row, slot = 6, n
        elif n == 3:
            return
        else:
            half, slot = divmod(r, SUB)
            row = {2: 0, 0: 2, 1: 4}.get(n, 8 + 2 * (n - 4)) + half
        gather[tile(row * SUB + slot), :] = value

    scan_down(par, zt, gated, w, local, EDGE, 0, False, read, write, EDGE)
    zero = jnp.zeros((SUB, LANES), F32)
    gather[tile(6 * SUB + TAPS), :] = zero
    for row in range(ROWS_OUT):
        for s in range(SUB):
            if row in (7, 22, 23):
                block = zero
            else:
                block = to_owner(gather[pl.ds(row * SUB * SUB + s, SUB, stride=SUB), :])
            spread[pl.ds(s * SUB * ROWS_OUT + row, SUB, stride=ROWS_OUT), :] = block
    out[...] = spread[...].astype(BF16)


def owner_kernel(count, scale, arrived, mine, out, x, y):
    x[...] = arrived[...].astype(F32)
    even = lax.broadcasted_iota(jnp.int32, (SUB, LANES), 0) % 2 == 0

    def pattern(ref, row):
        return jnp.where(even, ref[pl.ds(row, 1), :], ref[pl.ds(row + 1, 1), :])

    rate = pattern(mine, 0)
    weight = jnp.sqrt(one_minus_exp(2.0 * rate))
    coef = pattern(mine, 2) * weight
    leap = jnp.exp(-float(LEN) * rate)
    zero = jnp.zeros((SUB, LANES), F32)
    ahead, pole, total = zero, zero, zero
    for d in range(count):
        y[pl.ds(d * ROWS_BACK, 2), :] = ahead[0:2, :]
        now = x[pl.ds(d * ROWS_OUT, SUB), :]
        pole = pole + ahead * pattern(x, d * ROWS_OUT + 2)
        total = total + now
        ahead = ahead * leap + now
    back, low, high = zero, zero, zero
    for d in reversed(range(count)):
        y[pl.ds(d * ROWS_BACK + 2, 2), :] = back[0:2, :]
        low = low + back * x[pl.ds(d * ROWS_OUT + SUB, SUB), :]
        high = high + back * x[pl.ds(d * ROWS_OUT + 2 * SUB, SUB), :]
        back = back * leap + pattern(x, d * ROWS_OUT + 2)
    poles = (pole[0:2, :] + total[4:6, :]) * weight[0:2, :] * scale
    group = lane_group()[0:1, :]
    short = total[6:7, :]
    for part, first in ((low * coef, 0), (high * coef, 4)):
        part = part + pltpu.roll(part, SUB - 1, 0)
        for shift in (16, 32, 64):
            part = part + pltpu.roll(part, shift, 1)
        for n in range(min(4, TAPS - first)):
            short = short + jnp.where(group == first + n, part[2 * n : 2 * n + 1, :], 0.0)
    short = short * scale
    coarse = short.astype(BF16).astype(F32)
    fine = short - coarse
    for d in range(count):
        y[pl.ds(d * ROWS_BACK + 4, 2), :] = poles
        y[pl.ds(d * ROWS_BACK + 6, 1), :] = coarse
        y[pl.ds(d * ROWS_BACK + 7, 1), :] = fine
    out[...] = y[...].astype(BF16)


def leave_kernel(
    arrived, gated_a, gated_b, gate_a, gate_b, local_a, local_b, vt, head, par, cot,
    grad_q, grad_k, grad_v, grad_short, x, state, long_out, slope, vals,
):
    x[...] = arrived[...].astype(F32)
    for s in range(SUB):
        for row in range(4):
            block = x[pl.ds(s * SUB * ROWS_BACK + row, SUB, stride=ROWS_BACK), :]
            state[pl.ds(row * SUB * SUB + s, SUB, stride=SUB), :] = from_owner(block)
        coarse = x[pl.ds(s * SUB * ROWS_BACK + 6, SUB, stride=ROWS_BACK), :]
        fine = x[pl.ds(s * SUB * ROWS_BACK + 7, SUB, stride=ROWS_BACK), :]
        grad_short[s * LANES : (s + 1) * LANES, :] = from_owner(coarse + fine)[0:TAPS, :].T

    half = POLES // 2
    for part in range(2):
        modes = range(part * half, (part + 1) * half)
        decay = [decay_of(par, r) for r in modes]
        coef = [coef_of(par, r) for r in modes]
        ahead = tuple(state[tile(r), :] for r in modes)

        def forward(i, ahead, source, base, part=part, decay=decay, coef=coef):
            now = source[tile(i), :]
            total = None if part == 0 else long_out[tile(i + base), :]
            after = []
            for h, d, c in zip(ahead, decay, coef):
                h = h + now
                term = c * h
                total = term if total is None else total + term
                after.append(h * d)
            long_out[tile(i + base), :] = total
            return tuple(after)

        ahead = lax.fori_loop(
            0, EDGE, functools.partial(forward, source=gated_b, base=0), ahead, unroll=EDGE
        )
        lax.fori_loop(
            0, LEN - EDGE, functools.partial(forward, source=gated_a, base=EDGE), ahead, unroll=4
        )

    decay = [decay_of(par, r) for r in range(POLES)]
    back = [state[tile(POLES + r), :] for r in range(POLES)]
    for n in range(HALO):
        total = coef_of(par, 0) * back[0]
        for r in range(1, POLES):
            total = total + coef_of(par, r) * back[r]
        slope[tile(LEN + n), :] = total * head[tile(HALO + n), :]
        if n < HALO - 1:
            z_now = head[tile(n), :]
            back = [(b - z_now) / d for b, d in zip(back, decay)]

    def backward(i, terms, local, gate, count, base):
        t = count - 1 - i
        terms = tuple(q * d for q, d in zip(terms, decay))
        total = local[tile(t), :]
        sums = list(terms)
        while len(sums) > 1:
            sums = [a + b for a, b in zip(sums[0::2], sums[1::2])]
        total = total + sums[0]
        slope[tile(t + base), :] = total * vt[tile(t + base), :]
        vals[tile(t + base), :] = total * gate[tile(t), :]
        return terms

    terms = tuple(coef_of(par, r) * state[tile(POLES + r), :] for r in range(POLES))
    terms = lax.fori_loop(
        0, LEN - EDGE,
        functools.partial(backward, local=local_a, gate=gate_a, count=LEN - EDGE, base=EDGE),
        terms, unroll=4,
    )
    lax.fori_loop(
        0, EDGE,
        functools.partial(backward, local=local_b, gate=gate_b, count=EDGE, base=0),
        terms, unroll=EDGE,
    )

    taps = [tap_of(par, j) for j in range(TAPS)]

    def spread_taps(i, after):
        t = LEN - 1 - i
        slopes = (slope[tile(t), :], *after)
        total = taps[0] * slopes[0]
        for j in range(1, TAPS):
            total = total + taps[j] * slopes[j]
        slope[tile(t), :] = total
        return slopes[:HALO]

    lax.fori_loop(
        0, LEN, spread_taps, tuple(slope[tile(LEN + n), :] for n in range(HALO)), unroll=4
    )
    for s in range(SUB):
        rows = slice(s * LANES, (s + 1) * LANES)
        grad_q[rows, :] = (cot[rows, :].astype(F32) * long_out[across(s), :].T).astype(BF16)
        grad_k[rows, :] = slope[across(s), :].T.astype(BF16)
        grad_v[rows, :] = vals[across(s), :].T.astype(BF16)


def pole_kernel(a, b, c, d, out, x, y):
    x[...] = (a[...].astype(F32) + b[...].astype(F32)) + (c[...].astype(F32) + d[...].astype(F32))
    for s in range(SUB):
        for half in range(2):
            block = x[pl.ds(s * SUB * 2 + half, SUB, stride=2), :]
            y[half * SUB : (half + 1) * SUB, :] = from_owner(block)
        out[s * LANES : (s + 1) * LANES, :] = y[...].T


def call(kernel, name, outs, scratch, operands, in_specs=None, flops=0, moved=0):
    return pl.pallas_call(
        kernel,
        grid=(1,) if in_specs else (),
        out_shape=outs,
        in_specs=in_specs or [pl.BlockSpec(memory_space=pltpu.VMEM)] * len(operands),
        out_specs=[pl.BlockSpec(memory_space=pltpu.VMEM)] * len(outs),
        scratch_shapes=scratch,
        compiler_params=pltpu.CompilerParams(vmem_limit_bytes=VMEM),
        cost_estimate=pl.CostEstimate(flops=flops, bytes_accessed=moved, transcendentals=0),
        name=name,
    )(*operands)


def shape(rows, dtype=F32, lanes=LANES):
    return jax.ShapeDtypeStruct((rows, lanes), dtype)


def per_device(q_in, k_in, v_in, cotangent, taps_short, residues, rates):
    channels, length = q_in.shape
    count = lax.axis_size("seq")
    index = lax.axis_index("seq")
    chans = lax.axis_size("chan")
    assert (channels, length, count) == (SUB * LANES, LEN, SUB * SUB)
    scale = (length * count) ** (-0.5)
    full, edge = SUB * LEN, SUB * EDGE
    inner = full - edge
    tile_bytes = SUB * LANES * 4

    kt, vt, zt, tail, head, par = call(
        enter_kernel,
        "enter",
        [shape(full)] * 3 + [shape(SUB * HALO), shape(2 * SUB * HALO), shape(SUB * 40)],
        [],
        (q_in, k_in, v_in, cotangent, rates, residues, taps_short),
        flops=4 * 10**6,
        moved=3 * 10**6,
    )
    tail = lax.ppermute(tail, "seq", [(i, i + 1) for i in range(count - 1)])
    head = lax.ppermute(head, "seq", [(i + 1, i) for i in range(count - 1)])

    gated_a, gate_a, local_a, carry = call(
        inner_kernel,
        "inner",
        [shape(inner)] * 3 + [shape(SUB * (POLES * CARRY + TAPS))],
        [pltpu.VMEM((TAPS, inner, LANES), F32)],
        (kt, vt, zt, par),
        flops=48 * 10**6,
        moved=4 * 10**6,
    )
    first = pl.BlockSpec((edge, LANES), lambda i: (0, 0), memory_space=pltpu.VMEM)
    whole = pl.BlockSpec(memory_space=pltpu.VMEM)
    gated_b, gate_b, local_b, message = call(
        edge_kernel,
        "edge",
        [shape(edge)] * 3 + [shape(count * ROWS_OUT, BF16)],
        [
            pltpu.VMEM((TAPS, edge, LANES), F32),
            pltpu.VMEM((SUB * SUB * ROWS_OUT, LANES), F32),
            pltpu.VMEM((count * ROWS_OUT, LANES), F32),
        ],
        (kt, tail, vt, zt, par, carry),
        [first, whole, first, first, whole, whole],
        flops=6 * 10**6,
        moved=2 * 10**6,
    )

    def exchange(x, rows):
        x = x.reshape(count, rows, LANES)
        return lax.all_to_all(x, "seq", split_axis=0, concat_axis=0, tiled=True)

    arrived = exchange(message, ROWS_OUT).reshape(count * ROWS_OUT, LANES)
    start = (index // SUB) * LANES + ((SUB - index % SUB) % SUB) * 16
    mine = jnp.concatenate(
        [
            lax.dynamic_slice(a, (start, 0), (16, POLES)).T.reshape(2, LANES)
            for a in (rates, residues)
        ]
    )
    (back,) = call(
        functools.partial(owner_kernel, count, scale),
        "owner",
        [shape(count * ROWS_BACK, BF16)],
        [pltpu.VMEM((count * ROWS_OUT, LANES), F32), pltpu.VMEM((count * ROWS_BACK, LANES), F32)],
        (arrived, mine),
        flops=2 * 10**6,
        moved=10**6,
    )
    returned = exchange(back, ROWS_BACK)
    poles = returned[:, 4:6, :].reshape(2 * count, LANES)
    others = [
        lax.ppermute(poles, "chan", [(i, (i + n) % chans) for i in range(chans)])
        for n in range(1, chans)
    ]
    grad_q, grad_k, grad_v, grad_short = call(
        leave_kernel,
        "leave",
        [shape(channels, BF16)] * 3 + [shape(channels, F32, TAPS)],
        [
            pltpu.VMEM((count * ROWS_BACK, LANES), F32),
            pltpu.VMEM((SUB * 2 * POLES, LANES), F32),
            pltpu.VMEM((full, LANES), F32),
            pltpu.VMEM((full + SUB * HALO, LANES), F32),
            pltpu.VMEM((full, LANES), F32),
        ],
        (
            returned.reshape(count * ROWS_BACK, LANES),
            gated_a, gated_b, gate_a, gate_b, local_a, local_b, vt, head, par, cotangent,
        ),
        flops=16 * 10**6,
        moved=3 * 10**6,
    )
    (grad_residues,) = call(
        pole_kernel,
        "poles",
        [shape(channels, F32, POLES)],
        [pltpu.VMEM((2 * count, LANES), F32), pltpu.VMEM((POLES, LANES), F32)],
        (poles, *others),
        flops=10**5,
        moved=10**5,
    )
    return grad_q, grad_k, grad_v, grad_short, grad_residues


def solution(mesh):
    streams = P("chan", "seq")
    return jax.shard_map(
        per_device,
        mesh=mesh,
        in_specs=(streams,) * 4 + (P("chan", None), P(), P()),
        out_specs=(streams,) * 3 + (P("chan", None), P()),
        check_vma=False,
    )
```

time: 865 us -> 77.4 us (0.09); the launches traced: 856 us -> 77 us
  waiting for transfers between devices: 400 us -> 22.8 us
  blocking collectives: 242 us -> 0 us
  other arithmetic: 55.4 us -> 0.01 us
  local copies, waits for them, and re-layouts: 53.4 us -> 5.45 us
  matrix products: 31.5 us -> 0 us
  starting transfers between devices: 58.4 us -> 28.8 us
  Pallas kernels: 0 us -> 19 us
  between operations: 15.1 us -> 0.82 us
    psum x1 -> x0, waiting for transfers between devices: 246 us -> none  [per_device(): pole_sum = lax.psum(pole_part, ('seq', 'chan'))]
    psum x1 -> x0, blocking collectives: 242 us -> none  [per_device(): short_sum = lax.psum(short_part, 'seq')]
    all_to_all x6 -> x2, waiting for transfers between devices: 154 us -> 22.8 us  [exchange(): return lax.all_to_all(x, 'seq', split_axis=0, concat_axis=0, tiled=True)]
    reduce_sum x2 -> x0, other arithmetic: 42.1 us -> none  [the longest x1 40.9 us: spectral_long(): kern_r = jnp.sum(scaled_b * mode_r, axis=1)]
    dot_general x12 -> x0, matrix products: 31.5 us -> none  [the longest x2 5.97 us: transform(): imag_cos = jnp.einsum(form, imag_part, cosine, precision=HIGHEST)]
    all_to_all x6 -> x2, starting transfers between devices: 46.3 us -> 16.9 us  [exchange(): return lax.all_to_all(x, 'seq', split_axis=0, concat_axis=0, tiled=True)]
    pallas_call x0 -> x6, Pallas kernels: none -> 19 us  [call(): pl.pallas_call(kernel, grid=(1,) if in_specs else (), out_shape=outs, in_...]
  transfers between devices with their start and end apart: 9 -> 7, of which waited for: 6 -> 2; matrix products, arithmetic and copies ran while one was open for 4% -> 2% of each run, Pallas kernels for 0% -> 19%
where the time goes in v1:
time: 77.4 us; the launch traced here: 77 us
  starting transfers between devices  28.8 us (37%)
  waiting for transfers between devices  22.8 us (29%)
  Pallas kernels  19 us (25%)
  local copies, waits for them, and re-layouts  5.45 us (7%)
  between operations  0.82 us (1%)
    all_to_all x2, waiting for transfers between devices, exchange(): return lax.all_to_all(x, 'seq', split_axis=0, concat_axis=0, tiled=True)  22.8 us
    pallas_call x6, Pallas kernels, call(): pl.pallas_call(kernel, grid=(1,) if in_specs else (), out_shape=outs, in_...  19 us
    all_to_all x2, starting transfers between devices, exchange(): return lax.all_to_all(x, 'seq', split_axis=0, concat_axis=0, tiled=True)  16.9 us
    ppermute x3, starting transfers between devices, per_device(): lax.ppermute(poles, 'chan', [(i, (i + n) % chans) for i in range(chans)])  5.06 us
    ppermute x1, starting transfers between devices, per_device(): tail = lax.ppermute(tail, 'seq', [(i, i + 1) for i in range(count - 1)])  4.51 us
    unnamed x17, local copies, waits for them, and re-layouts  4.46 us
    ppermute x1, starting transfers between devices, per_device(): head = lax.ppermute(head, 'seq', [(i + 1, i) for i in range(count - 1)])  2.36 us
  transfers between devices with their start and end apart: 7, of which 2 were waited for; matrix products, arithmetic and copies ran while one was open for 2% of the time, Pallas kernels for 19%

profile of v1, /device:TPU:1, one launch (start us, length us, event | category | flops | bytes accessed | tf_op | source)
XLA Modules:
  0.0 77.0 jit_solution(12680576563225629422)
XLA Ops:
  0.6 0.0 copy-start.4
  0.6 1.1 %copy.12.rates = f32[1024,16]{1,0:T(8,128)S(1)} copy(f32[1024,16]{0,1:T(8,128)} %param.13) | data formatting | bytes 131072 | tf_op args[6]
  1.7 0.0 copy-done.4
  1.7 0.0 copy-start.5
  1.7 0.0 copy-start.2
  1.8 0.0 copy-start.3
  1.8 0.2 copy.13.residues
  2.0 0.5 copy-done.5
  2.5 0.0 copy-start
  2.5 0.0 copy-start.1
  2.5 0.2 copy.14.taps
  2.7 0.0 copy-done.2
  2.7 0.0 copy-done.3
  2.8 0.7 copy-done
  3.5 0.1 copy-done.1
  3.6 0.8 %enter.1 = (f32[1024,128]{1,0:T(8,128)S(1)}, f32[1024,128]{1,0:T(8,128)S(1)}, f32[1024,128]{1,0:T(8,128)S(1)}, f32[48,128]{1,0:T(8,128)S(1)}, f32[96,128]{1,0:T(8,128)S(1)}, /*index=5*/f32[320,128]{1,0:T(8,128)S(1)}) custom-call(bf16[1024,128]{1,0:T(8,128)(2,1)S(1)} %copy-done.1, bf16[1024,128]{1,0:T(8,128)(2,1)S(1)} %copy-done.2, ...), custom_call_target="tpu_custom_call" | custom-call | flops 4000000 | bytes 3000000 | tf_op jit(solution)/shard_map/enter/pallas_call | solution.py:354
  4.3 4.5 %collective-permute-start = (f32[48,128]{1,0:T(8,128)S(1)}, f32[48,128]{1,0:T(8,128)S(1)}, u32[]{:S(2)}, u32[]{:S(2)}) collective-permute-start(f32[48,128]{1,0:T(8,128)S(1)} %get-tuple-element.24), channel_id=1, source_target_pairs={{0,4},{4,8},{8,12},{12,16},{16,20},{20,24},{24,28},{28,32},{32,36}... | collective-permute-start | bytes 73736 | tf_op jit(solution)/shard_map/ppermute | solution.py:391
  8.9 8.2 %inner.1 = (f32[960,128]{1,0:T(8,128)S(1)}, f32[960,128]{1,0:T(8,128)S(1)}, f32[960,128]{1,0:T(8,128)S(1)}, f32[1464,128]{1,0:T(8,128)S(1)}) custom-call(f32[1024,128]{1,0:T(8,128)S(1)} %get-tuple-element.23.kt, f32[1024,128]{1,0:T(8,128)S(1)} %get-tuple-element.25.vt, f32[1024,128]{1,0:T(8,128)S(1)} %get-tuple-element.26.zt, ...), custom_call_target="tpu_custom_call" | custom-call | flops 48000000 | bytes 4000000 | tf_op jit(solution)/shard_map/inner/pallas_call | solution.py:354
  17.1 0.0 collective-permute-done.tail
  17.1 1.7 %edge.1 = (f32[64,128]{1,0:T(8,128)S(1)}, f32[64,128]{1,0:T(8,128)S(1)}, f32[64,128]{1,0:T(8,128)S(1)}, bf16[1536,128]{1,0:T(8,128)(2,1)}) custom-call(f32[1024,128]{1,0:T(8,128)S(1)} %get-tuple-element.23.kt, f32[48,128]{1,0:T(8,128)S(1)} %collective-permute-done.tail, f32[1024,128]{1,0:T(8,128)S(1)} %get-tuple-element.25.vt, ...), custom_call_target="tpu_custom_call" | custom-call | flops 6000000 | bytes 2000000 | tf_op jit(solution)/shard_map/edge/pallas_call | solution.py:354
  18.8 11.3 %all-to-all-start = ((bf16[64,24,128]{2,1,0:T(8,128)(2,1)}), bf16[64,24,128]{2,1,0:T(8,128)(2,1)S(1)}, u32[]{:S(2)}, u32[]{:S(2)}) async-start(bf16[64,24,128]{2,1,0:T(8,128)(2,1)} %bitcast), calls=%async_computation | async-start | bytes 786432 | tf_op jit(solution)/shard_map/all_to_all | solution.py:422
  30.1 0.8 %dynamic-slice_bitcast_fusion = (f32[16,16]{1,0:T(8,128)S(1)}, f32[16,16]{1,0:T(8,128)S(1)}) fusion(f32[1024,16]{0,1:T(8,128)} %param.12, s32[]{:T(128)S(6)} %select_n.22, f32[1024,16]{0,1:T(8,128)} %param.13), kind=kLoop, calls=%fused_computation | loop fusion | bytes 4100 | tf_op jit(solution)/shard_map/transpose | solution.py:428
  30.9 0.1 reshape.34
  31.0 0.1 reshape.33
  31.1 14.1 %all-to-all-done = bf16[64,24,128]{2,1,0:T(8,128)(2,1)S(1)} async-done(((bf16[64,24,128]{2,1,0:T(8,128)(2,1)}), bf16[64,24,128]{2,1,0:T(8,128)(2,1)S(1)}, u32[]{:S(2)}, u32[]{:S(2)}) %all-to-all-start) | async-done | bytes 393248 | tf_op jit(solution)/shard_map/all_to_all | solution.py:422
  45.1 1.1 %owner.1 = bf16[512,128]{1,0:T(8,128)(2,1)} custom-call(bf16[1536,128]{1,0:T(8,128)(2,1)S(1)} %bitcast.9, f32[4,128]{1,0:T(4,128)S(1)} %pad_maximum_fusion.mine), custom_call_target="tpu_custom_call" | custom-call | flops 2000000 | bytes 1000000 | tf_op jit(solution)/shard_map/owner/pallas_call | solution.py:354
  46.2 5.6 %all-to-all-start.1 = ((bf16[64,8,128]{2,1,0:T(8,128)(2,1)}), bf16[64,8,128]{2,1,0:T(8,128)(2,1)S(1)}, u32[]{:S(2)}, u32[]{:S(2)}) async-start(bf16[64,8,128]{2,1,0:T(8,128)(2,1)} %bitcast.4), calls=%async_computation.1 | async-start | bytes 262144 | tf_op jit(solution)/shard_map/all_to_all | solution.py:422
  51.8 2.4 %collective-permute-start.1 = (f32[96,128]{1,0:T(8,128)S(1)}, f32[96,128]{1,0:T(8,128)S(1)}, u32[]{:S(2)}, u32[]{:S(2)}) collective-permute-start(f32[96,128]{1,0:T(8,128)S(1)} %get-tuple-element.36), channel_id=1, source_target_pairs={{4,0},{8,4},{12,8},{16,12},{20,16},{24,20},{28,24},{32,28},{36,32}... | collective-permute-start | bytes 147464 | tf_op jit(solution)/shard_map/ppermute | solution.py:392
  54.2 8.7 %all-to-all-done.1 = bf16[64,8,128]{2,1,0:T(8,128)(2,1)S(1)} async-done(((bf16[64,8,128]{2,1,0:T(8,128)(2,1)}), bf16[64,8,128]{2,1,0:T(8,128)(2,1)S(1)}, u32[]{:S(2)}, u32[]{:S(2)}) %all-to-all-start.1) | async-done | bytes 131104 | tf_op jit(solution)/shard_map/all_to_all | solution.py:422
  63.0 1.4 %collective-permute-start.2 = (bf16[128,128]{1,0:T(8,128)(2,1)S(1)}, bf16[128,128]{1,0:T(8,128)(2,1)S(1)}, u32[]{:S(2)}, u32[]{:S(2)}) collective-permute-start(bf16[128,128]{1,0:T(8,128)(2,1)S(1)} %bitcast.11), channel_id=1, source_target_pairs={{0,1},{1,2},{2,3},{3,0},{4,5},{5,6},{6,7},{7,4},{8,9},{9,10},{10,1... | collective-permute-start | bytes 98312 | tf_op jit(solution)/shard_map/ppermute | solution.py:444
  64.4 2.6 %collective-permute-start.3 = (bf16[128,128]{1,0:T(8,128)(2,1)S(1)}, bf16[128,128]{1,0:T(8,128)(2,1)S(1)}, u32[]{:S(2)}, u32[]{:S(2)}) collective-permute-start(bf16[128,128]{1,0:T(8,128)(2,1)S(1)} %bitcast.12), channel_id=1, source_target_pairs={{0,2},{1,3},{2,0},{3,1},{4,6},{5,7},{6,4},{7,5},{8,10},{9,11},{10,... | collective-permute-start | bytes 98312 | tf_op jit(solution)/shard_map/ppermute | solution.py:444
  67.0 1.1 %collective-permute-start.4 = (bf16[128,128]{1,0:T(8,128)(2,1)S(1)}, bf16[128,128]{1,0:T(8,128)(2,1)S(1)}, u32[]{:S(2)}, u32[]{:S(2)}) collective-permute-start(bf16[128,128]{1,0:T(8,128)(2,1)S(1)} %bitcast.13), channel_id=1, source_target_pairs={{0,3},{1,0},{2,1},{3,2},{4,7},{5,4},{6,5},{7,6},{8,11},{9,8},{10,9... | collective-permute-start | bytes 98312 | tf_op jit(solution)/shard_map/ppermute | solution.py:444
  68.1 0.0 collective-permute-done.1.head
  68.1 6.5 %leave.1 = (bf16[1024,128]{1,0:T(8,128)(2,1)}, bf16[1024,128]{1,0:T(8,128)(2,1)}, bf16[1024,128]{1,0:T(8,128)(2,1)}, f32[1024,7]{1,0:T(8,128)S(1)}) custom-call(bf16[512,128]{1,0:T(8,128)(2,1)S(1)} %bitcast.10, f32[960,128]{1,0:T(8,128)S(1)} %get-tuple-element.30.gated_a, f32[64,128]{1,0:T(8,128)S(1)} %get-tuple-element.31.gated_b, ...), custom_call_target="tpu_custom_call" | custom-call | flops 16000000 | bytes 3000000 | tf_op jit(solution)/shard_map/leave/pallas_call | solution.py:354
  74.6 0.8 %copy.15 = f32[1024,7]{0,1:T(8,128)} copy(f32[1024,7]{1,0:T(8,128)S(1)} %get-tuple-element.44) | data formatting | bytes 57344
  75.4 0.0 collective-permute-done.2.b
  75.4 0.0 collective-permute-done.3.c
  75.4 0.0 collective-permute-done.4.d
  75.4 0.7 poles.1
  76.2 0.8 %copy.16 = f32[1024,16]{0,1:T(8,128)} copy(f32[1024,16]{1,0:T(8,128)S(1)} %poles.1) | data formatting | bytes 131072
  (2 shorter events, 0.0 us)
Async XLA Ops:
  0.6 1.1 %copy-start.4 = (f32[1024,16]{0,1:T(8,128)S(1)}, f32[1024,16]{0,1:T(8,128)}, u32[]{:S(2)}) copy-start(f32[1024,16]{0,1:T(8,128)} %param.12) | copy-start | bytes 196612
  1.7 0.8 copy-start.5
  1.7 1.0 %copy-start.2 = (bf16[1024,128]{1,0:T(8,128)(2,1)S(1)}, bf16[1024,128]{1,0:T(8,128)(2,1)}, u32[]{:S(2)}) copy-start(bf16[1024,128]{1,0:T(8,128)(2,1)} %k.1) | copy-start | bytes 786436
  1.8 1.0 %copy-start.3 = (bf16[1024,128]{1,0:T(8,128)(2,1)S(1)}, bf16[1024,128]{1,0:T(8,128)(2,1)}, u32[]{:S(2)}) copy-start(bf16[1024,128]{1,0:T(8,128)(2,1)} %v.1) | copy-start | bytes 786436
  2.5 1.0 %copy-start = (bf16[1024,128]{1,0:T(8,128)(2,1)S(1)}, bf16[1024,128]{1,0:T(8,128)(2,1)}, u32[]{:S(2)}) copy-start(bf16[1024,128]{1,0:T(8,128)(2,1)} %cot.3) | copy-start | bytes 786436
  2.5 1.1 %copy-start.1 = (bf16[1024,128]{1,0:T(8,128)(2,1)S(1)}, bf16[1024,128]{1,0:T(8,128)(2,1)}, u32[]{:S(2)}) copy-start(bf16[1024,128]{1,0:T(8,128)(2,1)} %q.1) | copy-start | bytes 786436
  4.3 12.8 %collective-permute-start = (f32[48,128]{1,0:T(8,128)S(1)}, f32[48,128]{1,0:T(8,128)S(1)}, u32[]{:S(2)}, u32[]{:S(2)}) collective-permute-start(f32[48,128]{1,0:T(8,128)S(1)} %get-tuple-element.24), channel_id=1, source_target_pairs={{0,4},{4,8},{8,12},{12,16},{16,20},{20,24},{24,28},{28,32},{32,36}... | collective-permute-start | bytes 73736 | tf_op jit(solution)/shard_map/ppermute | solution.py:391
  18.8 26.4 %all-to-all-start = ((bf16[64,24,128]{2,1,0:T(8,128)(2,1)}), bf16[64,24,128]{2,1,0:T(8,128)(2,1)S(1)}, u32[]{:S(2)}, u32[]{:S(2)}) async-start(bf16[64,24,128]{2,1,0:T(8,128)(2,1)} %bitcast), calls=%async_computation | async-start | bytes 786432 | tf_op jit(solution)/shard_map/all_to_all | solution.py:422
  46.2 16.7 %all-to-all-start.1 = ((bf16[64,8,128]{2,1,0:T(8,128)(2,1)}), bf16[64,8,128]{2,1,0:T(8,128)(2,1)S(1)}, u32[]{:S(2)}, u32[]{:S(2)}) async-start(bf16[64,8,128]{2,1,0:T(8,128)(2,1)} %bitcast.4), calls=%async_computation.1 | async-start | bytes 262144 | tf_op jit(solution)/shard_map/all_to_all | solution.py:422
  51.8 16.2 %collective-permute-start.1 = (f32[96,128]{1,0:T(8,128)S(1)}, f32[96,128]{1,0:T(8,128)S(1)}, u32[]{:S(2)}, u32[]{:S(2)}) collective-permute-start(f32[96,128]{1,0:T(8,128)S(1)} %get-tuple-element.36), channel_id=1, source_target_pairs={{4,0},{8,4},{12,8},{16,12},{20,16},{24,20},{28,24},{32,28},{36,32}... | collective-permute-start | bytes 147464 | tf_op jit(solution)/shard_map/ppermute | solution.py:392
  63.0 12.4 %collective-permute-start.2 = (bf16[128,128]{1,0:T(8,128)(2,1)S(1)}, bf16[128,128]{1,0:T(8,128)(2,1)S(1)}, u32[]{:S(2)}, u32[]{:S(2)}) collective-permute-start(bf16[128,128]{1,0:T(8,128)(2,1)S(1)} %bitcast.11), channel_id=1, source_target_pairs={{0,1},{1,2},{2,3},{3,0},{4,5},{5,6},{6,7},{7,4},{8,9},{9,10},{10,1... | collective-permute-start | bytes 98312 | tf_op jit(solution)/shard_map/ppermute | solution.py:444
  64.4 11.0 %collective-permute-start.3 = (bf16[128,128]{1,0:T(8,128)(2,1)S(1)}, bf16[128,128]{1,0:T(8,128)(2,1)S(1)}, u32[]{:S(2)}, u32[]{:S(2)}) collective-permute-start(bf16[128,128]{1,0:T(8,128)(2,1)S(1)} %bitcast.12), channel_id=1, source_target_pairs={{0,2},{1,3},{2,0},{3,1},{4,6},{5,7},{6,4},{7,5},{8,10},{9,11},{10,... | collective-permute-start | bytes 98312 | tf_op jit(solution)/shard_map/ppermute | solution.py:444
  67.0 8.4 %collective-permute-start.4 = (bf16[128,128]{1,0:T(8,128)(2,1)S(1)}, bf16[128,128]{1,0:T(8,128)(2,1)S(1)}, u32[]{:S(2)}, u32[]{:S(2)}) collective-permute-start(bf16[128,128]{1,0:T(8,128)(2,1)S(1)} %bitcast.13), channel_id=1, source_target_pairs={{0,3},{1,0},{2,1},{3,2},{4,7},{5,4},{6,5},{7,6},{8,11},{9,8},{10,9... | collective-permute-start | bytes 98312 | tf_op jit(solution)/shard_map/ppermute | solution.py:444

commit v2 on v1

--- a/solution.py
+++ b/solution.py
@@ -17,7 +17,7 @@
 HALO = TAPS - 1
 EDGE = 8
 CARRY = 4 + TAPS
-ROWS_OUT = 24
+ROWS_OUT = 22
 ROWS_BACK = 8
 VMEM = 48 * 1024 * 1024
 
@@ -64,23 +64,6 @@
     for bit in (1, 2, 4):
         y = jnp.where((group & bit) != 0, pltpu.roll(y, bit, 0), y)
     return skew_left(y)
-
-
-def enter_kernel(q, k, v, cot, rates, residues, taps, kt, vt, zt, tail, head, par):
-    for s in range(SUB):
-        rows = slice(s * LANES, (s + 1) * LANES)
-        kt[across(s), :] = k[rows, :].astype(F32).T
-        vt[across(s), :] = v[rows, :].astype(F32).T
-        zt[across(s), :] = (q[rows, :].astype(F32) * cot[rows, :].astype(F32)).T
-        rate = rates[rows, :].T
-        par[pl.ds(s, POLES, stride=SUB), :] = jnp.exp(-rate)
-        par[pl.ds(SUB * POLES + s, POLES, stride=SUB), :] = residues[rows, :].T * jnp.sqrt(
-            one_minus_exp(2.0 * rate)
-        )
-        par[pl.ds(2 * SUB * POLES + s, TAPS, stride=SUB), :] = taps[rows, :].T
-    tail[...] = kt[SUB * (LEN - HALO) : SUB * LEN, :]
-    head[0 : SUB * HALO, :] = zt[0 : SUB * HALO, :]
-    head[SUB * HALO : 2 * SUB * HALO, :] = vt[0 : SUB * HALO, :]
 
 
 def decay_of(par, r):
@@ -135,7 +118,26 @@
             write(POLES, j, value)
 
 
-def inner_kernel(kt, vt, zt, par, gated, gate, local, carry, w):
+def inner_kernel(
+    small, k, v, z, vt, edge, par, gated, gate, local, carry, kt, zt, w
+):
+    for s in range(SUB):
+        rows = slice(s * LANES, (s + 1) * LANES)
+        kt[across(s), :] = k[rows, :].astype(F32).T
+        vt[across(s), :] = v[rows, :].astype(F32).T
+        zt[across(s), :] = z[rows, :].T
+        rate = small[0:POLES, rows]
+        par[pl.ds(s, POLES, stride=SUB), :] = jnp.exp(-rate)
+        par[pl.ds(SUB * POLES + s, POLES, stride=SUB), :] = small[
+            POLES : 2 * POLES, rows
+        ] * jnp.sqrt(
+            one_minus_exp(2.0 * rate)
+        )
+        par[pl.ds(2 * SUB * POLES + s, TAPS, stride=SUB), :] = small[
+            2 * POLES : 2 * POLES + TAPS, rows
+        ]
+    for n, ref in enumerate((kt, zt, vt)):
+        edge[n * SUB * EDGE : (n + 1) * SUB * EDGE, :] = ref[0 : SUB * EDGE, :]
     count = LEN - EDGE
     taps = [tap_of(par, j) for j in range(TAPS)]
 
@@ -163,8 +165,11 @@
     scan_down(par, zt, gated, w, local, count, EDGE, True, read, write, 4)
 
 
-def edge_kernel(kt, tail, vt, zt, par, carry, gated, gate, local, out, w, gather, spread):
-    keys = [tail[tile(n), :] for n in range(HALO)] + [kt[tile(n), :] for n in range(EDGE)]
+def edge_kernel(edge, tail, par, carry, gated, gate, local, out, w, gather, spread, held):
+    held[...] = tail[...].astype(F32)
+    rows = SUB * EDGE
+    kt, zt, vt = (edge.at[pl.ds(n * rows, rows), :] for n in range(3))
+    keys = [held[tile(n), :] for n in range(HALO)] + [kt[tile(n), :] for n in range(EDGE)]
     taps = [tap_of(par, j) for j in range(TAPS)]
     for t in range(EDGE):
         now = taps[0] * keys[t + HALO]
@@ -181,20 +186,20 @@
 
     def write(r, n, value):
         if r == POLES:
-            row, slot = 6, n
+            row, slot = 20, n
         elif n == 3:
             return
         else:
             half, slot = divmod(r, SUB)
-            row = {2: 0, 0: 2, 1: 4}.get(n, 8 + 2 * (n - 4)) + half
+            row = {2: 0, 0: 2, 1: 4}.get(n, 6 + 2 * (n - 4)) + half
         gather[tile(row * SUB + slot), :] = value
 
     scan_down(par, zt, gated, w, local, EDGE, 0, False, read, write, EDGE)
     zero = jnp.zeros((SUB, LANES), F32)
-    gather[tile(6 * SUB + TAPS), :] = zero
+    gather[tile(20 * SUB + TAPS), :] = zero
     for row in range(ROWS_OUT):
         for s in range(SUB):
-            if row in (7, 22, 23):
+            if row == ROWS_OUT - 1:
                 block = zero
             else:
                 block = to_owner(gather[pl.ds(row * SUB * SUB + s, SUB, stride=SUB), :])
@@ -214,7 +219,7 @@
     coef = pattern(mine, 2) * weight
     leap = jnp.exp(-float(LEN) * rate)
     zero = jnp.zeros((SUB, LANES), F32)
-    ahead, pole, total = zero, zero, zero
+    ahead, pole, total, taps = zero, zero, zero, zero
     for d in range(count):
         y[pl.ds(d * ROWS_BACK, 2), :] = ahead[0:2, :]
         now = x[pl.ds(d * ROWS_OUT, SUB), :]
@@ -224,12 +229,14 @@
     back, low, high = zero, zero, zero
     for d in reversed(range(count)):
         y[pl.ds(d * ROWS_BACK + 2, 2), :] = back[0:2, :]
-        low = low + back * x[pl.ds(d * ROWS_OUT + SUB, SUB), :]
-        high = high + back * x[pl.ds(d * ROWS_OUT + 2 * SUB, SUB), :]
+        low = low + back * x[pl.ds(d * ROWS_OUT + 6, SUB), :]
+        last = x[pl.ds(d * ROWS_OUT + 14, SUB), :]
+        high = high + back * last
+        taps = taps + last
         back = back * leap + pattern(x, d * ROWS_OUT + 2)
     poles = (pole[0:2, :] + total[4:6, :]) * weight[0:2, :] * scale
     group = lane_group()[0:1, :]
-    short = total[6:7, :]
+    short = taps[6:7, :]
     for part, first in ((low * coef, 0), (high * coef, 4)):
         part = part + pltpu.roll(part, SUB - 1, 0)
         for shift in (16, 32, 64):
@@ -246,36 +253,24 @@
     out[...] = y[...].astype(BF16)
 
 
-def leave_kernel(
-    arrived, gated_a, gated_b, gate_a, gate_b, local_a, local_b, vt, head, par, cot,
-    grad_q, grad_k, grad_v, grad_short, x, state, long_out, slope, vals,
-):
-    x[...] = arrived[...].astype(F32)
-    for s in range(SUB):
-        for row in range(4):
-            block = x[pl.ds(s * SUB * ROWS_BACK + row, SUB, stride=ROWS_BACK), :]
-            state[pl.ds(row * SUB * SUB + s, SUB, stride=SUB), :] = from_owner(block)
-        coarse = x[pl.ds(s * SUB * ROWS_BACK + 6, SUB, stride=ROWS_BACK), :]
-        fine = x[pl.ds(s * SUB * ROWS_BACK + 7, SUB, stride=ROWS_BACK), :]
-        grad_short[s * LANES : (s + 1) * LANES, :] = from_owner(coarse + fine)[0:TAPS, :].T
-
+def forward_kernel(gated_a, gated_b, par, own_out):
     half = POLES // 2
     for part in range(2):
         modes = range(part * half, (part + 1) * half)
         decay = [decay_of(par, r) for r in modes]
         coef = [coef_of(par, r) for r in modes]
-        ahead = tuple(state[tile(r), :] for r in modes)
+        ahead = (jnp.zeros((SUB, LANES), F32),) * half
 
         def forward(i, ahead, source, base, part=part, decay=decay, coef=coef):
             now = source[tile(i), :]
-            total = None if part == 0 else long_out[tile(i + base), :]
+            total = None if part == 0 else own_out[tile(i + base), :]
             after = []
             for h, d, c in zip(ahead, decay, coef):
                 h = h + now
                 term = c * h
                 total = term if total is None else total + term
                 after.append(h * d)
-            long_out[tile(i + base), :] = total
+            own_out[tile(i + base), :] = total
             return tuple(after)
 
         ahead = lax.fori_loop(
@@ -285,69 +280,94 @@
             0, LEN - EDGE, functools.partial(forward, source=gated_a, base=EDGE), ahead, unroll=4
         )
 
+
+def add_up(terms):
+    terms = list(terms)
+    while len(terms) > 1:
+        terms = [a + b for a, b in zip(terms[0::2], terms[1::2])]
+    return terms[0]
+
+
+def unpack(arrived, x, state, first):
+    x[...] = arrived[...].astype(F32)
+    for s in range(SUB):
+        for row in range(2):
+            block = x[pl.ds(s * SUB * ROWS_BACK + first + row, SUB, stride=ROWS_BACK), :]
+            state[pl.ds(row * SUB * SUB + s, SUB, stride=SUB), :] = from_owner(block)
+
+
+def query_kernel(arrived, own_out, par, cot, grad_q, grad_short, x, state, long_out):
+    unpack(arrived, x, state, 0)
+    for s in range(SUB):
+        coarse = x[pl.ds(s * SUB * ROWS_BACK + 6, SUB, stride=ROWS_BACK), :]
+        fine = x[pl.ds(s * SUB * ROWS_BACK + 7, SUB, stride=ROWS_BACK), :]
+        grad_short[:, s * LANES : (s + 1) * LANES] = from_owner(coarse + fine)[0:TAPS, :]
     decay = [decay_of(par, r) for r in range(POLES)]
-    back = [state[tile(POLES + r), :] for r in range(POLES)]
+
+    def forward(t, terms):
+        long_out[tile(t), :] = own_out[tile(t), :] + add_up(terms)
+        return tuple(q * d for q, d in zip(terms, decay))
+
+    terms = tuple(coef_of(par, r) * state[tile(r), :] for r in range(POLES))
+    lax.fori_loop(0, LEN, forward, terms, unroll=4)
+    for s in range(SUB):
+        rows = slice(s * LANES, (s + 1) * LANES)
+        grad_q[rows, :] = (cot[rows, :].astype(F32) * long_out[across(s), :].T).astype(BF16)
+
+
+def key_kernel(
+    arrived, gate_a, gate_b, local_a, local_b, vt, head, par, grad_k, grad_v, x, state, slope, vals
+):
+    unpack(arrived, x, state, 2)
+    decay = [decay_of(par, r) for r in range(POLES)]
+    back = [state[tile(r), :] for r in range(POLES)]
+    growth = [1.0 / d for d in decay]
+    ahead = []
     for n in range(HALO):
-        total = coef_of(par, 0) * back[0]
-        for r in range(1, POLES):
-            total = total + coef_of(par, r) * back[r]
-        slope[tile(LEN + n), :] = total * head[tile(HALO + n), :]
+        ahead.append(
+            add_up(coef_of(par, r) * back[r] for r in range(POLES)) * head[tile(EDGE + n), :]
+        )
         if n < HALO - 1:
             z_now = head[tile(n), :]
-            back = [(b - z_now) / d for b, d in zip(back, decay)]
-
-    def backward(i, terms, local, gate, count, base):
+            back = [(b - z_now) * g for b, g in zip(back, growth)]
+    taps = [tap_of(par, j) for j in range(TAPS)]
+
+    def backward(i, carry, local, gate, count, base):
+        terms, ahead = carry
         t = count - 1 - i
         terms = tuple(q * d for q, d in zip(terms, decay))
-        total = local[tile(t), :]
-        sums = list(terms)
-        while len(sums) > 1:
-            sums = [a + b for a, b in zip(sums[0::2], sums[1::2])]
-        total = total + sums[0]
-        slope[tile(t + base), :] = total * vt[tile(t + base), :]
+        total = local[tile(t), :] + add_up(terms)
         vals[tile(t + base), :] = total * gate[tile(t), :]
-        return terms
-
-    terms = tuple(coef_of(par, r) * state[tile(POLES + r), :] for r in range(POLES))
-    terms = lax.fori_loop(
+        slopes = (total * vt[tile(t + base), :], *ahead)
+        slope[tile(t + base), :] = functools.reduce(
+            lambda a, b: a + b, [taps[j] * slopes[j] for j in range(TAPS)]
+        )
+        return terms, slopes[:HALO]
+
+    terms = tuple(coef_of(par, r) * state[tile(r), :] for r in range(POLES))
+    carry = (terms, tuple(ahead))
+    carry = lax.fori_loop(
         0, LEN - EDGE,
         functools.partial(backward, local=local_a, gate=gate_a, count=LEN - EDGE, base=EDGE),
-        terms, unroll=4,
+        carry, unroll=4,
     )
     lax.fori_loop(
         0, EDGE,
         functools.partial(backward, local=local_b, gate=gate_b, count=EDGE, base=0),
-        terms, unroll=EDGE,
-    )
-
-    taps = [tap_of(par, j) for j in range(TAPS)]
-
-    def spread_taps(i, after):
-        t = LEN - 1 - i
-        slopes = (slope[tile(t), :], *after)
-        total = taps[0] * slopes[0]
-        for j in range(1, TAPS):
-            total = total + taps[j] * slopes[j]
-        slope[tile(t), :] = total
-        return slopes[:HALO]
-
-    lax.fori_loop(
-        0, LEN, spread_taps, tuple(slope[tile(LEN + n), :] for n in range(HALO)), unroll=4
+        carry, unroll=EDGE,
     )
     for s in range(SUB):
         rows = slice(s * LANES, (s + 1) * LANES)
-        grad_q[rows, :] = (cot[rows, :].astype(F32) * long_out[across(s), :].T).astype(BF16)
         grad_k[rows, :] = slope[across(s), :].T.astype(BF16)
         grad_v[rows, :] = vals[across(s), :].T.astype(BF16)
 
 
-def pole_kernel(a, b, c, d, out, x, y):
-    x[...] = (a[...].astype(F32) + b[...].astype(F32)) + (c[...].astype(F32) + d[...].astype(F32))
+def pole_kernel(near, far, out, x):
+    x[...] = near[...].astype(F32) + far[...].astype(F32)
     for s in range(SUB):
         for half in range(2):
             block = x[pl.ds(s * SUB * 2 + half, SUB, stride=2), :]
-            y[half * SUB : (half + 1) * SUB, :] = from_owner(block)
-        out[s * LANES : (s + 1) * LANES, :] = y[...].T
+            out[half * SUB : (half + 1) * SUB, s * LANES : (s + 1) * LANES] = from_owner(block)
 
 
 def call(kernel, name, outs, scratch, operands, in_specs=None, flops=0, moved=0):
@@ -377,31 +397,27 @@
     scale = (length * count) ** (-0.5)
     full, edge = SUB * LEN, SUB * EDGE
     inner = full - edge
-    tile_bytes = SUB * LANES * 4
-
-    kt, vt, zt, tail, head, par = call(
-        enter_kernel,
-        "enter",
-        [shape(full)] * 3 + [shape(SUB * HALO), shape(2 * SUB * HALO), shape(SUB * 40)],
-        [],
-        (q_in, k_in, v_in, cotangent, rates, residues, taps_short),
-        flops=4 * 10**6,
-        moved=3 * 10**6,
-    )
+
+    tail = k_in[:, length - HALO :].T.reshape(SUB * HALO, LANES)
     tail = lax.ppermute(tail, "seq", [(i, i + 1) for i in range(count - 1)])
-    head = lax.ppermute(head, "seq", [(i + 1, i) for i in range(count - 1)])
-
-    gated_a, gate_a, local_a, carry = call(
+    grad_z = q_in.astype(F32) * cotangent.astype(F32)
+    small = jnp.concatenate([rates.T, residues.T, taps_short.T])
+    vt, ends, par, gated_a, gate_a, local_a, carry = call(
         inner_kernel,
         "inner",
-        [shape(inner)] * 3 + [shape(SUB * (POLES * CARRY + TAPS))],
-        [pltpu.VMEM((TAPS, inner, LANES), F32)],
-        (kt, vt, zt, par),
+        [shape(full), shape(3 * edge), shape(SUB * 40)]
+        + [shape(inner)] * 3
+        + [shape(SUB * (POLES * CARRY + TAPS))],
+        [
+            pltpu.VMEM((full, LANES), F32),
+            pltpu.VMEM((full, LANES), F32),
+            pltpu.VMEM((TAPS, inner, LANES), F32),
+        ],
+        (small, k_in, v_in, grad_z),
         flops=48 * 10**6,
         moved=4 * 10**6,
     )
-    first = pl.BlockSpec((edge, LANES), lambda i: (0, 0), memory_space=pltpu.VMEM)
-    whole = pl.BlockSpec(memory_space=pltpu.VMEM)
+    head = lax.ppermute(ends[edge:], "seq", [(i + 1, i) for i in range(count - 1)])
     gated_b, gate_b, local_b, message = call(
         edge_kernel,
         "edge",
@@ -410,25 +426,35 @@
             pltpu.VMEM((TAPS, edge, LANES), F32),
             pltpu.VMEM((SUB * SUB * ROWS_OUT, LANES), F32),
             pltpu.VMEM((count * ROWS_OUT, LANES), F32),
+            pltpu.VMEM((SUB * HALO, LANES), F32),
         ],
-        (kt, tail, vt, zt, par, carry),
-        [first, whole, first, first, whole, whole],
+        (ends, tail, par, carry),
         flops=6 * 10**6,
         moved=2 * 10**6,
     )
 
     def exchange(x, rows):
-        x = x.reshape(count, rows, LANES)
+        x = x.reshape(count, rows // 2, 2, LANES)
         return lax.all_to_all(x, "seq", split_axis=0, concat_axis=0, tiled=True)
 
     arrived = exchange(message, ROWS_OUT).reshape(count * ROWS_OUT, LANES)
+    (own_out,) = call(
+        forward_kernel,
+        "forward",
+        [shape(full)],
+        [],
+        (gated_a, gated_b, par),
+        flops=10 * 10**6,
+        moved=10**6,
+    )
     start = (index // SUB) * LANES + ((SUB - index % SUB) % SUB) * 16
     mine = jnp.concatenate(
         [
-            lax.dynamic_slice(a, (start, 0), (16, POLES)).T.reshape(2, LANES)
+            lax.dynamic_slice(a.T, (0, start), (POLES, 16)).reshape(2, LANES)
             for a in (rates, residues)
         ]
     )
+    arrived, own_out, head, mine = lax.optimization_barrier((arrived, own_out, head, mine))
     (back,) = call(
         functools.partial(owner_kernel, count, scale),
         "owner",
@@ -439,39 +465,48 @@
         moved=10**6,
     )
     returned = exchange(back, ROWS_BACK)
-    poles = returned[:, 4:6, :].reshape(2 * count, LANES)
-    others = [
-        lax.ppermute(poles, "chan", [(i, (i + n) % chans) for i in range(chans)])
-        for n in range(1, chans)
+    poles = returned[:, 2].reshape(2 * count, LANES)
+    returned = returned.reshape(count * ROWS_BACK, LANES)
+
+    def other(x, bit):
+        return lax.ppermute(x, "chan", [(i, i ^ bit) for i in range(chans)])
+
+    swap = [
+        pltpu.VMEM((count * ROWS_BACK, LANES), F32),
+        pltpu.VMEM((SUB * POLES, LANES), F32),
     ]
-    grad_q, grad_k, grad_v, grad_short = call(
-        leave_kernel,
-        "leave",
-        [shape(channels, BF16)] * 3 + [shape(channels, F32, TAPS)],
-        [
-            pltpu.VMEM((count * ROWS_BACK, LANES), F32),
-            pltpu.VMEM((SUB * 2 * POLES, LANES), F32),
-            pltpu.VMEM((full, LANES), F32),
-            pltpu.VMEM((full + SUB * HALO, LANES), F32),
-            pltpu.VMEM((full, LANES), F32),
-        ],
-        (
-            returned.reshape(count * ROWS_BACK, LANES),
-            gated_a, gated_b, gate_a, gate_b, local_a, local_b, vt, head, par, cotangent,
-        ),
-        flops=16 * 10**6,
-        moved=3 * 10**6,
+    poles_near = other(poles, 1)
+    grad_q, grad_short = call(
+        query_kernel,
+        "query",
+        [shape(channels, BF16), shape(TAPS, F32, channels)],
+        [*swap, pltpu.VMEM((full, LANES), F32)],
+        (returned, own_out, par, cotangent),
+        flops=5 * 10**6,
+        moved=10**6,
+    )
+    poles_near, grad_q = lax.optimization_barrier((poles_near, grad_q))
+    poles = (poles.astype(F32) + poles_near.astype(F32)).astype(BF16)
+    poles_far = other(poles, 2)
+    grad_k, grad_v = call(
+        key_kernel,
+        "key",
+        [shape(channels, BF16)] * 2,
+        [*swap, pltpu.VMEM((full, LANES), F32), pltpu.VMEM((full, LANES), F32)],
+        (returned, gate_a, gate_b, local_a, local_b, vt, head, par),
+        flops=8 * 10**6,
+        moved=2 * 10**6,
     )
     (grad_residues,) = call(
         pole_kernel,
         "poles",
-        [shape(channels, F32, POLES)],
-        [pltpu.VMEM((2 * count, LANES), F32), pltpu.VMEM((POLES, LANES), F32)],
-        (poles, *others),
+        [shape(POLES, F32, channels)],
+        [pltpu.VMEM((2 * count, LANES), F32)],
+        (poles, poles_far),
         flops=10**5,
         moved=10**5,
     )
-    return grad_q, grad_k, grad_v, grad_short, grad_residues
+    return grad_q, grad_k, grad_v, grad_short.T, grad_residues.T
 
 
 def solution(mesh):

time: 77.4 us -> 70.8 us (0.915)
  blocking collectives: 0 us -> 16.4 us
  waiting for transfers between devices: 22.8 us -> 10.4 us
  starting transfers between devices: 28.8 us -> 22.4 us
  local copies, waits for them, and re-layouts: 5.45 us -> 2.53 us
  Pallas kernels: 19 us -> 17.9 us
    all_to_all x0 -> x1, blocking collectives: none -> 16.4 us  [exchange(): return lax.all_to_all(x, 'seq', split_axis=0, concat_axis=0, tiled=True)]
    all_to_all x2 -> x1, waiting for transfers between devices: 22.8 us -> 7.87 us  [exchange(): return lax.all_to_all(x, 'seq', split_axis=0, concat_axis=0, tiled=True)]
    all_to_all x2 -> x1, starting transfers between devices: 16.9 us -> 11.3 us  [exchange(): return lax.all_to_all(x, 'seq', split_axis=0, concat_axis=0, tiled=True)]
    unnamed x17 -> x14, local copies, waits for them, and re-layouts: 4.46 us -> 0.95 us
    ppermute x4 -> x3, waiting for transfers between devices: 0.01 us -> 2.49 us  [the longest x1 2.48 us: per_device(): lax.ppermute(ends[edge:], 'seq', [(i + 1, i) for i in range(count - 1)])]
    pallas_call x6 -> x7, Pallas kernels: 19 us -> 17.9 us  [call(): pl.pallas_call(kernel, grid=(1,) if in_specs else (), out_shape=outs, in_...]
    ppermute x4 -> x3, starting transfers between devices: 7.43 us -> 6.45 us  [the longest x2 4.09 us: other(): return lax.ppermute(x, 'chan', [(i, i ^ bit) for i in range(chans)])]
  transfers between devices with their start and end apart: 7 -> 5, of which waited for: 2 -> 2; matrix products, arithmetic and copies ran while one was open for 2% -> 0% of each run, Pallas kernels for 19% -> 21%
where the time goes in v2:
time: 70.8 us; the launch traced here: 70.5 us
  starting transfers between devices  22.4 us (32%)
  Pallas kernels  17.9 us (25%)
  blocking collectives  16.4 us (23%)
  waiting for transfers between devices  10.4 us (15%)
  local copies, waits for them, and re-layouts  2.53 us (4%)
  between operations  0.87 us (1%)
    pallas_call x7, Pallas kernels, call(): pl.pallas_call(kernel, grid=(1,) if in_specs else (), out_shape=outs, in_...  17.9 us
    all_to_all x1, blocking collectives, exchange(): return lax.all_to_all(x, 'seq', split_axis=0, concat_axis=0, tiled=True)  16.4 us
    all_to_all x1, starting transfers between devices, exchange(): return lax.all_to_all(x, 'seq', split_axis=0, concat_axis=0, tiled=True)  11.3 us
    all_to_all x1, waiting for transfers between devices, exchange(): return lax.all_to_all(x, 'seq', split_axis=0, concat_axis=0, tiled=True)  7.87 us
    ppermute x1, starting transfers between devices, per_device(): tail = lax.ppermute(tail, 'seq', [(i, i + 1) for i in range(count - 1)])  4.64 us
    ppermute x2, starting transfers between devices, other(): return lax.ppermute(x, 'chan', [(i, i ^ bit) for i in range(chans)])  4.09 us
    ppermute x1, waiting for transfers between devices, per_device(): lax.ppermute(ends[edge:], 'seq', [(i + 1, i) for i in range(count - 1)])  2.48 us
    ppermute x1, starting transfers between devices, per_device(): lax.ppermute(ends[edge:], 'seq', [(i + 1, i) for i in range(count - 1)])  2.36 us
  transfers between devices with their start and end apart: 5, of which 2 were waited for; matrix products, arithmetic and copies ran while one was open for 0% of the time, Pallas kernels for 21%

profile of v2, /device:TPU:1, one launch (start us, length us, event | category | flops | bytes accessed | tf_op | source)
XLA Modules:
  0.0 70.5 jit_solution(3038094768647842925)
XLA Ops:
  0.6 0.0 copy-start.3
  0.6 1.1 %slice_bitcast_fusion = bf16[6,1024]{0,1:T(8,128)(2,1)S(1)} fusion(bf16[1024,128]{1,0:T(8,128)(2,1)} %k.1), kind=kLoop, calls=%fused_computation.1 | loop fusion | bytes 24576 | tf_op jit(solution)/shard_map/transpose | solution.py:401
  1.8 0.0 copy-start.1
  1.8 0.1 copy.15
  1.9 0.1 reshape.31
  2.0 0.0 copy-start.4
  2.0 0.0 copy-start.5
  2.0 0.0 copy-start.6
  2.0 4.6 %collective-permute-start = (bf16[48,128]{1,0:T(8,128)(2,1)S(1)}, bf16[48,128]{1,0:T(8,128)(2,1)S(1)}, u32[]{:S(2)}, u32[]{:S(2)}) collective-permute-start(bf16[48,128]{1,0:T(8,128)(2,1)S(1)} %reshape.31), channel_id=1, source_target_pairs={{0,4},{4,8},{8,12},{12,16},{16,20},{20,24},{24,28},{28,32},{32,36}... | collective-permute-start | bytes 36872 | tf_op jit(solution)/shard_map/ppermute | solution.py:402
  6.7 0.0 copy-done.3
  6.7 0.0 copy-done.1
  6.7 0.0 copy-start.2
  6.7 0.1 convert_multiply_fusion.z
  6.8 0.0 copy-start
  6.8 0.0 copy-done.4
  6.8 0.0 copy-done.5
  6.8 0.0 copy-done.6
  6.8 0.8 %copy-done.2 = bf16[1024,128]{1,0:T(8,128)(2,1)S(1)} copy-done((bf16[1024,128]{1,0:T(8,128)(2,1)S(1)}, bf16[1024,128]{1,0:T(8,128)(2,1)}, u32[]{:S(2)}) %copy-start.2) | copy-done | bytes 262168
  7.6 0.1 copy-done
  7.7 8.7 %inner.1 = (f32[1024,128]{1,0:T(8,128)S(1)}, f32[192,128]{1,0:T(8,128)S(1)}, f32[320,128]{1,0:T(8,128)S(1)}, f32[960,128]{1,0:T(8,128)S(1)}, f32[960,128]{1,0:T(...) custom-call(f32[39,1024]{1,0:T(8,128)S(1)} %pad_maximum_fusion.small, bf16[1024,128]{1,0:T(8,128)(2,1)S(1)} %copy-done, ...), custom_call_target="tpu_custom_call" | custom-call | flops 48000000 | bytes 4000000 | tf_op jit(solution)/shard_map/inner/pallas_call | solution.py:374
  16.4 0.0 collective-permute-done.tail
  16.4 1.6 %edge.1 = (f32[64,128]{1,0:T(8,128)S(1)}, f32[64,128]{1,0:T(8,128)S(1)}, f32[64,128]{1,0:T(8,128)S(1)}, bf16[1408,128]{1,0:T(8,128)(2,1)}) custom-call(f32[192,128]{1,0:T(8,128)S(1)} %get-tuple-element.26.edge, bf16[48,128]{1,0:T(8,128)(2,1)S(1)} %collective-permute-done.tail, f32[320,128]{1,0:T(8,128)S(1)} %get-tuple-element.27.par, ...), custom_call_target="tpu_custom_call" | custom-call | flops 6000000 | bytes 2000000 | tf_op jit(solution)/shard_map/edge/pallas_call | solution.py:374
  18.1 11.3 %all-to-all-start = ((bf16[64,11,2,128]{3,2,1,0:T(2,128)(2,1)}), bf16[64,11,2,128]{3,2,1,0:T(2,128)(2,1)S(1)}, u32[]{:S(2)}, u32[]{:S(2)}) async-start(bf16[64,11,2,128]{3,2,1,0:T(2,128)(2,1)} %bitcast.4), calls=%async_computation | async-start | bytes 720896 | tf_op jit(solution)/shard_map/all_to_all | solution.py:438
  29.4 2.4 %collective-permute-start.1 = (f32[128,128]{1,0:T(8,128)S(1)}, f32[128,128]{1,0:T(8,128)S(1)}, u32[]{:S(2)}, u32[]{:S(2)}) collective-permute-start(f32[128,128]{1,0:T(8,128)S(1)} %slice.10), channel_id=1, source_target_pairs={{4,0},{8,4},{12,8},{16,12},{20,16},{24,20},{28,24},{32,28},{36,32}... | collective-permute-start | bytes 196616 | tf_op jit(solution)/shard_map/ppermute | solution.py:420
  31.8 0.1 dynamic-slice_bitcast_fusion
  31.9 0.1 reshape.35
  31.9 0.1 reshape.34
  32.0 1.5 %forward.1.own_out = f32[1024,128]{1,0:T(8,128)S(1)} custom-call(f32[960,128]{1,0:T(8,128)S(1)} %get-tuple-element.30.gated_a, f32[64,128]{1,0:T(8,128)S(1)} %get-tuple-element.31.gated_b, f32[320,128]{1,0:T(8,128)S(1)} %get-tuple-element.27.par), custom_call_target="tpu_custom_call" | custom-call | flops 10000000 | bytes 1000000 | tf_op jit(solution)/shard_map/forward/pallas_call | solution.py:374
  33.5 2.5 %collective-permute-done.1.head = f32[128,128]{1,0:T(8,128)S(1)} collective-permute-done((f32[128,128]{1,0:T(8,128)S(1)}, f32[128,128]{1,0:T(8,128)S(1)}, u32[]{:S(2)}, u32[]{:S(2)}) %collective-permute-start.1) | collective-permute-done | bytes 65568 | tf_op jit(solution)/shard_map/ppermute | solution.py:420
  36.0 7.9 %all-to-all-done = bf16[64,11,2,128]{3,2,1,0:T(2,128)(2,1)S(1)} async-done(((bf16[64,11,2,128]{3,2,1,0:T(2,128)(2,1)}), bf16[64,11,2,128]{3,2,1,0:T(2,128)(2,1)S(1)}, u32[]{:S(2)}, u32[]{:S(2)}) %all-to-all-start) | async-done | bytes 360480 | tf_op jit(solution)/shard_map/all_to_all | solution.py:438
  43.9 0.5 owner.1
  44.3 16.4 %all_to_all.10 = bf16[64,4,2,128]{3,2,1,0:T(2,128)(2,1)S(1)} all-to-all(bf16[64,4,2,128]{3,2,1,0:T(2,128)(2,1)S(1)} %bitcast.19), channel_id=1, replica_groups=mesh['seq'=64,'chan'=4] {'seq'}, dimensions={0} | all-to-all | bytes 262144 | tf_op jit(solution)/shard_map/all_to_all | solution.py:438
  60.7 1.4 %collective-permute-start.2 = (bf16[128,128]{1,0:T(8,128)(2,1)S(1)}, bf16[128,128]{1,0:T(8,128)(2,1)S(1)}, u32[]{:S(2)}, u32[]{:S(2)}) collective-permute-start(bf16[128,128]{1,0:T(8,128)(2,1)S(1)} %bitcast.20), channel_id=1, source_target_pairs={{0,1},{1,0},{2,3},{3,2},{4,5},{5,4},{6,7},{7,6},{8,9},{9,8},{10,11... | collective-permute-start | bytes 98312 | tf_op jit(solution)/shard_map/ppermute | solution.py:472
  62.1 2.0 %query.1 = (bf16[1024,128]{1,0:T(8,128)(2,1)}, f32[7,1024]{1,0:T(8,128)}) custom-call(bf16[512,128]{1,0:T(8,128)(2,1)S(1)} %bitcast.17, f32[1024,128]{1,0:T(8,128)S(1)} %forward.1.own_out, f32[320,128]{1,0:T(8,128)S(1)} %get-tuple-element.27.par, bf16[1024,128]{1,0:T(8,128)(2,1)S(1)} %copy-done.1), custom_call_target="tpu_custom_call" | custom-call | flops 5000000 | bytes 1000000 | tf_op jit(solution)/shard_map/query/pallas_call | solution.py:374
  64.1 0.0 collective-permute-done.2
  64.1 2.7 %collective-permute-start.3 = (bf16[128,128]{1,0:T(8,128)(2,1)S(1)}, bf16[128,128]{1,0:T(8,128)(2,1)S(1)}, u32[]{:S(2)}, u32[]{:S(2)}) collective-permute-start(bf16[128,128]{1,0:T(8,128)(2,1)S(1)} %add_convert_fusion.near), channel_id=1, source_target_pairs={{0,2},{1,3},{2,0},{3,1},{4,6},{5,7},{6,4},{7,5},{8,10},{9,11},{10,... | collective-permute-start | bytes 98312 | tf_op jit(solution)/shard_map/ppermute | solution.py:472
  66.8 2.7 %key.1 = (bf16[1024,128]{1,0:T(8,128)(2,1)}, bf16[1024,128]{1,0:T(8,128)(2,1)}) custom-call(bf16[512,128]{1,0:T(8,128)(2,1)S(1)} %bitcast.18, f32[960,128]{1,0:T(8,128)S(1)} %get-tuple-element.37.gate_a, f32[64,128]{1,0:T(8,128)S(1)} %get-tuple-element.38.gate_b, f32[960,128]{1,0:T(8,128)S(1)} %get-tuple-element.39.local_a, ...), custom_call_target="tpu_custom_call" | custom-call | flops 8000000 | bytes 2000000 | tf_op jit(solution)/shard_map/key/pallas_call | solution.py:374
  69.5 0.0 collective-permute-done.3.far
  69.5 1.1 %poles.1 = f32[16,1024]{1,0:T(8,128)} custom-call(bf16[128,128]{1,0:T(8,128)(2,1)S(1)} %add_convert_fusion.near, bf16[128,128]{1,0:T(8,128)(2,1)S(1)} %collective-permute-done.3.far), custom_call_target="tpu_custom_call" | custom-call | flops 100000 | bytes 100000 | tf_op jit(solution)/shard_map/poles/pallas_call | solution.py:374
  (5 shorter events, 0.1 us)
Async XLA Ops:
  0.6 6.0 %copy-start.3 = (bf16[1024,128]{1,0:T(8,128)(2,1)S(1)}, bf16[1024,128]{1,0:T(8,128)(2,1)}, u32[]{:S(2)}) copy-start(bf16[1024,128]{1,0:T(8,128)(2,1)} %param.7) | copy-start | bytes 786436
  1.8 4.9 %copy-start.1 = (bf16[1024,128]{1,0:T(8,128)(2,1)S(1)}, bf16[1024,128]{1,0:T(8,128)(2,1)}, u32[]{:S(2)}) copy-start(bf16[1024,128]{1,0:T(8,128)(2,1)} %cot.1) | copy-start | bytes 786436
  2.0 4.8 %copy-start.4 = (f32[1024,16]{0,1:T(8,128)S(1)}, f32[1024,16]{0,1:T(8,128)}, u32[]{:S(2)}) copy-start(f32[1024,16]{0,1:T(8,128)} %param.12) | copy-start | bytes 196612
  2.0 4.8 %copy-start.5 = (f32[1024,16]{0,1:T(8,128)S(1)}, f32[1024,16]{0,1:T(8,128)}, u32[]{:S(2)}) copy-start(f32[1024,16]{0,1:T(8,128)} %param.13) | copy-start | bytes 196612
  2.0 4.8 %copy-start.6 = (f32[1024,7]{0,1:T(8,128)S(1)}, f32[1024,7]{0,1:T(8,128)}, u32[]{:S(2)}) copy-start(f32[1024,7]{0,1:T(8,128)} %param.11) | copy-start | bytes 86020
  2.0 14.4 %collective-permute-start = (bf16[48,128]{1,0:T(8,128)(2,1)S(1)}, bf16[48,128]{1,0:T(8,128)(2,1)S(1)}, u32[]{:S(2)}, u32[]{:S(2)}) collective-permute-start(bf16[48,128]{1,0:T(8,128)(2,1)S(1)} %reshape.31), channel_id=1, source_target_pairs={{0,4},{4,8},{8,12},{12,16},{16,20},{20,24},{24,28},{28,32},{32,36}... | collective-permute-start | bytes 36872 | tf_op jit(solution)/shard_map/ppermute | solution.py:402
  6.7 1.0 %copy-start.2 = (bf16[1024,128]{1,0:T(8,128)(2,1)S(1)}, bf16[1024,128]{1,0:T(8,128)(2,1)}, u32[]{:S(2)}) copy-start(bf16[1024,128]{1,0:T(8,128)(2,1)} %v.1) | copy-start | bytes 786436
  6.8 1.0 %copy-start = (bf16[1024,128]{1,0:T(8,128)(2,1)S(1)}, bf16[1024,128]{1,0:T(8,128)(2,1)}, u32[]{:S(2)}) copy-start(bf16[1024,128]{1,0:T(8,128)(2,1)} %k.1) | copy-start | bytes 786436
  18.1 25.8 %all-to-all-start = ((bf16[64,11,2,128]{3,2,1,0:T(2,128)(2,1)}), bf16[64,11,2,128]{3,2,1,0:T(2,128)(2,1)S(1)}, u32[]{:S(2)}, u32[]{:S(2)}) async-start(bf16[64,11,2,128]{3,2,1,0:T(2,128)(2,1)} %bitcast.4), calls=%async_computation | async-start | bytes 720896 | tf_op jit(solution)/shard_map/all_to_all | solution.py:438
  29.4 6.6 %collective-permute-start.1 = (f32[128,128]{1,0:T(8,128)S(1)}, f32[128,128]{1,0:T(8,128)S(1)}, u32[]{:S(2)}, u32[]{:S(2)}) collective-permute-start(f32[128,128]{1,0:T(8,128)S(1)} %slice.10), channel_id=1, source_target_pairs={{4,0},{8,4},{12,8},{16,12},{20,16},{24,20},{28,24},{32,28},{36,32}... | collective-permute-start | bytes 196616 | tf_op jit(solution)/shard_map/ppermute | solution.py:420
  60.7 3.4 %collective-permute-start.2 = (bf16[128,128]{1,0:T(8,128)(2,1)S(1)}, bf16[128,128]{1,0:T(8,128)(2,1)S(1)}, u32[]{:S(2)}, u32[]{:S(2)}) collective-permute-start(bf16[128,128]{1,0:T(8,128)(2,1)S(1)} %bitcast.20), channel_id=1, source_target_pairs={{0,1},{1,0},{2,3},{3,2},{4,5},{5,4},{6,7},{7,6},{8,9},{9,8},{10,11... | collective-permute-start | bytes 98312 | tf_op jit(solution)/shard_map/ppermute | solution.py:472
  64.1 5.4 %collective-permute-start.3 = (bf16[128,128]{1,0:T(8,128)(2,1)S(1)}, bf16[128,128]{1,0:T(8,128)(2,1)S(1)}, u32[]{:S(2)}, u32[]{:S(2)}) collective-permute-start(bf16[128,128]{1,0:T(8,128)(2,1)S(1)} %add_convert_fusion.near), channel_id=1, source_target_pairs={{0,2},{1,3},{2,0},{3,1},{4,6},{5,7},{6,4},{7,5},{8,10},{9,11},{10,... | collective-permute-start | bytes 98312 | tf_op jit(solution)/shard_map/ppermute | solution.py:472

commit v3 on v2

v3 whole, which is shorter than its diff:
```python
import functools

import jax
import jax.numpy as jnp
from jax import lax
from jax.experimental import pallas as pl
from jax.experimental.pallas import tpu as pltpu
from jax.sharding import PartitionSpec as P

F32 = jnp.float32
BF16 = jnp.bfloat16
LANES = 128
SUB = 8
LEN = 128
POLES = 16
TAPS = 7
HALO = TAPS - 1
EDGE = 8
MODE = 4 + TAPS
ROWS_OUT = 24
ROW_SHORT, ROW_V, ROW_MOMENT, ROW_K, ROW_Z = 6, 7, 8, 22, 23
ROWS_BACK = 8
VMEM = 48 * 1024 * 1024
VMEM_FIRST = 62 * 1024 * 1024


def one_minus_exp(x):
    series = 1.0 - x * (1.0 / 7.0)
    for order in (6.0, 5.0, 4.0, 3.0, 2.0):
        series = 1.0 - x * (1.0 / order) * series
    return x * series


def tile(index):
    if isinstance(index, int):
        return pl.ds(SUB * index, SUB)
    return pl.ds(pl.multiple_of(SUB * index, SUB), SUB)


def across(block):
    return pl.ds(block, LEN, stride=SUB)


def lane_group():
    return lax.broadcasted_iota(jnp.int32, (SUB, LANES), 1) // 16


def to_owner(x):
    y = pltpu.roll(x, 0, 1, stride=16, stride_axis=0)
    group = lane_group()
    for bit in (1, 2, 4):
        y = jnp.where((group & bit) != 0, pltpu.roll(y, SUB - bit, 0), y)
    return pltpu.roll(y, 0, 1, stride=16, stride_axis=0)


def skew_left(x):
    row = lax.broadcasted_iota(jnp.int32, (SUB, LANES), 0)
    for bit in (1, 2, 4):
        x = jnp.where((row & bit) != 0, pltpu.roll(x, LANES - 16 * bit, 1), x)
    return x


def from_owner(x):
    y = skew_left(x)
    group = lane_group()
    for bit in (1, 2, 4):
        y = jnp.where((group & bit) != 0, pltpu.roll(y, bit, 0), y)
    return skew_left(y)


def decay_of(par, r):
    return par[tile(r), :]


def coef_of(par, r):
    return par[tile(POLES + r), :]


def add_in_order(terms):
    return functools.reduce(lambda a, b: a + b, terms)


def tap_of(par, j):
    return par[tile(2 * POLES + j), :]


def scan_down(par, z, gated, w, local, gather):
    zero = jnp.zeros((SUB, LANES), F32)
    for pair in range(POLES // 2):
        modes = (2 * pair, 2 * pair + 1)
        decay = [decay_of(par, r) for r in modes]
        coef = [coef_of(par, r) for r in modes]
        final = pair == POLES // 2 - 1
        state = tuple(
            tuple(decay[n] if m == 3 else zero for m in range(MODE)) for n in range(2)
        )
        sums = (zero,) * TAPS if final else ()

        def step(i, carry, pair=pair, decay=decay, coef=coef, final=final):
            state, sums = carry
            t = LEN - 1 - i
            z_now = z[tile(t), :]
            g_now = gated[tile(t), :]
            w_now = [w[j, tile(t), :] for j in range(TAPS)]
            total = None if pair == 0 else local[tile(t), :]
            after = []
            for n in range(2):
                back, pole, ahead, power, *moments = state[n]
                back = back * decay[n] + z_now
                pole = pole + g_now * back
                ahead = ahead + power * g_now
                moments = [m + power * x for m, x in zip(moments, w_now)]
                power = power * decay[n]
                term = coef[n] * back
                total = term if total is None else total + term
                after.append((back, pole, ahead, power, *moments))
            local[tile(t), :] = total
            if final:
                sums = tuple(a + total * x for a, x in zip(sums, w_now))
            return tuple(after), sums

        state, sums = lax.fori_loop(0, LEN, step, (state, sums), unroll=4)
        for n, r in enumerate(modes):
            half, slot = divmod(r, SUB)
            back, pole, ahead, _, *moments = state[n]
            gather[tile(half * SUB + slot), :] = ahead
            gather[tile((2 + half) * SUB + slot), :] = back
            gather[tile((4 + half) * SUB + slot), :] = pole
            for j, value in enumerate(moments):
                gather[tile((ROW_MOMENT + 2 * j + half) * SUB + slot), :] = value
        for j, value in enumerate(sums):
            gather[tile(ROW_SHORT * SUB + j), :] = value


def first_kernel(*refs):
    sources, targets, refs = refs[:7], refs[7:15], refs[15:]
    (k, v, q, cot, rates, residues, amounts), refs = refs[:7], refs[7:]
    (vt, gate, gated, local, par, tail, head, message), refs = refs[:8], refs[8:]
    kt, zt, w, gather, spread, came, went = refs
    copies = [
        pltpu.make_async_copy(a, b, came.at[n])
        for n, (a, b) in enumerate(zip(sources, (k, v, q, cot, rates, residues, amounts)))
    ]
    leaving = [
        pltpu.make_async_copy(a, b, went.at[n])
        for n, (a, b) in enumerate(zip((vt, gate, gated, local, par, tail, head, message), targets))
    ]
    for copy in copies:
        copy.start()
    copies[0].wait()
    for s in range(SUB):
        kt[across(s), :] = k[s * LANES : (s + 1) * LANES, :].astype(F32).T
    copies[1].wait()
    for s in range(SUB):
        vt[across(s), :] = v[s * LANES : (s + 1) * LANES, :].astype(F32).T
    leaving[0].start()
    for copy in copies[2:]:
        copy.wait()
    for s in range(SUB):
        rows = slice(s * LANES, (s + 1) * LANES)
        zt[across(s), :] = (q[rows, :].astype(F32) * cot[rows, :].astype(F32)).T
        rate = rates[:, rows]
        par[pl.ds(s, POLES, stride=SUB), :] = jnp.exp(-rate)
        par[pl.ds(SUB * POLES + s, POLES, stride=SUB), :] = residues[:, rows] * jnp.sqrt(
            one_minus_exp(2.0 * rate)
        )
        par[pl.ds(2 * SUB * POLES + s, TAPS, stride=SUB), :] = amounts[:, rows]
    edge = SUB * EDGE
    last = slice(SUB * (LEN - HALO), SUB * LEN)
    tail[...] = kt[last, :]
    head[0:edge, :] = zt[0:edge, :]
    head[edge:, :] = vt[0:edge, :]
    for n in (4, 5, 6):
        leaving[n].start()
    for row, block in (
        (ROW_V, vt[0:edge, :]),
        (ROW_K, kt[SUB * (LEN - EDGE) : SUB * LEN, :]),
        (ROW_Z, zt[0:edge, :]),
    ):
        gather[row * edge : (row + 1) * edge, :] = block

    taps = [tap_of(par, j) for j in range(TAPS)]

    def prepare(t, before):
        keys = (kt[tile(t), :], *before)
        now = taps[0] * keys[0]
        for j in range(1, TAPS):
            now = now + taps[j] * keys[j]
        value = vt[tile(t), :]
        gate[tile(t), :] = now
        gated[tile(t), :] = now * value
        for j in range(TAPS):
            w[j, tile(t), :] = value * keys[j]
        return keys[:HALO]

    gather[tile(ROW_SHORT * SUB + TAPS), :] = jnp.zeros((SUB, LANES), F32)
    zero = gather[tile(ROW_SHORT * SUB + TAPS), :]
    lax.fori_loop(0, LEN, prepare, (zero,) * HALO, unroll=4)
    leaving[1].start()
    leaving[2].start()
    scan_down(par, zt, gated, w, local, gather)
    leaving[3].start()
    for row in range(ROWS_OUT):
        for s in range(SUB):
            block = to_owner(gather[pl.ds(row * SUB * SUB + s, SUB, stride=SUB), :])
            spread[pl.ds(s * SUB * ROWS_OUT + row, SUB, stride=ROWS_OUT), :] = block
    message[...] = spread[...].astype(BF16)
    leaving[7].start()
    for copy in leaving:
        copy.wait()


def owner_kernel(count, scale, arrived, mine, out, x, y, kept, fix):
    x[0:ROWS_OUT, :] = jnp.zeros((ROWS_OUT, LANES), F32)
    x[ROWS_OUT:, :] = arrived[...].astype(F32)
    even = lax.broadcasted_iota(jnp.int32, (SUB, LANES), 0) % 2 == 0
    group = lane_group()
    zero = jnp.zeros((SUB, LANES), F32)

    def pattern(ref, row):
        return jnp.where(even, ref[pl.ds(row, 1), :], ref[pl.ds(row + 1, 1), :])

    rate = pattern(mine, 0)
    weight = jnp.sqrt(one_minus_exp(2.0 * rate))
    coef = pattern(mine, 2) * weight
    leap = jnp.exp(-float(LEN) * rate)
    taps = [mine[pl.ds(4 + j, 1), :] for j in range(TAPS)]
    rates = [mine[pl.ds(half, 1), :] for half in range(2)]
    growth = [jnp.broadcast_to(jnp.exp(r), (SUB, LANES)) for r in rates]
    powers = [
        [jnp.broadcast_to(jnp.exp(-float(LEN - t) * r), (SUB, LANES)) for t in range(HALO)]
        for r in rates
    ]
    taps = [jnp.broadcast_to(tap, (SUB, LANES)) for tap in taps]

    source = lax.broadcasted_iota(jnp.int32, (LANES, SUB * LANES), 0)
    target = lax.broadcasted_iota(jnp.int32, (LANES, SUB * LANES), 1)
    same = (source // 16 == target // LANES) & (source % 16 == target % 16)
    everywhere = jnp.where(same, 1.0, 0.0).astype(BF16)
    for n, (row, first) in enumerate(((ROW_V, 1), (ROW_Z, 1), (ROW_K, 0))):
        rows = x[pl.ds(first * ROWS_OUT + row, count, stride=ROWS_OUT), :].astype(BF16)
        kept[n] = jnp.dot(rows, everywhere, preferred_element_type=F32)

    def edge_of(b):
        at = pl.ds(b * SUB, SUB)
        value, slope = (
            [kept[n, at, t * LANES : (t + 1) * LANES] for t in range(HALO)] for n in range(2)
        )
        key = [kept[2, at, (EDGE - m) * LANES : (EDGE - m + 1) * LANES] for m in range(1, TAPS)]
        return value, slope, [None, *key]

    def shards(row, b):
        return pl.ds((b * SUB + 1) * ROWS_OUT + row, SUB, stride=ROWS_OUT)

    fix[...] = jnp.zeros(fix.shape, F32)
    batches = count // SUB
    poles = [zero, zero]
    for b in range(batches):
        value, slope, key = edge_of(b)
        extra = [
            value[t] * add_in_order(taps[j] * key[j - t] for j in range(t + 1, TAPS))
            for t in range(HALO)
        ]
        for half in range(2):
            back = x[shards(2 + half, b), :]
            fix[pl.ds(b * SUB * SUB + half, SUB, stride=SUB), :] = add_in_order(
                extra[t] * powers[half][t] for t in range(HALO)
            )
            for t in range(HALO):
                poles[half] = poles[half] + extra[t] * back
                if t < HALO - 1:
                    back = (back - slope[t]) * growth[half]

    ahead, pole, total = zero, zero, zero
    for d in range(count):
        base = (d + 1) * ROWS_OUT
        y[pl.ds(d * ROWS_BACK, 2), :] = ahead[0:2, :]
        now = x[pl.ds(base, SUB), :]
        pole = pole + ahead * pattern(x, base + 2)
        total = total + now
        ahead = ahead * leap + (now + fix[tile(d), :])
    back, low, high = zero, zero, zero
    for d in reversed(range(count)):
        base = (d + 1) * ROWS_OUT
        y[pl.ds(d * ROWS_BACK + 2, 2), :] = back[0:2, :]
        low = low + back * x[pl.ds(base + SUB, SUB), :]
        high = high + back * x[pl.ds(base + 2 * SUB, SUB), :]
        back = back * leap + pattern(x, base + 2)

    edges = [[zero] * TAPS for _ in range(2)]
    for b in range(batches):
        value, slope, key = edge_of(b)
        start = b * SUB
        states = []
        for half in range(2):
            own = x[shards(2 + half, b), :]
            later = y[pl.ds(start * ROWS_BACK + 2 + half, SUB, stride=ROWS_BACK), :]
            states.append(own + later * powers[half][0])
        for t in range(HALO):
            for j in range(t + 1, TAPS):
                product = value[t] * key[j - t]
                for half in range(2):
                    edges[half][j] = edges[half][j] + states[half] * product
            states = [(a - slope[t]) * g for a, g in zip(states, growth)]

    def down(rows):
        return jnp.sum(rows, axis=0, keepdims=True)

    owned = jnp.concatenate([down(p) for p in poles])
    owned = (owned + pole[0:2, :] + total[4:6, :]) * weight[0:2, :] * scale
    short = total[ROW_SHORT : ROW_SHORT + 1, :]
    group = group[0:1, :]
    for part, first in ((low * coef, 0), (high * coef, 4)):
        part = part + pltpu.roll(part, SUB - 1, 0)
        for shift in (16, 32, 64):
            part = part + pltpu.roll(part, shift, 1)
        for n in range(min(4, TAPS - first)):
            short = short + jnp.where(group == first + n, part[2 * n : 2 * n + 1, :], 0.0)
    for j in range(1, TAPS):
        part = down(edges[0][j]) * coef[0:1, :] + down(edges[1][j]) * coef[1:2, :]
        for shift in (16, 32, 64):
            part = part + pltpu.roll(part, shift, 1)
        short = short + jnp.where(group == j, part, 0.0)
    short = short * scale
    coarse = short.astype(BF16).astype(F32)
    fine = short - coarse
    for d in range(count):
        y[pl.ds(d * ROWS_BACK + 4, 2), :] = owned
        y[pl.ds(d * ROWS_BACK + 6, 1), :] = coarse
        y[pl.ds(d * ROWS_BACK + 7, 1), :] = fine
    out[...] = y[...].astype(BF16)


def forward_kernel(gated, par, own_out):
    half = POLES // 2
    for part in range(2):
        modes = range(part * half, (part + 1) * half)
        decay = [decay_of(par, r) for r in modes]
        coef = [coef_of(par, r) for r in modes]
        ahead = (jnp.zeros((SUB, LANES), F32),) * half

        def forward(i, ahead, part=part, decay=decay, coef=coef):
            now = gated[tile(i), :]
            total = None if part == 0 else own_out[tile(i), :]
            after = []
            for h, d, c in zip(ahead, decay, coef):
                h = h + now
                term = c * h
                total = term if total is None else total + term
                after.append(h * d)
            own_out[tile(i), :] = total
            return tuple(after)

        lax.fori_loop(0, LEN, forward, ahead, unroll=4)


def halo_gates(tail, par):
    return [
        add_in_order(tap_of(par, j) * tail[tile(HALO + t - j), :] for j in range(t + 1, TAPS))
        for t in range(HALO)
    ]


def add_up(terms):
    terms = list(terms)
    while len(terms) > 1:
        terms = [a + b for a, b in zip(terms[0::2], terms[1::2])]
    return terms[0]


def unpack(arrived, x, state, first):
    x[...] = arrived[...].astype(F32)
    for s in range(SUB):
        for row in range(2):
            block = x[pl.ds(s * SUB * ROWS_BACK + first + row, SUB, stride=ROWS_BACK), :]
            state[pl.ds(row * SUB * SUB + s, SUB, stride=SUB), :] = from_owner(block)


def query_kernel(arrived, own_out, tail, vt, par, cot, grad_q, grad_short, x, state, long_out):
    unpack(arrived, x, state, 0)
    for s in range(SUB):
        coarse = x[pl.ds(s * SUB * ROWS_BACK + 6, SUB, stride=ROWS_BACK), :]
        fine = x[pl.ds(s * SUB * ROWS_BACK + 7, SUB, stride=ROWS_BACK), :]
        grad_short[:, s * LANES : (s + 1) * LANES] = from_owner(coarse + fine)[0:TAPS, :]
    decay = [decay_of(par, r) for r in range(POLES)]

    def forward(t, terms):
        long_out[tile(t), :] = own_out[tile(t), :] + add_up(terms)
        return tuple(q * d for q, d in zip(terms, decay))

    terms = tuple(coef_of(par, r) * state[tile(r), :] for r in range(POLES))
    gates = halo_gates(tail, par)
    for t in range(EDGE):
        if t < HALO:
            extra = gates[t] * vt[tile(t), :]
            terms = tuple(q + coef_of(par, r) * extra for r, q in enumerate(terms))
        terms = forward(t, terms)
    lax.fori_loop(EDGE, LEN, forward, terms, unroll=4)
    for s in range(SUB):
        rows = slice(s * LANES, (s + 1) * LANES)
        grad_q[rows, :] = (cot[rows, :].astype(F32) * long_out[across(s), :].T).astype(BF16)


def key_kernel(
    arrived, gate, local, vt, tail, head, par, query,
    grad_k, grad_v, grad_q, x, state, slope, vals, gone,
):
    leaving = pltpu.make_async_copy(query, grad_q, gone)
    leaving.start()
    unpack(arrived, x, state, 2)
    decay = [decay_of(par, r) for r in range(POLES)]
    back = [state[tile(r), :] for r in range(POLES)]
    growth = [1.0 / d for d in decay]
    ahead = []
    for n in range(HALO):
        ahead.append(
            add_up(coef_of(par, r) * back[r] for r in range(POLES)) * head[tile(EDGE + n), :]
        )
        if n < HALO - 1:
            z_now = head[tile(n), :]
            back = [(b - z_now) * g for b, g in zip(back, growth)]
    taps = [tap_of(par, j) for j in range(TAPS)]

    def backward(i, carry, extra=None):
        terms, ahead = carry
        t = LEN - 1 - i
        terms = tuple(q * d for q, d in zip(terms, decay))
        total = local[tile(t), :] + add_up(terms)
        now = gate[tile(t), :]
        vals[tile(t), :] = total * (now if extra is None else now + extra)
        slopes = (total * vt[tile(t), :], *ahead)
        slope[tile(t), :] = add_in_order(taps[j] * slopes[j] for j in range(TAPS))
        return terms, slopes[:HALO]

    terms = tuple(coef_of(par, r) * state[tile(r), :] for r in range(POLES))
    carry = (terms, tuple(ahead))
    carry = lax.fori_loop(0, LEN - EDGE, backward, carry, unroll=4)
    gates = halo_gates(tail, par)
    for t in reversed(range(EDGE)):
        carry = backward(LEN - 1 - t, carry, gates[t] if t < HALO else None)
    for s in range(SUB):
        rows = slice(s * LANES, (s + 1) * LANES)
        grad_k[rows, :] = slope[across(s), :].T.astype(BF16)
        grad_v[rows, :] = vals[across(s), :].T.astype(BF16)
    leaving.wait()


def pole_kernel(near, far, out, x):
    x[...] = near[...].astype(F32) + far[...].astype(F32)
    for s in range(SUB):
        for half in range(2):
            block = x[pl.ds(s * SUB * 2 + half, SUB, stride=2), :]
            out[half * SUB : (half + 1) * SUB, s * LANES : (s + 1) * LANES] = from_owner(block)


def call(
    kernel, name, outs, scratch, operands, flops=0, moved=0, space=pltpu.VMEM, vmem=VMEM, last=None
):
    spaces = [space] * (len(outs) - 1) + [last or space]
    return pl.pallas_call(
        kernel,
        out_shape=outs,
        in_specs=[pl.BlockSpec(memory_space=space)] * len(operands),
        out_specs=[pl.BlockSpec(memory_space=s) for s in spaces],
        scratch_shapes=scratch,
        compiler_params=pltpu.CompilerParams(vmem_limit_bytes=vmem),
        cost_estimate=pl.CostEstimate(flops=flops, bytes_accessed=moved, transcendentals=0),
        name=name,
    )(*operands)


def shape(rows, dtype=F32, lanes=LANES):
    return jax.ShapeDtypeStruct((rows, lanes), dtype)


def per_device(q_in, k_in, v_in, cotangent, taps_short, residues, rates):
    channels, length = q_in.shape
    count = lax.axis_size("seq")
    index = lax.axis_index("seq")
    chans = lax.axis_size("chan")
    assert (channels, length, count) == (SUB * LANES, LEN, SUB * SUB)
    scale = (length * count) ** (-0.5)
    full, edge, halo = SUB * LEN, SUB * EDGE, SUB * HALO

    operands = (k_in, v_in, q_in, cotangent, rates.T, residues.T, taps_short.T)
    outs = [shape(full)] * 4 + [shape(SUB * 40), shape(halo), shape(2 * edge)]
    outs.append(shape(count * ROWS_OUT, BF16))
    vt, gate, gated, local, par, tail, head, message = call(
        first_kernel,
        "first",
        outs,
        [
            *(pltpu.VMEM(a.shape, a.dtype) for a in (*operands, *outs)),
            pltpu.VMEM((full, LANES), F32),
            pltpu.VMEM((full, LANES), F32),
            pltpu.VMEM((TAPS, full, LANES), F32),
            pltpu.VMEM((SUB * SUB * ROWS_OUT, LANES), F32),
            pltpu.VMEM((count * ROWS_OUT, LANES), F32),
            pltpu.SemaphoreType.DMA((len(operands),)),
            pltpu.SemaphoreType.DMA((len(outs),)),
        ],
        operands,
        flops=48 * 10**6,
        moved=4 * 10**6,
        space=pltpu.HBM,
        vmem=VMEM_FIRST,
    )

    def exchange(x, rows):
        x = x.reshape(count, rows // 2, 2, LANES)
        return lax.all_to_all(x, "seq", split_axis=0, concat_axis=0, tiled=True)

    arrived = exchange(message, ROWS_OUT).reshape(count * ROWS_OUT, LANES)
    start = (index // SUB) * LANES + ((SUB - index % SUB) % SUB) * 16
    mine = [
        lax.dynamic_slice(a.T, (0, start), (POLES, 16)).reshape(2, LANES) for a in (rates, residues)
    ]
    own_taps = lax.dynamic_slice(taps_short.T, (0, start), (TAPS, 16))
    mine = jnp.concatenate([*mine, jnp.tile(own_taps, (1, LANES // 16))])
    tail = lax.ppermute(tail, "seq", [(i, i + 1) for i in range(count - 1)])
    head = lax.ppermute(head, "seq", [(i + 1, i) for i in range(count - 1)])
    (own_out,) = call(
        forward_kernel,
        "forward",
        [shape(full)],
        [],
        (gated, par),
        flops=10 * 10**6,
        moved=10**6,
    )
    arrived, own_out, tail, head, mine = lax.optimization_barrier(
        (arrived, own_out, tail, head, mine)
    )
    (back,) = call(
        functools.partial(owner_kernel, count, scale),
        "owner",
        [shape(count * ROWS_BACK, BF16)],
        [
            pltpu.VMEM(((count + 1) * ROWS_OUT, LANES), F32),
            pltpu.VMEM((count * ROWS_BACK, LANES), F32),
            pltpu.VMEM((3, count, SUB * LANES), F32),
            pltpu.VMEM((count * SUB, LANES), F32),
        ],
        (arrived, mine),
        flops=2 * 10**6,
        moved=10**6,
    )
    returned = exchange(back, ROWS_BACK)
    poles = returned[:, 2].reshape(2 * count, LANES)
    returned = returned.reshape(count * ROWS_BACK, LANES)

    def other(x, bit):
        return lax.ppermute(x, "chan", [(i, i ^ bit) for i in range(chans)])

    swap = [
        pltpu.VMEM((count * ROWS_BACK, LANES), F32),
        pltpu.VMEM((SUB * POLES, LANES), F32),
    ]
    near = other(poles, 1)
    query, grad_short = call(
        query_kernel,
        "query",
        [shape(channels, BF16), shape(TAPS, F32, channels)],
        [*swap, pltpu.VMEM((full, LANES), F32)],
        (returned, own_out, tail, vt, par, cotangent),
        flops=5 * 10**6,
        moved=10**6,
    )
    near, query = lax.optimization_barrier((near, query))
    near = (poles.astype(F32) + near.astype(F32)).astype(BF16)
    far = other(near, 3)
    grad_k, grad_v, grad_q = call(
        key_kernel,
        "key",
        [shape(channels, BF16)] * 3,
        [
            *swap,
            pltpu.VMEM((full, LANES), F32),
            pltpu.VMEM((full, LANES), F32),
            pltpu.SemaphoreType.DMA,
        ],
        (returned, gate, local, vt, tail, head, par, query),
        flops=8 * 10**6,
        moved=2 * 10**6,
        last=pltpu.HBM,
    )
    (grad_residues,) = call(
        pole_kernel,
        "poles",
        [shape(POLES, F32, channels)],
        [pltpu.VMEM((2 * count, LANES), F32)],
        (near, far),
        flops=10**5,
        moved=10**5,
    )
    return grad_q, grad_k, grad_v, grad_short.T, grad_residues.T


def solution(mesh):
    streams = P("chan", "seq")
    return jax.shard_map(
        per_device,
        mesh=mesh,
        in_specs=(streams,) * 4 + (P("chan", None), P(), P()),
        out_specs=(streams,) * 3 + (P("chan", None), P()),
        check_vma=False,
    )
```

time: 70.8 us -> 68.4 us (0.966)
  waiting for transfers between devices: 10.4 us -> 6.05 us
  Pallas kernels: 17.9 us -> 19.4 us
  blocking collectives: 16.4 us -> 17.2 us
    all_to_all x1, waiting for transfers between devices: 7.87 us -> 4.92 us  [exchange(): return lax.all_to_all(x, 'seq', split_axis=0, concat_axis=0, tiled=True)]
    all_to_all x1, starting transfers between devices: 11.3 us -> 13.1 us  [exchange(): return lax.all_to_all(x, 'seq', split_axis=0, concat_axis=0, tiled=True)]
    pallas_call x7 -> x6, Pallas kernels: 17.9 us -> 19.4 us  [call(): pl.pallas_call(kernel, out_shape=outs, in_specs=[pl.BlockSpec(memory_spac...]
    ppermute x1, waiting for transfers between devices: 2.48 us -> 1.12 us  [per_device(): head = lax.ppermute(head, 'seq', [(i + 1, i) for i in range(count - 1)])]
    transpose x2 -> x0, local copies, waits for them, and re-layouts: 1.26 us -> none  [per_device(): tail = k_in[:, length - HALO:].T.reshape(SUB * HALO, LANES)]
    ppermute x1, starting transfers between devices: 4.64 us -> 3.67 us  [per_device(): tail = lax.ppermute(tail, 'seq', [(i, i + 1) for i in range(count - 1)])]
    unnamed x14 -> x16, local copies, waits for them, and re-layouts: 0.95 us -> 0.04 us
    all_to_all x1, blocking collectives: 16.4 us -> 17.2 us  [exchange(): return lax.all_to_all(x, 'seq', split_axis=0, concat_axis=0, tiled=True)]
  transfers between devices with their start and end apart: 5 -> 5, of which waited for: 2 -> 2; matrix products, arithmetic and copies ran while one was open for 0% -> 3% of each run, Pallas kernels for 21% -> 8%
where the time goes in v3:
time: 68.4 us; the launch traced here: 68 us
  starting transfers between devices  22.7 us (33%)
  Pallas kernels  19.4 us (28%)
  blocking collectives  17.2 us (25%)
  waiting for transfers between devices  6.05 us (9%)
  local copies, waits for them, and re-layouts  1.86 us (3%)
  between operations  0.84 us (1%)
    pallas_call x6, Pallas kernels, call(): pl.pallas_call(kernel, out_shape=outs, in_specs=[pl.BlockSpec(memory_spac...  19.4 us
    all_to_all x1, blocking collectives, exchange(): return lax.all_to_all(x, 'seq', split_axis=0, concat_axis=0, tiled=True)  17.2 us
    all_to_all x1, starting transfers between devices, exchange(): return lax.all_to_all(x, 'seq', split_axis=0, concat_axis=0, tiled=True)  13.1 us
    all_to_all x1, waiting for transfers between devices, exchange(): return lax.all_to_all(x, 'seq', split_axis=0, concat_axis=0, tiled=True)  4.92 us
    ppermute x2, starting transfers between devices, other(): return lax.ppermute(x, 'chan', [(i, i ^ bit) for i in range(chans)])  3.97 us
    ppermute x1, starting transfers between devices, per_device(): tail = lax.ppermute(tail, 'seq', [(i, i + 1) for i in range(count - 1)])  3.67 us
    ppermute x1, starting transfers between devices, per_device(): head = lax.ppermute(head, 'seq', [(i + 1, i) for i in range(count - 1)])  1.92 us
  transfers between devices with their start and end apart: 5, of which 2 were waited for; matrix products, arithmetic and copies ran while one was open for 3% of the time, Pallas kernels for 8%

profile of v3, /device:TPU:1, one launch (start us, length us, event | category | flops | bytes accessed | tf_op | source)
XLA Modules:
  0.0 68.0 jit_solution(3561632940962235197)
XLA Ops:
  0.6 11.7 %first.1 = (f32[1024,128]{1,0:T(8,128)}, f32[1024,128]{1,0:T(8,128)}, f32[1024,128]{1,0:T(8,128)}, f32[1024,128]{1,0:T(8,128)}, f32[320,128]{1,0:T(8,128)}, /*in...) custom-call(bf16[1024,128]{1,0:T(8,128)(2,1)} %refs_0_.1, bf16[1024,128]{1,0:T(8,128)(2,1)} %refs_1_.1, ...), custom_call_target="tpu_custom_call" | custom-call | flops 48000000 | bytes 4000000 | tf_op jit(solution)/shard_map/first/pallas_call | solution.py:460
  12.3 0.0 copy-start.3
  12.3 0.0 copy-start.7
  12.4 0.0 copy-start.6
  12.4 13.1 %all-to-all-start = ((bf16[64,12,2,128]{3,2,1,0:T(2,128)(2,1)}), bf16[64,12,2,128]{3,2,1,0:T(2,128)(2,1)S(1)}, u32[]{:S(2)}, u32[]{:S(2)}) async-start(bf16[64,12,2,128]{3,2,1,0:T(2,128)(2,1)} %bitcast.20), calls=%async_computation | async-start | bytes 786432 | tf_op jit(solution)/shard_map/all_to_all | solution.py:511
  25.5 0.0 copy-start.1
  25.5 0.0 copy-done.7
  25.5 3.7 %collective-permute-start = (f32[48,128]{1,0:T(8,128)S(1)}, f32[48,128]{1,0:T(8,128)S(1)}, u32[]{:S(2)}, u32[]{:S(2)}) collective-permute-start(f32[48,128]{1,0:T(8,128)S(1)} %copy-done.7), channel_id=1, source_target_pairs={{0,4},{4,8},{8,12},{12,16},{16,20},{20,24},{24,28},{28,32},{32,36}... | collective-permute-start | bytes 73736 | tf_op jit(solution)/shard_map/ppermute | solution.py:520
  29.2 0.0 copy-done.6
  29.2 1.9 %collective-permute-start.1 = (f32[128,128]{1,0:T(8,128)S(1)}, f32[128,128]{1,0:T(8,128)S(1)}, u32[]{:S(2)}, u32[]{:S(2)}) collective-permute-start(f32[128,128]{1,0:T(8,128)S(1)} %copy-done.6), channel_id=1, source_target_pairs={{4,0},{8,4},{12,8},{16,12},{20,16},{24,20},{28,24},{32,28},{36,32}... | collective-permute-start | bytes 196616 | tf_op jit(solution)/shard_map/ppermute | solution.py:521
  31.2 0.8 %dynamic-slice_bitcast_fusion.2 = f32[7,16]{1,0:T(8,128)S(1)} fusion(f32[1024,7]{0,1:T(8,128)} %param.11, s32[]{:T(128)S(6)} %select_n.23), kind=kLoop, calls=%fused_computation.4 | loop fusion | bytes 900 | tf_op jit(solution)/shard_map/dynamic_slice | solution.py:518
  32.0 0.1 tile.10
  32.0 0.8 %dynamic-slice_bitcast_fusion = (f32[16,16]{1,0:T(8,128)S(1)}, f32[16,16]{1,0:T(8,128)S(1)}) fusion(f32[1024,16]{0,1:T(8,128)} %param.12, s32[]{:T(128)S(6)} %select_n.23, f32[1024,16]{0,1:T(8,128)} %param.13), kind=kLoop, calls=%fused_computation.2 | loop fusion | bytes 4100 | tf_op jit(solution)/shard_map/dynamic_slice | solution.py:516
  32.8 0.1 reshape.35
  32.9 0.1 reshape.34
  33.0 0.0 copy-done.3
  33.0 0.0 copy-done.1
  33.0 1.5 %forward.1.own_out = f32[1024,128]{1,0:T(8,128)S(1)} custom-call(f32[1024,128]{1,0:T(8,128)S(1)} %copy-done.3, f32[320,128]{1,0:T(8,128)S(1)} %copy-done.1), custom_call_target="tpu_custom_call" | custom-call | flops 10000000 | bytes 1000000 | tf_op jit(solution)/shard_map/forward/pallas_call | solution.py:460
  34.5 0.0 copy-start
  34.5 0.0 collective-permute-done.tail
  34.5 1.1 %collective-permute-done.1.head = f32[128,128]{1,0:T(8,128)S(1)} collective-permute-done((f32[128,128]{1,0:T(8,128)S(1)}, f32[128,128]{1,0:T(8,128)S(1)}, u32[]{:S(2)}, u32[]{:S(2)}) %collective-permute-start.1) | collective-permute-done | bytes 65568 | tf_op jit(solution)/shard_map/ppermute | solution.py:521
  35.7 4.9 %all-to-all-done = bf16[64,12,2,128]{3,2,1,0:T(2,128)(2,1)S(1)} async-done(((bf16[64,12,2,128]{3,2,1,0:T(2,128)(2,1)}), bf16[64,12,2,128]{3,2,1,0:T(2,128)(2,1)S(1)}, u32[]{:S(2)}, u32[]{:S(2)}) %all-to-all-start) | async-done | bytes 393248 | tf_op jit(solution)/shard_map/all_to_all | solution.py:511
  40.6 0.8 %owner.1 = bf16[512,128]{1,0:T(8,128)(2,1)S(1)} custom-call(bf16[1536,128]{1,0:T(8,128)(2,1)S(1)} %bitcast.16, f32[11,128]{1,0:T(8,128)S(1)} %pad_maximum_fusion.mine), custom_call_target="tpu_custom_call" | custom-call | flops 2000000 | bytes 1000000 | tf_op jit(solution)/shard_map/owner/pallas_call | solution.py:460
  41.4 0.0 copy-start.2
  41.4 17.2 %all_to_all.10 = bf16[64,4,2,128]{3,2,1,0:T(2,128)(2,1)S(1)} all-to-all(bf16[64,4,2,128]{3,2,1,0:T(2,128)(2,1)S(1)} %bitcast.19), channel_id=1, replica_groups=mesh['seq'=64,'chan'=4] {'seq'}, dimensions={0} | all-to-all | bytes 262144 | tf_op jit(solution)/shard_map/all_to_all | solution.py:511
  58.7 1.4 %collective-permute-start.2 = (bf16[128,128]{1,0:T(8,128)(2,1)S(1)}, bf16[128,128]{1,0:T(8,128)(2,1)S(1)}, u32[]{:S(2)}, u32[]{:S(2)}) collective-permute-start(bf16[128,128]{1,0:T(8,128)(2,1)S(1)} %bitcast.21), channel_id=1, source_target_pairs={{0,1},{1,0},{2,3},{3,2},{4,5},{5,4},{6,7},{7,6},{8,9},{9,8},{10,11... | collective-permute-start | bytes 98312 | tf_op jit(solution)/shard_map/ppermute | solution.py:553
  60.0 0.0 copy-done
  60.0 0.0 copy-done.2
  60.0 0.0 copy-start.4
  60.0 0.0 copy-start.5
  60.0 1.7 %query.1 = (bf16[1024,128]{1,0:T(8,128)(2,1)S(1)}, f32[7,1024]{1,0:T(8,128)}) custom-call(bf16[512,128]{1,0:T(8,128)(2,1)S(1)} %bitcast.17, f32[1024,128]{1,0:T(8,128)S(1)} %forward.1.own_out, f32[48,128]{1,0:T(8,128)S(1)} %collective-permute-done.tail, f32[1024,128]{1,0:T(8,128)S(1)} %copy-done, f32[320,128]{1,0:T(8,128)S(1)} %copy-done.1, ...), custom_call_target="tpu_custom_call" | custom-call | flops 5000000 | bytes 1000000 | tf_op jit(solution)/shard_map/query/pallas_call | solution.py:460
  61.7 0.0 collective-permute-done.2
  61.8 2.6 %collective-permute-start.3 = (bf16[128,128]{1,0:T(8,128)(2,1)S(1)}, bf16[128,128]{1,0:T(8,128)(2,1)S(1)}, u32[]{:S(2)}, u32[]{:S(2)}) collective-permute-start(bf16[128,128]{1,0:T(8,128)(2,1)S(1)} %add_convert_fusion.near), channel_id=1, source_target_pairs={{0,3},{1,2},{2,1},{3,0},{4,7},{5,6},{6,5},{7,4},{8,11},{9,10},{10,... | collective-permute-start | bytes 98312 | tf_op jit(solution)/shard_map/ppermute | solution.py:553
  64.3 0.0 copy-done.4
  64.3 0.0 copy-done.5
  64.3 2.6 %key.1 = (bf16[1024,128]{1,0:T(8,128)(2,1)}, bf16[1024,128]{1,0:T(8,128)(2,1)}, bf16[1024,128]{1,0:T(8,128)(2,1)}) custom-call(bf16[512,128]{1,0:T(8,128)(2,1)S(1)} %bitcast.18, f32[1024,128]{1,0:T(8,128)S(1)} %copy-done.4, f32[1024,128]{1,0:T(8,128)S(1)} %copy-done.5, f32[1024,128]{1,0:T(8,128)S(1)} %copy-done, f32[48,128]{1,0:T(8,128)S(1)} %collective-permute-done.tail, ...), custom_call_target="tpu_custom_call" | custom-call | flops 8000000 | bytes 2000000 | tf_op jit(solution)/shard_map/key/pallas_call | solution.py:460
  66.9 0.0 collective-permute-done.3.far
  67.0 1.1 %poles.1 = f32[16,1024]{1,0:T(8,128)} custom-call(bf16[128,128]{1,0:T(8,128)(2,1)S(1)} %add_convert_fusion.near, bf16[128,128]{1,0:T(8,128)(2,1)S(1)} %collective-permute-done.3.far), custom_call_target="tpu_custom_call" | custom-call | flops 100000 | bytes 100000 | tf_op jit(solution)/shard_map/poles/pallas_call | solution.py:460
  (4 shorter events, 0.1 us)
Async XLA Ops:
  12.3 20.7 %copy-start.3 = (f32[1024,128]{1,0:T(8,128)S(1)}, f32[1024,128]{1,0:T(8,128)}, u32[]{:S(2)}) copy-start(f32[1024,128]{1,0:T(8,128)} %get-tuple-element.26.gated) | copy-start | bytes 1572868
  12.3 13.2 %copy-start.7 = (f32[48,128]{1,0:T(8,128)S(1)}, f32[48,128]{1,0:T(8,128)}, u32[]{:S(2)}) copy-start(f32[48,128]{1,0:T(8,128)} %get-tuple-element.28) | copy-start | bytes 73732
  12.4 16.9 %copy-start.6 = (f32[128,128]{1,0:T(8,128)S(1)}, f32[128,128]{1,0:T(8,128)}, u32[]{:S(2)}) copy-start(f32[128,128]{1,0:T(8,128)} %get-tuple-element.29) | copy-start | bytes 196612
  12.4 28.2 %all-to-all-start = ((bf16[64,12,2,128]{3,2,1,0:T(2,128)(2,1)}), bf16[64,12,2,128]{3,2,1,0:T(2,128)(2,1)S(1)}, u32[]{:S(2)}, u32[]{:S(2)}) async-start(bf16[64,12,2,128]{3,2,1,0:T(2,128)(2,1)} %bitcast.20), calls=%async_computation | async-start | bytes 786432 | tf_op jit(solution)/shard_map/all_to_all | solution.py:511
  25.5 7.5 %copy-start.1 = (f32[320,128]{1,0:T(8,128)S(1)}, f32[320,128]{1,0:T(8,128)}, u32[]{:S(2)}) copy-start(f32[320,128]{1,0:T(8,128)} %get-tuple-element.27.par) | copy-start | bytes 491524
  25.5 9.0 %collective-permute-start = (f32[48,128]{1,0:T(8,128)S(1)}, f32[48,128]{1,0:T(8,128)S(1)}, u32[]{:S(2)}, u32[]{:S(2)}) collective-permute-start(f32[48,128]{1,0:T(8,128)S(1)} %copy-done.7), channel_id=1, source_target_pairs={{0,4},{4,8},{8,12},{12,16},{16,20},{20,24},{24,28},{28,32},{32,36}... | collective-permute-start | bytes 73736 | tf_op jit(solution)/shard_map/ppermute | solution.py:520
  29.2 6.5 %collective-permute-start.1 = (f32[128,128]{1,0:T(8,128)S(1)}, f32[128,128]{1,0:T(8,128)S(1)}, u32[]{:S(2)}, u32[]{:S(2)}) collective-permute-start(f32[128,128]{1,0:T(8,128)S(1)} %copy-done.6), channel_id=1, source_target_pairs={{4,0},{8,4},{12,8},{16,12},{20,16},{24,20},{28,24},{32,28},{36,32}... | collective-permute-start | bytes 196616 | tf_op jit(solution)/shard_map/ppermute | solution.py:521
  34.5 25.5 %copy-start = (f32[1024,128]{1,0:T(8,128)S(1)}, f32[1024,128]{1,0:T(8,128)}, u32[]{:S(2)}) copy-start(f32[1024,128]{1,0:T(8,128)} %get-tuple-element.34.vt) | copy-start | bytes 1572868
  41.4 18.6 %copy-start.2 = (bf16[1024,128]{1,0:T(8,128)(2,1)S(1)}, bf16[1024,128]{1,0:T(8,128)(2,1)}, u32[]{:S(2)}) copy-start(bf16[1024,128]{1,0:T(8,128)(2,1)} %cot.1) | copy-start | bytes 786436
  58.7 3.1 %collective-permute-start.2 = (bf16[128,128]{1,0:T(8,128)(2,1)S(1)}, bf16[128,128]{1,0:T(8,128)(2,1)S(1)}, u32[]{:S(2)}, u32[]{:S(2)}) collective-permute-start(bf16[128,128]{1,0:T(8,128)(2,1)S(1)} %bitcast.21), channel_id=1, source_target_pairs={{0,1},{1,0},{2,3},{3,2},{4,5},{5,4},{6,7},{7,6},{8,9},{9,8},{10,11... | collective-permute-start | bytes 98312 | tf_op jit(solution)/shard_map/ppermute | solution.py:553
  60.0 4.3 %copy-start.4 = (f32[1024,128]{1,0:T(8,128)S(1)}, f32[1024,128]{1,0:T(8,128)}, u32[]{:S(2)}) copy-start(f32[1024,128]{1,0:T(8,128)} %get-tuple-element.32.gate) | copy-start | bytes 1572868
  60.0 4.3 %copy-start.5 = (f32[1024,128]{1,0:T(8,128)S(1)}, f32[1024,128]{1,0:T(8,128)}, u32[]{:S(2)}) copy-start(f32[1024,128]{1,0:T(8,128)} %get-tuple-element.33.local) | copy-start | bytes 1572868
  61.8 5.2 %collective-permute-start.3 = (bf16[128,128]{1,0:T(8,128)(2,1)S(1)}, bf16[128,128]{1,0:T(8,128)(2,1)S(1)}, u32[]{:S(2)}, u32[]{:S(2)}) collective-permute-start(bf16[128,128]{1,0:T(8,128)(2,1)S(1)} %add_convert_fusion.near), channel_id=1, source_target_pairs={{0,3},{1,2},{2,1},{3,0},{4,7},{5,6},{6,5},{7,4},{8,11},{9,10},{10,... | collective-permute-start | bytes 98312 | tf_op jit(solution)/shard_map/ppermute | solution.py:553

commit v4 on v3

--- a/solution.py
+++ b/solution.py
@@ -16,8 +16,9 @@
 TAPS = 7
 HALO = TAPS - 1
 EDGE = 8
-MODE = 4 + TAPS
 ROWS_OUT = 24
+FIR_TERMS = tuple((n, q) for n in range(9) for q in range(2) if (n, q) != (8, 1))
+BACK_MODES, BACK_UNROLL, AHEAD_MODES, AHEAD_UNROLL = 8, 16, 2, 16
 ROW_SHORT, ROW_V, ROW_MOMENT, ROW_K, ROW_Z = 6, 7, 8, 22, 23
 ROWS_BACK = 8
 VMEM = 48 * 1024 * 1024
@@ -84,59 +85,131 @@
     return par[tile(2 * POLES + j), :]
 
 
-def scan_down(par, z, gated, w, local, gather):
+def add_up(terms):
+    terms = list(terms)
+    while len(terms) > 1:
+        terms = [a + b for a, b in zip(terms[0::2], terms[1::2])]
+    return terms[0]
+
+
+def key_sums(now, before):
+    even = (now[0], now[1] - now[0], before[0] - now[0])
+    odd = (now[2], now[3] - now[2], now[1] - now[2])
+    earlier = (before[1], before[0] - before[1], before[2] - before[1])
+    return [x for e, o, p in zip(even, odd, earlier) for x in (e, o - e, p - e)]
+
+
+def correlate(sums, u, keys):
+    lines = (
+        (u[0] + u[1], u[2] + u[3]),
+        (u[1], u[3]),
+        (u[0], u[2]),
+    )
+    factors = []
+    for even, odd in lines:
+        factors += [even + odd, odd, even]
+    return [
+        total + factors[line] * keys[q][line]
+        for total, (line, q) in zip(sums, FIR_TERMS)
+    ]
+
+
+def moments(sums):
+    part = dict(zip(FIR_TERMS, sums))
+    lines = []
+    for n in range(3):
+        line = []
+        for q in range(2):
+            line.append(part[3 * n, q] + part[3 * n + 1, q])
+            if (3 * n + 2, q) in part:
+                line.append(part[3 * n + 2, q] + part[3 * n, q])
+        lines.append(line)
+    both, odd, even = lines
+    out = []
+    for j in range(TAPS):
+        n = j // 2
+        out.append(both[n] + (even[n] if j % 2 else odd[n]))
+    return out
+
+
+def scan_down(par, z, v, gate, gated, keys, local, gather):
     zero = jnp.zeros((SUB, LANES), F32)
-    for pair in range(POLES // 2):
-        modes = (2 * pair, 2 * pair + 1)
+    terms = len(FIR_TERMS)
+
+    def keys_of(m):
+        return tuple(keys[n, tile(m + 1), :] for n in range(9))
+
+    for first in range(0, POLES, BACK_MODES):
+        modes = range(first, first + BACK_MODES)
         decay = [decay_of(par, r) for r in modes]
         coef = [coef_of(par, r) for r in modes]
-        final = pair == POLES // 2 - 1
-        state = tuple(
-            tuple(decay[n] if m == 3 else zero for m in range(MODE)) for n in range(2)
+
+        def back_step(i, state, first=first, decay=decay, coef=coef):
+            at = tile(LEN - 1 - i)
+            z_now, g_now = z[at, :], gated[at, :]
+            after, parts = [], []
+            for (back, pole), d, c in zip(state, decay, coef):
+                back = back * d + z_now
+                after.append((back, pole + g_now * back))
+                parts.append(c * back)
+            total = add_up(parts)
+            local[at, :] = total if first == 0 else local[at, :] + total
+            return tuple(after)
+
+        state = lax.fori_loop(
+            0, LEN, back_step, ((zero, zero),) * BACK_MODES, unroll=BACK_UNROLL
         )
-        sums = (zero,) * TAPS if final else ()
-
-        def step(i, carry, pair=pair, decay=decay, coef=coef, final=final):
-            state, sums = carry
-            t = LEN - 1 - i
-            z_now = z[tile(t), :]
-            g_now = gated[tile(t), :]
-            w_now = [w[j, tile(t), :] for j in range(TAPS)]
-            total = None if pair == 0 else local[tile(t), :]
-            after = []
-            for n in range(2):
-                back, pole, ahead, power, *moments = state[n]
-                back = back * decay[n] + z_now
-                pole = pole + g_now * back
-                ahead = ahead + power * g_now
-                moments = [m + power * x for m, x in zip(moments, w_now)]
-                power = power * decay[n]
-                term = coef[n] * back
-                total = term if total is None else total + term
-                after.append((back, pole, ahead, power, *moments))
-            local[tile(t), :] = total
-            if final:
-                sums = tuple(a + total * x for a, x in zip(sums, w_now))
-            return tuple(after), sums
-
-        state, sums = lax.fori_loop(0, LEN, step, (state, sums), unroll=4)
-        for n, r in enumerate(modes):
+        for (back, pole), r in zip(state, modes):
             half, slot = divmod(r, SUB)
-            back, pole, ahead, _, *moments = state[n]
-            gather[tile(half * SUB + slot), :] = ahead
             gather[tile((2 + half) * SUB + slot), :] = back
             gather[tile((4 + half) * SUB + slot), :] = pole
-            for j, value in enumerate(moments):
+
+    for first in range(0, POLES, AHEAD_MODES):
+        modes = range(first, first + AHEAD_MODES)
+        decay = [decay_of(par, r) for r in modes]
+
+        def ahead_step(i, carry, decay=decay):
+            state, now = carry
+            m = LEN // 4 - 1 - i
+            at = [tile(4 * m + n) for n in range(4)]
+            before = keys_of(m - 1)
+            keyed = (now, before)
+            after = []
+            for (ahead, power, sums), d in zip(state, decay):
+                u = [None] * 4
+                for p in reversed(range(4)):
+                    u[p] = power * v[at[p], :]
+                    ahead = ahead + u[p] * gate[at[p], :]
+                    power = power * d
+                after.append((ahead, power, tuple(correlate(sums, u, keyed))))
+            return tuple(after), before
+
+        state = tuple((zero, d, (zero,) * terms) for d in decay)
+        carry = (state, keys_of(LEN // 4 - 1))
+        state, _ = lax.fori_loop(0, LEN // 4, ahead_step, carry, unroll=AHEAD_UNROLL)
+        for (ahead, _, sums), r in zip(state, modes):
+            half, slot = divmod(r, SUB)
+            gather[tile(half * SUB + slot), :] = ahead
+            for j, value in enumerate(moments(sums)):
                 gather[tile((ROW_MOMENT + 2 * j + half) * SUB + slot), :] = value
-        for j, value in enumerate(sums):
-            gather[tile(ROW_SHORT * SUB + j), :] = value
+
+    def step(m, carry):
+        sums, before = carry
+        at = [tile(4 * m + n) for n in range(4)]
+        now = keys_of(m)
+        u = [local[p, :] * v[p, :] for p in at]
+        return tuple(correlate(sums, u, (now, before))), now
+
+    sums, _ = lax.fori_loop(0, LEN // 4, step, ((zero,) * terms, keys_of(-1)), unroll=8)
+    for j, value in enumerate(moments(sums)):
+        gather[tile(ROW_SHORT * SUB + j), :] = value
 
 
 def first_kernel(*refs):
     sources, targets, refs = refs[:7], refs[7:15], refs[15:]
     (k, v, q, cot, rates, residues, amounts), refs = refs[:7], refs[7:]
     (vt, gate, gated, local, par, tail, head, message), refs = refs[:8], refs[8:]
-    kt, zt, w, gather, spread, came, went = refs
+    kt, zt, keys, gather, spread, came, went = refs
     copies = [
         pltpu.make_async_copy(a, b, came.at[n])
         for n, (a, b) in enumerate(zip(sources, (k, v, q, cot, rates, residues, amounts)))
@@ -181,24 +254,26 @@
 
     taps = [tap_of(par, j) for j in range(TAPS)]
 
-    def prepare(t, before):
-        keys = (kt[tile(t), :], *before)
-        now = taps[0] * keys[0]
-        for j in range(1, TAPS):
-            now = now + taps[j] * keys[j]
-        value = vt[tile(t), :]
-        gate[tile(t), :] = now
-        gated[tile(t), :] = now * value
-        for j in range(TAPS):
-            w[j, tile(t), :] = value * keys[j]
-        return keys[:HALO]
+    def prepare(m, before):
+        at = [tile(4 * m + n) for n in range(4)]
+        now = [kt[p, :] for p in at]
+        line = [*reversed(now), *before]
+        for n in range(4):
+            total = add_in_order(taps[j] * line[3 - n + j] for j in range(TAPS))
+            gate[at[n], :] = total
+            gated[at[n], :] = total * vt[at[n], :]
+        for n, value in enumerate(key_sums(now, before)):
+            keys[n, tile(m + 1), :] = value
+        return tuple(line[:HALO])
 
     gather[tile(ROW_SHORT * SUB + TAPS), :] = jnp.zeros((SUB, LANES), F32)
     zero = gather[tile(ROW_SHORT * SUB + TAPS), :]
-    lax.fori_loop(0, LEN, prepare, (zero,) * HALO, unroll=4)
+    for n in range(9):
+        keys[n, tile(0), :] = zero
+    lax.fori_loop(0, LEN // 4, prepare, (zero,) * HALO, unroll=2)
     leaving[1].start()
     leaving[2].start()
-    scan_down(par, zt, gated, w, local, gather)
+    scan_down(par, zt, vt, gate, gated, keys, local, gather)
     leaving[3].start()
     for row in range(ROWS_OUT):
         for s in range(SUB):
@@ -351,7 +426,7 @@
             own_out[tile(i), :] = total
             return tuple(after)
 
-        lax.fori_loop(0, LEN, forward, ahead, unroll=4)
+        lax.fori_loop(0, LEN, forward, ahead, unroll=16)
 
 
 def halo_gates(tail, par):
@@ -359,13 +434,6 @@
         add_in_order(tap_of(par, j) * tail[tile(HALO + t - j), :] for j in range(t + 1, TAPS))
         for t in range(HALO)
     ]
-
-
-def add_up(terms):
-    terms = list(terms)
-    while len(terms) > 1:
-        terms = [a + b for a, b in zip(terms[0::2], terms[1::2])]
-    return terms[0]
 
 
 def unpack(arrived, x, state, first):
@@ -395,7 +463,7 @@
             extra = gates[t] * vt[tile(t), :]
             terms = tuple(q + coef_of(par, r) * extra for r, q in enumerate(terms))
         terms = forward(t, terms)
-    lax.fori_loop(EDGE, LEN, forward, terms, unroll=4)
+    lax.fori_loop(EDGE, LEN, forward, terms, unroll=24)
     for s in range(SUB):
         rows = slice(s * LANES, (s + 1) * LANES)
         grad_q[rows, :] = (cot[rows, :].astype(F32) * long_out[across(s), :].T).astype(BF16)
@@ -434,7 +502,7 @@
 
     terms = tuple(coef_of(par, r) * state[tile(r), :] for r in range(POLES))
     carry = (terms, tuple(ahead))
-    carry = lax.fori_loop(0, LEN - EDGE, backward, carry, unroll=4)
+    carry = lax.fori_loop(0, LEN - EDGE, backward, carry, unroll=24)
     gates = halo_gates(tail, par)
     for t in reversed(range(EDGE)):
         carry = backward(LEN - 1 - t, carry, gates[t] if t < HALO else None)
@@ -493,7 +561,7 @@
             *(pltpu.VMEM(a.shape, a.dtype) for a in (*operands, *outs)),
             pltpu.VMEM((full, LANES), F32),
             pltpu.VMEM((full, LANES), F32),
-            pltpu.VMEM((TAPS, full, LANES), F32),
+            pltpu.VMEM((9, full // 4 + SUB, LANES), F32),
             pltpu.VMEM((SUB * SUB * ROWS_OUT, LANES), F32),
             pltpu.VMEM((count * ROWS_OUT, LANES), F32),
             pltpu.SemaphoreType.DMA((len(operands),)),

time: 68.4 us -> 66.4 us (0.971)
  Pallas kernels: 19.4 us -> 16.9 us
    pallas_call x6, Pallas kernels: 19.4 us -> 16.9 us  [call(): pl.pallas_call(kernel, out_shape=outs, in_specs=[pl.BlockSpec(memory_spac...]
where the time goes in v4:
time: 66.4 us; the launch traced here: 66.1 us
  starting transfers between devices  22.8 us (34%)
  blocking collectives  17.2 us (26%)
  Pallas kernels  16.9 us (25%)
  waiting for transfers between devices  6.38 us (10%)
  local copies, waits for them, and re-layouts  1.86 us (3%)
  between operations  0.84 us (1%)
    all_to_all x1, blocking collectives, exchange(): return lax.all_to_all(x, 'seq', split_axis=0, concat_axis=0, tiled=True)  17.2 us
    pallas_call x6, Pallas kernels, call(): pl.pallas_call(kernel, out_shape=outs, in_specs=[pl.BlockSpec(memory_spac...  16.9 us
    all_to_all x1, starting transfers between devices, exchange(): return lax.all_to_all(x, 'seq', split_axis=0, concat_axis=0, tiled=True)  13.1 us
    all_to_all x1, waiting for transfers between devices, exchange(): return lax.all_to_all(x, 'seq', split_axis=0, concat_axis=0, tiled=True)  4.92 us
    ppermute x2, starting transfers between devices, other(): return lax.ppermute(x, 'chan', [(i, i ^ bit) for i in range(chans)])  4.12 us
    ppermute x1, starting transfers between devices, per_device(): tail = lax.ppermute(tail, 'seq', [(i, i + 1) for i in range(count - 1)])  3.67 us
    ppermute x1, starting transfers between devices, per_device(): head = lax.ppermute(head, 'seq', [(i + 1, i) for i in range(count - 1)])  1.92 us
    ppermute x1, waiting for transfers between devices, per_device(): head = lax.ppermute(head, 'seq', [(i + 1, i) for i in range(count - 1)])  1.45 us
  transfers between devices with their start and end apart: 5, of which 2 were waited for; matrix products, arithmetic and copies ran while one was open for 3% of the time, Pallas kernels for 8%

profile of v4, /device:TPU:1, one launch (start us, length us, event | category | flops | bytes accessed | tf_op | source)
XLA Modules:
  0.0 66.1 jit_solution(9359797587843982190)
XLA Ops:
  0.6 9.9 %first.1 = (f32[1024,128]{1,0:T(8,128)}, f32[1024,128]{1,0:T(8,128)}, f32[1024,128]{1,0:T(8,128)}, f32[1024,128]{1,0:T(8,128)}, f32[320,128]{1,0:T(8,128)}, /*in...) custom-call(bf16[1024,128]{1,0:T(8,128)(2,1)} %refs_0_.1, bf16[1024,128]{1,0:T(8,128)(2,1)} %refs_1_.1, ...), custom_call_target="tpu_custom_call" | custom-call | flops 48000000 | bytes 4000000 | tf_op jit(solution)/shard_map/first/pallas_call | solution.py:528
  10.5 0.0 copy-start.3
  10.6 0.0 copy-start.7
  10.6 0.0 copy-start.6
  10.6 13.1 %all-to-all-start = ((bf16[64,12,2,128]{3,2,1,0:T(2,128)(2,1)}), bf16[64,12,2,128]{3,2,1,0:T(2,128)(2,1)S(1)}, u32[]{:S(2)}, u32[]{:S(2)}) async-start(bf16[64,12,2,128]{3,2,1,0:T(2,128)(2,1)} %bitcast.20), calls=%async_computation | async-start | bytes 786432 | tf_op jit(solution)/shard_map/all_to_all | solution.py:579
  23.7 0.0 copy-start.1
  23.7 0.0 copy-done.7
  23.7 3.7 %collective-permute-start = (f32[48,128]{1,0:T(8,128)S(1)}, f32[48,128]{1,0:T(8,128)S(1)}, u32[]{:S(2)}, u32[]{:S(2)}) collective-permute-start(f32[48,128]{1,0:T(8,128)S(1)} %copy-done.7), channel_id=1, source_target_pairs={{0,4},{4,8},{8,12},{12,16},{16,20},{20,24},{24,28},{28,32},{32,36}... | collective-permute-start | bytes 73736 | tf_op jit(solution)/shard_map/ppermute | solution.py:588
  27.4 0.0 copy-done.6
  27.4 1.9 %collective-permute-start.1 = (f32[128,128]{1,0:T(8,128)S(1)}, f32[128,128]{1,0:T(8,128)S(1)}, u32[]{:S(2)}, u32[]{:S(2)}) collective-permute-start(f32[128,128]{1,0:T(8,128)S(1)} %copy-done.6), channel_id=1, source_target_pairs={{4,0},{8,4},{12,8},{16,12},{20,16},{24,20},{28,24},{32,28},{36,32}... | collective-permute-start | bytes 196616 | tf_op jit(solution)/shard_map/ppermute | solution.py:589
  29.4 0.8 %dynamic-slice_bitcast_fusion.2 = f32[7,16]{1,0:T(8,128)S(1)} fusion(f32[1024,7]{0,1:T(8,128)} %param.11, s32[]{:T(128)S(6)} %select_n.23), kind=kLoop, calls=%fused_computation.4 | loop fusion | bytes 900 | tf_op jit(solution)/shard_map/dynamic_slice | solution.py:586
  30.2 0.1 tile.10
  30.2 0.8 %dynamic-slice_bitcast_fusion = (f32[16,16]{1,0:T(8,128)S(1)}, f32[16,16]{1,0:T(8,128)S(1)}) fusion(f32[1024,16]{0,1:T(8,128)} %param.12, s32[]{:T(128)S(6)} %select_n.23, f32[1024,16]{0,1:T(8,128)} %param.13), kind=kLoop, calls=%fused_computation.2 | loop fusion | bytes 4100 | tf_op jit(solution)/shard_map/dynamic_slice | solution.py:584
  31.0 0.1 reshape.35
  31.1 0.1 reshape.34
  31.2 0.0 copy-done.3
  31.2 0.0 copy-done.1
  31.2 1.2 %forward.1.own_out = f32[1024,128]{1,0:T(8,128)S(1)} custom-call(f32[1024,128]{1,0:T(8,128)S(1)} %copy-done.3, f32[320,128]{1,0:T(8,128)S(1)} %copy-done.1), custom_call_target="tpu_custom_call" | custom-call | flops 10000000 | bytes 1000000 | tf_op jit(solution)/shard_map/forward/pallas_call | solution.py:528
  32.4 0.0 copy-start
  32.4 0.0 collective-permute-done.tail
  32.4 1.4 %collective-permute-done.1.head = f32[128,128]{1,0:T(8,128)S(1)} collective-permute-done((f32[128,128]{1,0:T(8,128)S(1)}, f32[128,128]{1,0:T(8,128)S(1)}, u32[]{:S(2)}, u32[]{:S(2)}) %collective-permute-start.1) | collective-permute-done | bytes 65568 | tf_op jit(solution)/shard_map/ppermute | solution.py:589
  33.9 4.9 %all-to-all-done = bf16[64,12,2,128]{3,2,1,0:T(2,128)(2,1)S(1)} async-done(((bf16[64,12,2,128]{3,2,1,0:T(2,128)(2,1)}), bf16[64,12,2,128]{3,2,1,0:T(2,128)(2,1)S(1)}, u32[]{:S(2)}, u32[]{:S(2)}) %all-to-all-start) | async-done | bytes 393248 | tf_op jit(solution)/shard_map/all_to_all | solution.py:579
  38.8 0.8 %owner.1 = bf16[512,128]{1,0:T(8,128)(2,1)S(1)} custom-call(bf16[1536,128]{1,0:T(8,128)(2,1)S(1)} %bitcast.16, f32[11,128]{1,0:T(8,128)S(1)} %pad_maximum_fusion.mine), custom_call_target="tpu_custom_call" | custom-call | flops 2000000 | bytes 1000000 | tf_op jit(solution)/shard_map/owner/pallas_call | solution.py:528
  39.6 0.0 copy-start.2
  39.6 17.2 %all_to_all.10 = bf16[64,4,2,128]{3,2,1,0:T(2,128)(2,1)S(1)} all-to-all(bf16[64,4,2,128]{3,2,1,0:T(2,128)(2,1)S(1)} %bitcast.19), channel_id=1, replica_groups=mesh['seq'=64,'chan'=4] {'seq'}, dimensions={0} | all-to-all | bytes 262144 | tf_op jit(solution)/shard_map/all_to_all | solution.py:579
  56.9 1.4 %collective-permute-start.2 = (bf16[128,128]{1,0:T(8,128)(2,1)S(1)}, bf16[128,128]{1,0:T(8,128)(2,1)S(1)}, u32[]{:S(2)}, u32[]{:S(2)}) collective-permute-start(bf16[128,128]{1,0:T(8,128)(2,1)S(1)} %bitcast.21), channel_id=1, source_target_pairs={{0,1},{1,0},{2,3},{3,2},{4,5},{5,4},{6,7},{7,6},{8,9},{9,8},{10,11... | collective-permute-start | bytes 98312 | tf_op jit(solution)/shard_map/ppermute | solution.py:621
  58.2 0.0 copy-done
  58.3 0.0 copy-done.2
  58.3 0.0 copy-start.4
  58.3 0.0 copy-start.5
  58.3 1.5 %query.1 = (bf16[1024,128]{1,0:T(8,128)(2,1)S(1)}, f32[7,1024]{1,0:T(8,128)}) custom-call(bf16[512,128]{1,0:T(8,128)(2,1)S(1)} %bitcast.17, f32[1024,128]{1,0:T(8,128)S(1)} %forward.1.own_out, f32[48,128]{1,0:T(8,128)S(1)} %collective-permute-done.tail, f32[1024,128]{1,0:T(8,128)S(1)} %copy-done, f32[320,128]{1,0:T(8,128)S(1)} %copy-done.1, ...), custom_call_target="tpu_custom_call" | custom-call | flops 5000000 | bytes 1000000 | tf_op jit(solution)/shard_map/query/pallas_call | solution.py:528
  59.8 0.0 collective-permute-done.2
  59.8 2.7 %collective-permute-start.3 = (bf16[128,128]{1,0:T(8,128)(2,1)S(1)}, bf16[128,128]{1,0:T(8,128)(2,1)S(1)}, u32[]{:S(2)}, u32[]{:S(2)}) collective-permute-start(bf16[128,128]{1,0:T(8,128)(2,1)S(1)} %add_convert_fusion.near), channel_id=1, source_target_pairs={{0,3},{1,2},{2,1},{3,0},{4,7},{5,6},{6,5},{7,4},{8,11},{9,10},{10,... | collective-permute-start | bytes 98312 | tf_op jit(solution)/shard_map/ppermute | solution.py:621
  62.6 0.0 copy-done.4
  62.6 0.0 copy-done.5
  62.6 2.4 %key.1 = (bf16[1024,128]{1,0:T(8,128)(2,1)}, bf16[1024,128]{1,0:T(8,128)(2,1)}, bf16[1024,128]{1,0:T(8,128)(2,1)}) custom-call(bf16[512,128]{1,0:T(8,128)(2,1)S(1)} %bitcast.18, f32[1024,128]{1,0:T(8,128)S(1)} %copy-done.4, f32[1024,128]{1,0:T(8,128)S(1)} %copy-done.5, f32[1024,128]{1,0:T(8,128)S(1)} %copy-done, f32[48,128]{1,0:T(8,128)S(1)} %collective-permute-done.tail, ...), custom_call_target="tpu_custom_call" | custom-call | flops 8000000 | bytes 2000000 | tf_op jit(solution)/shard_map/key/pallas_call | solution.py:528
  65.0 0.0 collective-permute-done.3.far
  65.0 1.1 %poles.1 = f32[16,1024]{1,0:T(8,128)} custom-call(bf16[128,128]{1,0:T(8,128)(2,1)S(1)} %add_convert_fusion.near, bf16[128,128]{1,0:T(8,128)(2,1)S(1)} %collective-permute-done.3.far), custom_call_target="tpu_custom_call" | custom-call | flops 100000 | bytes 100000 | tf_op jit(solution)/shard_map/poles/pallas_call | solution.py:528
  (4 shorter events, 0.1 us)
Async XLA Ops:
  10.5 20.7 %copy-start.3 = (f32[1024,128]{1,0:T(8,128)S(1)}, f32[1024,128]{1,0:T(8,128)}, u32[]{:S(2)}) copy-start(f32[1024,128]{1,0:T(8,128)} %get-tuple-element.26.gated) | copy-start | bytes 1572868
  10.6 13.2 %copy-start.7 = (f32[48,128]{1,0:T(8,128)S(1)}, f32[48,128]{1,0:T(8,128)}, u32[]{:S(2)}) copy-start(f32[48,128]{1,0:T(8,128)} %get-tuple-element.28) | copy-start | bytes 73732
  10.6 16.9 %copy-start.6 = (f32[128,128]{1,0:T(8,128)S(1)}, f32[128,128]{1,0:T(8,128)}, u32[]{:S(2)}) copy-start(f32[128,128]{1,0:T(8,128)} %get-tuple-element.29) | copy-start | bytes 196612
  10.6 28.2 %all-to-all-start = ((bf16[64,12,2,128]{3,2,1,0:T(2,128)(2,1)}), bf16[64,12,2,128]{3,2,1,0:T(2,128)(2,1)S(1)}, u32[]{:S(2)}, u32[]{:S(2)}) async-start(bf16[64,12,2,128]{3,2,1,0:T(2,128)(2,1)} %bitcast.20), calls=%async_computation | async-start | bytes 786432 | tf_op jit(solution)/shard_map/all_to_all | solution.py:579
  23.7 7.5 %copy-start.1 = (f32[320,128]{1,0:T(8,128)S(1)}, f32[320,128]{1,0:T(8,128)}, u32[]{:S(2)}) copy-start(f32[320,128]{1,0:T(8,128)} %get-tuple-element.27.par) | copy-start | bytes 491524
  23.7 8.7 %collective-permute-start = (f32[48,128]{1,0:T(8,128)S(1)}, f32[48,128]{1,0:T(8,128)S(1)}, u32[]{:S(2)}, u32[]{:S(2)}) collective-permute-start(f32[48,128]{1,0:T(8,128)S(1)} %copy-done.7), channel_id=1, source_target_pairs={{0,4},{4,8},{8,12},{12,16},{16,20},{20,24},{24,28},{28,32},{32,36}... | collective-permute-start | bytes 73736 | tf_op jit(solution)/shard_map/ppermute | solution.py:588
  27.4 6.5 %collective-permute-start.1 = (f32[128,128]{1,0:T(8,128)S(1)}, f32[128,128]{1,0:T(8,128)S(1)}, u32[]{:S(2)}, u32[]{:S(2)}) collective-permute-start(f32[128,128]{1,0:T(8,128)S(1)} %copy-done.6), channel_id=1, source_target_pairs={{4,0},{8,4},{12,8},{16,12},{20,16},{24,20},{28,24},{32,28},{36,32}... | collective-permute-start | bytes 196616 | tf_op jit(solution)/shard_map/ppermute | solution.py:589
  32.4 25.8 %copy-start = (f32[1024,128]{1,0:T(8,128)S(1)}, f32[1024,128]{1,0:T(8,128)}, u32[]{:S(2)}) copy-start(f32[1024,128]{1,0:T(8,128)} %get-tuple-element.34.vt) | copy-start | bytes 1572868
  39.6 18.6 %copy-start.2 = (bf16[1024,128]{1,0:T(8,128)(2,1)S(1)}, bf16[1024,128]{1,0:T(8,128)(2,1)}, u32[]{:S(2)}) copy-start(bf16[1024,128]{1,0:T(8,128)(2,1)} %cot.1) | copy-start | bytes 786436
  56.9 2.9 %collective-permute-start.2 = (bf16[128,128]{1,0:T(8,128)(2,1)S(1)}, bf16[128,128]{1,0:T(8,128)(2,1)S(1)}, u32[]{:S(2)}, u32[]{:S(2)}) collective-permute-start(bf16[128,128]{1,0:T(8,128)(2,1)S(1)} %bitcast.21), channel_id=1, source_target_pairs={{0,1},{1,0},{2,3},{3,2},{4,5},{5,4},{6,7},{7,6},{8,9},{9,8},{10,11... | collective-permute-start | bytes 98312 | tf_op jit(solution)/shard_map/ppermute | solution.py:621
  58.3 4.3 %copy-start.4 = (f32[1024,128]{1,0:T(8,128)S(1)}, f32[1024,128]{1,0:T(8,128)}, u32[]{:S(2)}) copy-start(f32[1024,128]{1,0:T(8,128)} %get-tuple-element.32.gate) | copy-start | bytes 1572868
  58.3 4.3 %copy-start.5 = (f32[1024,128]{1,0:T(8,128)S(1)}, f32[1024,128]{1,0:T(8,128)}, u32[]{:S(2)}) copy-start(f32[1024,128]{1,0:T(8,128)} %get-tuple-element.33.local) | copy-start | bytes 1572868
  59.8 5.2 %collective-permute-start.3 = (bf16[128,128]{1,0:T(8,128)(2,1)S(1)}, bf16[128,128]{1,0:T(8,128)(2,1)S(1)}, u32[]{:S(2)}, u32[]{:S(2)}) collective-permute-start(bf16[128,128]{1,0:T(8,128)(2,1)S(1)} %add_convert_fusion.near), channel_id=1, source_target_pairs={{0,3},{1,2},{2,1},{3,0},{4,7},{5,6},{6,5},{7,4},{8,11},{9,10},{10,... | collective-permute-start | bytes 98312 | tf_op jit(solution)/shard_map/ppermute | solution.py:621

commit v5 on v4

--- a/solution.py
+++ b/solution.py
@@ -46,27 +46,23 @@
     return lax.broadcasted_iota(jnp.int32, (SUB, LANES), 1) // 16
 
 
+def skewed(x, way):
+    row = lax.broadcasted_iota(jnp.int32, (SUB, LANES), 0)
+    lane = lax.broadcasted_iota(jnp.int32, (SUB, LANES), 1)
+    return jnp.take_along_axis(x, (lane + way * 16 * row) % LANES, axis=1)
+
+
+def turned(x, way):
+    row = lax.broadcasted_iota(jnp.int32, (SUB, LANES), 0)
+    return jnp.take_along_axis(x, (row + way * lane_group()) % SUB, axis=0)
+
+
 def to_owner(x):
-    y = pltpu.roll(x, 0, 1, stride=16, stride_axis=0)
-    group = lane_group()
-    for bit in (1, 2, 4):
-        y = jnp.where((group & bit) != 0, pltpu.roll(y, SUB - bit, 0), y)
-    return pltpu.roll(y, 0, 1, stride=16, stride_axis=0)
-
-
-def skew_left(x):
-    row = lax.broadcasted_iota(jnp.int32, (SUB, LANES), 0)
-    for bit in (1, 2, 4):
-        x = jnp.where((row & bit) != 0, pltpu.roll(x, LANES - 16 * bit, 1), x)
-    return x
+    return skewed(turned(skewed(x, -1), 1), -1)
 
 
 def from_owner(x):
-    y = skew_left(x)
-    group = lane_group()
-    for bit in (1, 2, 4):
-        y = jnp.where((group & bit) != 0, pltpu.roll(y, bit, 0), y)
-    return skew_left(y)
+    return skewed(turned(skewed(x, 1), -1), 1)
 
 
 def decay_of(par, r):
@@ -206,9 +202,9 @@
 
 
 def first_kernel(*refs):
-    sources, targets, refs = refs[:7], refs[7:15], refs[15:]
+    sources, targets, refs = refs[:7], refs[7:14], refs[14:]
     (k, v, q, cot, rates, residues, amounts), refs = refs[:7], refs[7:]
-    (vt, gate, gated, local, par, tail, head, message), refs = refs[:8], refs[8:]
+    (vt, gate, gated, local, par, head, message), refs = refs[:7], refs[7:]
     kt, zt, keys, gather, spread, came, went = refs
     copies = [
         pltpu.make_async_copy(a, b, came.at[n])
@@ -216,7 +212,7 @@
     ]
     leaving = [
         pltpu.make_async_copy(a, b, went.at[n])
-        for n, (a, b) in enumerate(zip((vt, gate, gated, local, par, tail, head, message), targets))
+        for n, (a, b) in enumerate(zip((vt, gate, gated, local, par, head, message), targets))
     ]
     for copy in copies:
         copy.start()
@@ -239,11 +235,9 @@
         )
         par[pl.ds(2 * SUB * POLES + s, TAPS, stride=SUB), :] = amounts[:, rows]
     edge = SUB * EDGE
-    last = slice(SUB * (LEN - HALO), SUB * LEN)
-    tail[...] = kt[last, :]
     head[0:edge, :] = zt[0:edge, :]
     head[edge:, :] = vt[0:edge, :]
-    for n in (4, 5, 6):
+    for n in (4, 5):
         leaving[n].start()
     for row, block in (
         (ROW_V, vt[0:edge, :]),
@@ -280,33 +274,44 @@
             block = to_owner(gather[pl.ds(row * SUB * SUB + s, SUB, stride=SUB), :])
             spread[pl.ds(s * SUB * ROWS_OUT + row, SUB, stride=ROWS_OUT), :] = block
     message[...] = spread[...].astype(BF16)
-    leaving[7].start()
+    leaving[6].start()
     for copy in leaving:
         copy.wait()
 
 
-def owner_kernel(count, scale, arrived, mine, out, x, y, kept, fix):
+def owner_kernel(
+    count, scale, index, arrived, rate_rows, residue_rows, tap_rows, out, x, y, kept, fix, mine
+):
     x[0:ROWS_OUT, :] = jnp.zeros((ROWS_OUT, LANES), F32)
     x[ROWS_OUT:, :] = arrived[...].astype(F32)
     even = lax.broadcasted_iota(jnp.int32, (SUB, LANES), 0) % 2 == 0
     group = lane_group()
     zero = jnp.zeros((SUB, LANES), F32)
 
+    block = pl.ds(pl.multiple_of((index[0] // SUB) * LANES, LANES), LANES)
+    place = index[0] % SUB
+    for n, ref in enumerate((rate_rows, residue_rows)):
+        for half in range(2):
+            mine[...] = to_owner(ref[half * SUB : (half + 1) * SUB, block])
+            fix[2 * n + half : 2 * n + half + 1, :] = mine[pl.ds(place, 1), :]
+    held = jnp.where(group[0:TAPS, :] == (SUB - place) % SUB, tap_rows[:, block], 0.0)
+    for shift in (16, 32, 64):
+        held = held + pltpu.roll(held, shift, 1)
+    taps = [jnp.broadcast_to(held[j : j + 1, :], (SUB, LANES)) for j in range(TAPS)]
+
     def pattern(ref, row):
         return jnp.where(even, ref[pl.ds(row, 1), :], ref[pl.ds(row + 1, 1), :])
 
-    rate = pattern(mine, 0)
+    rate = pattern(fix, 0)
     weight = jnp.sqrt(one_minus_exp(2.0 * rate))
-    coef = pattern(mine, 2) * weight
+    coef = pattern(fix, 2) * weight
     leap = jnp.exp(-float(LEN) * rate)
-    taps = [mine[pl.ds(4 + j, 1), :] for j in range(TAPS)]
-    rates = [mine[pl.ds(half, 1), :] for half in range(2)]
+    rates = [fix[pl.ds(half, 1), :] for half in range(2)]
     growth = [jnp.broadcast_to(jnp.exp(r), (SUB, LANES)) for r in rates]
     powers = [
         [jnp.broadcast_to(jnp.exp(-float(LEN - t) * r), (SUB, LANES)) for t in range(HALO)]
         for r in rates
     ]
-    taps = [jnp.broadcast_to(tap, (SUB, LANES)) for tap in taps]
 
     source = lax.broadcasted_iota(jnp.int32, (LANES, SUB * LANES), 0)
     target = lax.broadcasted_iota(jnp.int32, (LANES, SUB * LANES), 1)
@@ -397,12 +402,10 @@
             part = part + pltpu.roll(part, shift, 1)
         short = short + jnp.where(group == j, part, 0.0)
     short = short * scale
-    coarse = short.astype(BF16).astype(F32)
-    fine = short - coarse
     for d in range(count):
         y[pl.ds(d * ROWS_BACK + 4, 2), :] = owned
-        y[pl.ds(d * ROWS_BACK + 6, 1), :] = coarse
-        y[pl.ds(d * ROWS_BACK + 7, 1), :] = fine
+        y[pl.ds(d * ROWS_BACK + 6, 1), :] = short
+        y[pl.ds(d * ROWS_BACK + 7, 1), :] = x[pl.ds(d * ROWS_OUT + ROW_K, 1), :]
     out[...] = y[...].astype(BF16)
 
 
@@ -429,9 +432,9 @@
         lax.fori_loop(0, LEN, forward, ahead, unroll=16)
 
 
-def halo_gates(tail, par):
+def halo_gates(last, par):
     return [
-        add_in_order(tap_of(par, j) * tail[tile(HALO + t - j), :] for j in range(t + 1, TAPS))
+        add_in_order(tap_of(par, j) * last[tile(EDGE + t - j), :] for j in range(t + 1, TAPS))
         for t in range(HALO)
     ]
 
@@ -444,12 +447,15 @@
             state[pl.ds(row * SUB * SUB + s, SUB, stride=SUB), :] = from_owner(block)
 
 
-def query_kernel(arrived, own_out, tail, vt, par, cot, grad_q, grad_short, x, state, long_out):
+def query_kernel(
+    arrived, own_out, vt, par, cot, grad_q, extra_gate, grad_short, x, state, long_out, last
+):
     unpack(arrived, x, state, 0)
     for s in range(SUB):
-        coarse = x[pl.ds(s * SUB * ROWS_BACK + 6, SUB, stride=ROWS_BACK), :]
-        fine = x[pl.ds(s * SUB * ROWS_BACK + 7, SUB, stride=ROWS_BACK), :]
-        grad_short[:, s * LANES : (s + 1) * LANES] = from_owner(coarse + fine)[0:TAPS, :]
+        short = x[pl.ds(s * SUB * ROWS_BACK + 6, SUB, stride=ROWS_BACK), :]
+        grad_short[:, s * LANES : (s + 1) * LANES] = from_owner(short)[0:TAPS, :]
+        keys = x[pl.ds(s * SUB * ROWS_BACK + 7, SUB, stride=ROWS_BACK), :]
+        last[pl.ds(s, SUB, stride=SUB), :] = from_owner(keys)
     decay = [decay_of(par, r) for r in range(POLES)]
 
     def forward(t, terms):
@@ -457,9 +463,10 @@
         return tuple(q * d for q, d in zip(terms, decay))
 
     terms = tuple(coef_of(par, r) * state[tile(r), :] for r in range(POLES))
-    gates = halo_gates(tail, par)
+    gates = halo_gates(last, par)
     for t in range(EDGE):
         if t < HALO:
+            extra_gate[tile(t), :] = gates[t]
             extra = gates[t] * vt[tile(t), :]
             terms = tuple(q + coef_of(par, r) * extra for r, q in enumerate(terms))
         terms = forward(t, terms)
@@ -470,7 +477,7 @@
 
 
 def key_kernel(
-    arrived, gate, local, vt, tail, head, par, query,
+    arrived, gate, local, vt, extra_gate, head, par, query,
     grad_k, grad_v, grad_q, x, state, slope, vals, gone,
 ):
     leaving = pltpu.make_async_copy(query, grad_q, gone)
@@ -503,9 +510,9 @@
     terms = tuple(coef_of(par, r) * state[tile(r), :] for r in range(POLES))
     carry = (terms, tuple(ahead))
     carry = lax.fori_loop(0, LEN - EDGE, backward, carry, unroll=24)
-    gates = halo_gates(tail, par)
     for t in reversed(range(EDGE)):
-        carry = backward(LEN - 1 - t, carry, gates[t] if t < HALO else None)
+        extra = extra_gate[tile(t), :] if t < HALO else None
+        carry = backward(LEN - 1 - t, carry, extra)
     for s in range(SUB):
         rows = slice(s * LANES, (s + 1) * LANES)
         grad_k[rows, :] = slope[across(s), :].T.astype(BF16)
@@ -528,7 +535,10 @@
     return pl.pallas_call(
         kernel,
         out_shape=outs,
-        in_specs=[pl.BlockSpec(memory_space=space)] * len(operands),
+        in_specs=[
+            pl.BlockSpec(memory_space=pltpu.SMEM if a.dtype == jnp.int32 else space)
+            for a in operands
+        ],
         out_specs=[pl.BlockSpec(memory_space=s) for s in spaces],
         scratch_shapes=scratch,
         compiler_params=pltpu.CompilerParams(vmem_limit_bytes=vmem),
@@ -551,9 +561,9 @@
     full, edge, halo = SUB * LEN, SUB * EDGE, SUB * HALO
 
     operands = (k_in, v_in, q_in, cotangent, rates.T, residues.T, taps_short.T)
-    outs = [shape(full)] * 4 + [shape(SUB * 40), shape(halo), shape(2 * edge)]
+    outs = [shape(full)] * 4 + [shape(SUB * 40), shape(2 * edge)]
     outs.append(shape(count * ROWS_OUT, BF16))
-    vt, gate, gated, local, par, tail, head, message = call(
+    vt, gate, gated, local, par, head, message = call(
         first_kernel,
         "first",
         outs,
@@ -579,13 +589,6 @@
         return lax.all_to_all(x, "seq", split_axis=0, concat_axis=0, tiled=True)
 
     arrived = exchange(message, ROWS_OUT).reshape(count * ROWS_OUT, LANES)
-    start = (index // SUB) * LANES + ((SUB - index % SUB) % SUB) * 16
-    mine = [
-        lax.dynamic_slice(a.T, (0, start), (POLES, 16)).reshape(2, LANES) for a in (rates, residues)
-    ]
-    own_taps = lax.dynamic_slice(taps_short.T, (0, start), (TAPS, 16))
-    mine = jnp.concatenate([*mine, jnp.tile(own_taps, (1, LANES // 16))])
-    tail = lax.ppermute(tail, "seq", [(i, i + 1) for i in range(count - 1)])
     head = lax.ppermute(head, "seq", [(i + 1, i) for i in range(count - 1)])
     (own_out,) = call(
         forward_kernel,
@@ -596,9 +599,7 @@
         flops=10 * 10**6,
         moved=10**6,
     )
-    arrived, own_out, tail, head, mine = lax.optimization_barrier(
-        (arrived, own_out, tail, head, mine)
-    )
+    arrived, own_out, head = lax.optimization_barrier((arrived, own_out, head))
     (back,) = call(
         functools.partial(owner_kernel, count, scale),
         "owner",
@@ -608,8 +609,9 @@
             pltpu.VMEM((count * ROWS_BACK, LANES), F32),
             pltpu.VMEM((3, count, SUB * LANES), F32),
             pltpu.VMEM((count * SUB, LANES), F32),
+            pltpu.VMEM((SUB, LANES), F32),
         ],
-        (arrived, mine),
+        (index.reshape(1), arrived, rates.T, residues.T, taps_short.T),
         flops=2 * 10**6,
         moved=10**6,
     )
@@ -625,12 +627,12 @@
         pltpu.VMEM((SUB * POLES, LANES), F32),
     ]
     near = other(poles, 1)
-    query, grad_short = call(
+    query, extra_gate, grad_short = call(
         query_kernel,
         "query",
-        [shape(channels, BF16), shape(TAPS, F32, channels)],
-        [*swap, pltpu.VMEM((full, LANES), F32)],
-        (returned, own_out, tail, vt, par, cotangent),
+        [shape(channels, BF16), shape(halo), shape(TAPS, F32, channels)],
+        [*swap, pltpu.VMEM((full, LANES), F32), pltpu.VMEM((edge, LANES), F32)],
+        (returned, own_out, vt, par, cotangent),
         flops=5 * 10**6,
         moved=10**6,
     )
@@ -647,7 +649,7 @@
             pltpu.VMEM((full, LANES), F32),
             pltpu.SemaphoreType.DMA,
         ],
-        (returned, gate, local, vt, tail, head, par, query),
+        (returned, gate, local, vt, extra_gate, head, par, query),
         flops=8 * 10**6,
         moved=2 * 10**6,
         last=pltpu.HBM,

time: 66.4 us -> 65.3 us (0.983)
  waiting for transfers between devices: 6.38 us -> 11.6 us
  starting transfers between devices: 22.8 us -> 19.7 us
  local copies, waits for them, and re-layouts: 1.86 us -> 0.08 us
  Pallas kernels: 16.9 us -> 16 us
    ppermute x1 -> x0, starting transfers between devices: 3.67 us -> none  [per_device(): tail = lax.ppermute(tail, 'seq', [(i, i + 1) for i in range(count - 1)])]
    all_to_all x1, waiting for transfers between devices: 4.92 us -> 8.49 us  [exchange(): return lax.all_to_all(x, 'seq', split_axis=0, concat_axis=0, tiled=True)]
    dynamic_slice x2 -> x0, local copies, waits for them, and re-layouts: 1.55 us -> none  [the longest x1 0.79 us: per_device(): lax.dynamic_slice(a.T, (0, start), (POLES, 16)).reshape(2, LANES)]
    ppermute x1, waiting for transfers between devices: 1.45 us -> 2.93 us  [per_device(): head = lax.ppermute(head, 'seq', [(i + 1, i) for i in range(count - 1)])]
    pallas_call x6, Pallas kernels: 16.9 us -> 16 us  [call(): pl.pallas_call(kernel, out_shape=outs, in_specs=[pl.BlockSpec(memory_spac...]
  transfers between devices with their start and end apart: 5 -> 4, of which waited for: 2 -> 3; matrix products, arithmetic and copies ran while one was open for 3% -> 0% of each run, Pallas kernels for 8% -> 7%
where the time goes in v5:
time: 65.3 us; the launch traced here: 64.8 us
  starting transfers between devices  19.7 us (30%)
  blocking collectives  16.6 us (25%)
  Pallas kernels  16 us (25%)
  waiting for transfers between devices  11.6 us (18%)
  between operations  0.8 us (1%)
    all_to_all x1, blocking collectives, exchange(): return lax.all_to_all(x, 'seq', split_axis=0, concat_axis=0, tiled=True)  16.6 us
    pallas_call x6, Pallas kernels, call(): pl.pallas_call(kernel, out_shape=outs, in_specs=[pl.BlockSpec(memory_spac...  16 us
    all_to_all x1, starting transfers between devices, exchange(): return lax.all_to_all(x, 'seq', split_axis=0, concat_axis=0, tiled=True)  13.1 us
    all_to_all x1, waiting for transfers between devices, exchange(): return lax.all_to_all(x, 'seq', split_axis=0, concat_axis=0, tiled=True)  8.49 us
    ppermute x2, starting transfers between devices, other(): return lax.ppermute(x, 'chan', [(i, i ^ bit) for i in range(chans)])  4.2 us
    ppermute x1, waiting for transfers between devices, per_device(): head = lax.ppermute(head, 'seq', [(i + 1, i) for i in range(count - 1)])  2.93 us
    ppermute x1, starting transfers between devices, per_device(): head = lax.ppermute(head, 'seq', [(i + 1, i) for i in range(count - 1)])  2.36 us
  transfers between devices with their start and end apart: 4, of which 3 were waited for; matrix products, arithmetic and copies ran while one was open for 0% of the time, Pallas kernels for 7%

profile of v5, /device:TPU:1, one launch (start us, length us, event | category | flops | bytes accessed | tf_op | source)
XLA Modules:
  0.0 64.8 jit_solution(17487952475122142155)
XLA Ops:
  0.6 9.7 %first.1 = (f32[1024,128]{1,0:T(8,128)}, f32[1024,128]{1,0:T(8,128)}, f32[1024,128]{1,0:T(8,128)}, f32[1024,128]{1,0:T(8,128)}, f32[320,128]{1,0:T(8,128)}, /*in...) custom-call(bf16[1024,128]{1,0:T(8,128)(2,1)} %refs_0_.1, bf16[1024,128]{1,0:T(8,128)(2,1)} %refs_1_.1, ...), custom_call_target="tpu_custom_call" | custom-call | flops 48000000 | bytes 4000000 | tf_op jit(solution)/shard_map/first/pallas_call | solution.py:535
  10.3 0.0 copy-start.3
  10.3 0.0 copy-start.9
  10.3 0.0 copy-start.1
  10.3 13.1 %all-to-all-start = ((bf16[64,12,2,128]{3,2,1,0:T(2,128)(2,1)}), bf16[64,12,2,128]{3,2,1,0:T(2,128)(2,1)S(1)}, u32[]{:S(2)}, u32[]{:S(2)}) async-start(bf16[64,12,2,128]{3,2,1,0:T(2,128)(2,1)} %bitcast.21), calls=%async_computation | async-start | bytes 786432 | tf_op jit(solution)/shard_map/all_to_all | solution.py:589
  23.5 0.0 copy-done.9
  23.5 2.4 %collective-permute-start = (f32[128,128]{1,0:T(8,128)S(1)}, f32[128,128]{1,0:T(8,128)S(1)}, u32[]{:S(2)}, u32[]{:S(2)}) collective-permute-start(f32[128,128]{1,0:T(8,128)S(1)} %copy-done.9), channel_id=1, source_target_pairs={{4,0},{8,4},{12,8},{16,12},{20,16},{24,20},{28,24},{32,28},{36,32}... | collective-permute-start | bytes 196616 | tf_op jit(solution)/shard_map/ppermute | solution.py:592
  25.9 0.0 copy-done.3
  25.9 0.0 copy-done.1
  25.9 0.0 copy-start.6
  25.9 0.0 copy-start.7
  25.9 0.0 copy-start.8
  25.9 1.2 %forward.1.own_out = f32[1024,128]{1,0:T(8,128)S(1)} custom-call(f32[1024,128]{1,0:T(8,128)S(1)} %copy-done.3, f32[320,128]{1,0:T(8,128)S(1)} %copy-done.1), custom_call_target="tpu_custom_call" | custom-call | flops 10000000 | bytes 1000000 | tf_op jit(solution)/shard_map/forward/pallas_call | solution.py:535
  27.1 0.0 copy-start
  27.1 2.9 %collective-permute-done.head = f32[128,128]{1,0:T(8,128)S(1)} collective-permute-done((f32[128,128]{1,0:T(8,128)S(1)}, f32[128,128]{1,0:T(8,128)S(1)}, u32[]{:S(2)}, u32[]{:S(2)}) %collective-permute-start) | collective-permute-done | bytes 65568 | tf_op jit(solution)/shard_map/ppermute | solution.py:592
  30.0 8.5 %all-to-all-done = bf16[64,12,2,128]{3,2,1,0:T(2,128)(2,1)S(1)} async-done(((bf16[64,12,2,128]{3,2,1,0:T(2,128)(2,1)}), bf16[64,12,2,128]{3,2,1,0:T(2,128)(2,1)S(1)}, u32[]{:S(2)}, u32[]{:S(2)}) %all-to-all-start) | async-done | bytes 393248 | tf_op jit(solution)/shard_map/all_to_all | solution.py:589
  38.5 0.0 copy-done.6
  38.5 0.0 copy-done.7
  38.5 0.0 copy-done.8
  38.5 0.9 %owner.1 = bf16[512,128]{1,0:T(8,128)(2,1)S(1)} custom-call(s32[1]{0:T(128)} %bitcast.index, bf16[1536,128]{1,0:T(8,128)(2,1)S(1)} %bitcast.11, f32[16,1024]{1,0:T(8,128)S(1)} %bitcast.16, f32[16,1024]{1,0:T(8,128)S(1)} %bitcast.18, f32[7,1024]{1,0:T(8,128)S(1)} %bitcast.20), custom_call_target="tpu_custom_call" | custom-call | flops 2000000 | bytes 1000000 | tf_op jit(solution)/shard_map/owner/pallas_call | solution.py:535
  39.5 0.0 copy-start.2
  39.5 16.6 %all_to_all.10 = bf16[64,4,2,128]{3,2,1,0:T(2,128)(2,1)S(1)} all-to-all(bf16[64,4,2,128]{3,2,1,0:T(2,128)(2,1)S(1)} %bitcast.14), channel_id=1, replica_groups=mesh['seq'=64,'chan'=4] {'seq'}, dimensions={0} | all-to-all | bytes 262144 | tf_op jit(solution)/shard_map/all_to_all | solution.py:589
  56.1 1.4 %collective-permute-start.1 = (bf16[128,128]{1,0:T(8,128)(2,1)S(1)}, bf16[128,128]{1,0:T(8,128)(2,1)S(1)}, u32[]{:S(2)}, u32[]{:S(2)}) collective-permute-start(bf16[128,128]{1,0:T(8,128)(2,1)S(1)} %bitcast.22), channel_id=1, source_target_pairs={{0,1},{1,0},{2,3},{3,2},{4,5},{5,4},{6,7},{7,6},{8,9},{9,8},{10,11... | collective-permute-start | bytes 98312 | tf_op jit(solution)/shard_map/ppermute | solution.py:623
  57.5 0.0 copy-done
  57.5 0.0 copy-done.2
  57.5 0.0 copy-start.4
  57.5 0.0 copy-start.5
  57.5 1.3 %query.1 = (bf16[1024,128]{1,0:T(8,128)(2,1)S(1)}, f32[48,128]{1,0:T(8,128)S(1)}, f32[7,1024]{1,0:T(8,128)}) custom-call(bf16[512,128]{1,0:T(8,128)(2,1)S(1)} %bitcast.12, f32[1024,128]{1,0:T(8,128)S(1)} %forward.1.own_out, f32[1024,128]{1,0:T(8,128)S(1)} %copy-done, f32[320,128]{1,0:T(8,128)S(1)} %copy-done.1, bf16[1024,128]{1,0:T(8,128)(2,1)S(1)} %copy-done.2), custom_call_target="tpu_custom_call" | custom-call | flops 5000000 | bytes 1000000 | tf_op jit(solution)/shard_map/query/pallas_call | solution.py:535
  58.8 0.2 collective-permute-done.1
  59.0 2.8 %collective-permute-start.2 = (bf16[128,128]{1,0:T(8,128)(2,1)S(1)}, bf16[128,128]{1,0:T(8,128)(2,1)S(1)}, u32[]{:S(2)}, u32[]{:S(2)}) collective-permute-start(bf16[128,128]{1,0:T(8,128)(2,1)S(1)} %add_convert_fusion.near), channel_id=1, source_target_pairs={{0,3},{1,2},{2,1},{3,0},{4,7},{5,6},{6,5},{7,4},{8,11},{9,10},{10,... | collective-permute-start | bytes 98312 | tf_op jit(solution)/shard_map/ppermute | solution.py:623
  61.8 0.0 copy-done.4
  61.8 0.0 copy-done.5
  61.8 2.1 %key.1 = (bf16[1024,128]{1,0:T(8,128)(2,1)}, bf16[1024,128]{1,0:T(8,128)(2,1)}, bf16[1024,128]{1,0:T(8,128)(2,1)}) custom-call(bf16[512,128]{1,0:T(8,128)(2,1)S(1)} %bitcast.13, f32[1024,128]{1,0:T(8,128)S(1)} %copy-done.4, f32[1024,128]{1,0:T(8,128)S(1)} %copy-done.5, f32[1024,128]{1,0:T(8,128)S(1)} %copy-done, f32[48,128]{1,0:T(8,128)S(1)} %get-tuple-element.32.extra_gate, ...), custom_call_target="tpu_custom_call" | custom-call | flops 8000000 | bytes 2000000 | tf_op jit(solution)/shard_map/key/pallas_call | solution.py:535
  64.0 0.0 collective-permute-done.2.far
  64.0 0.8 %poles.1 = f32[16,1024]{1,0:T(8,128)} custom-call(bf16[128,128]{1,0:T(8,128)(2,1)S(1)} %add_convert_fusion.near, bf16[128,128]{1,0:T(8,128)(2,1)S(1)} %collective-permute-done.2.far), custom_call_target="tpu_custom_call" | custom-call | flops 100000 | bytes 100000 | tf_op jit(solution)/shard_map/poles/pallas_call | solution.py:535
  (2 shorter events, 0.0 us)
Async XLA Ops:
  10.3 15.6 %copy-start.3 = (f32[1024,128]{1,0:T(8,128)S(1)}, f32[1024,128]{1,0:T(8,128)}, u32[]{:S(2)}) copy-start(f32[1024,128]{1,0:T(8,128)} %get-tuple-element.24.gated) | copy-start | bytes 1572868
  10.3 13.2 %copy-start.9 = (f32[128,128]{1,0:T(8,128)S(1)}, f32[128,128]{1,0:T(8,128)}, u32[]{:S(2)}) copy-start(f32[128,128]{1,0:T(8,128)} %get-tuple-element.26) | copy-start | bytes 196612
  10.3 15.5 %copy-start.1 = (f32[320,128]{1,0:T(8,128)S(1)}, f32[320,128]{1,0:T(8,128)}, u32[]{:S(2)}) copy-start(f32[320,128]{1,0:T(8,128)} %get-tuple-element.25.par) | copy-start | bytes 491524
  10.3 28.2 %all-to-all-start = ((bf16[64,12,2,128]{3,2,1,0:T(2,128)(2,1)}), bf16[64,12,2,128]{3,2,1,0:T(2,128)(2,1)S(1)}, u32[]{:S(2)}, u32[]{:S(2)}) async-start(bf16[64,12,2,128]{3,2,1,0:T(2,128)(2,1)} %bitcast.21), calls=%async_computation | async-start | bytes 786432 | tf_op jit(solution)/shard_map/all_to_all | solution.py:589
  23.5 6.6 %collective-permute-start = (f32[128,128]{1,0:T(8,128)S(1)}, f32[128,128]{1,0:T(8,128)S(1)}, u32[]{:S(2)}, u32[]{:S(2)}) collective-permute-start(f32[128,128]{1,0:T(8,128)S(1)} %copy-done.9), channel_id=1, source_target_pairs={{4,0},{8,4},{12,8},{16,12},{20,16},{24,20},{28,24},{32,28},{36,32}... | collective-permute-start | bytes 196616 | tf_op jit(solution)/shard_map/ppermute | solution.py:592
  25.9 12.7 %copy-start.6 = (f32[1024,16]{0,1:T(8,128)S(1)}, f32[1024,16]{0,1:T(8,128)}, u32[]{:S(2)}) copy-start(f32[1024,16]{0,1:T(8,128)} %param.13) | copy-start | bytes 196612
  25.9 12.6 %copy-start.7 = (f32[1024,16]{0,1:T(8,128)S(1)}, f32[1024,16]{0,1:T(8,128)}, u32[]{:S(2)}) copy-start(f32[1024,16]{0,1:T(8,128)} %param.12) | copy-start | bytes 196612
  25.9 12.6 %copy-start.8 = (f32[1024,7]{0,1:T(8,128)S(1)}, f32[1024,7]{0,1:T(8,128)}, u32[]{:S(2)}) copy-start(f32[1024,7]{0,1:T(8,128)} %param.11) | copy-start | bytes 86020
  27.1 30.4 %copy-start = (f32[1024,128]{1,0:T(8,128)S(1)}, f32[1024,128]{1,0:T(8,128)}, u32[]{:S(2)}) copy-start(f32[1024,128]{1,0:T(8,128)} %get-tuple-element.30.vt) | copy-start | bytes 1572868
  39.5 18.1 %copy-start.2 = (bf16[1024,128]{1,0:T(8,128)(2,1)S(1)}, bf16[1024,128]{1,0:T(8,128)(2,1)}, u32[]{:S(2)}) copy-start(bf16[1024,128]{1,0:T(8,128)(2,1)} %cot.1) | copy-start | bytes 786436
  56.1 2.9 %collective-permute-start.1 = (bf16[128,128]{1,0:T(8,128)(2,1)S(1)}, bf16[128,128]{1,0:T(8,128)(2,1)S(1)}, u32[]{:S(2)}, u32[]{:S(2)}) collective-permute-start(bf16[128,128]{1,0:T(8,128)(2,1)S(1)} %bitcast.22), channel_id=1, source_target_pairs={{0,1},{1,0},{2,3},{3,2},{4,5},{5,4},{6,7},{7,6},{8,9},{9,8},{10,11... | collective-permute-start | bytes 98312 | tf_op jit(solution)/shard_map/ppermute | solution.py:623
  57.5 4.3 %copy-start.4 = (f32[1024,128]{1,0:T(8,128)S(1)}, f32[1024,128]{1,0:T(8,128)}, u32[]{:S(2)}) copy-start(f32[1024,128]{1,0:T(8,128)} %get-tuple-element.28.gate) | copy-start | bytes 1572868
  57.5 4.3 %copy-start.5 = (f32[1024,128]{1,0:T(8,128)S(1)}, f32[1024,128]{1,0:T(8,128)}, u32[]{:S(2)}) copy-start(f32[1024,128]{1,0:T(8,128)} %get-tuple-element.29.local) | copy-start | bytes 1572868
  59.0 5.0 %collective-permute-start.2 = (bf16[128,128]{1,0:T(8,128)(2,1)S(1)}, bf16[128,128]{1,0:T(8,128)(2,1)S(1)}, u32[]{:S(2)}, u32[]{:S(2)}) collective-permute-start(bf16[128,128]{1,0:T(8,128)(2,1)S(1)} %add_convert_fusion.near), channel_id=1, source_target_pairs={{0,3},{1,2},{2,1},{3,0},{4,7},{5,6},{6,5},{7,4},{8,11},{9,10},{10,... | collective-permute-start | bytes 98312 | tf_op jit(solution)/shard_map/ppermute | solution.py:623

commit v6 on v5

--- a/solution.py
+++ b/solution.py
@@ -18,7 +18,7 @@
 EDGE = 8
 ROWS_OUT = 24
 FIR_TERMS = tuple((n, q) for n in range(9) for q in range(2) if (n, q) != (8, 1))
-BACK_MODES, BACK_UNROLL, AHEAD_MODES, AHEAD_UNROLL = 8, 16, 2, 16
+BACK_MODES, BACK_UNROLL, AHEAD_MODES, AHEAD_UNROLL = 8, 16, 2, 32
 ROW_SHORT, ROW_V, ROW_MOMENT, ROW_K, ROW_Z = 6, 7, 8, 22, 23
 ROWS_BACK = 8
 VMEM = 48 * 1024 * 1024
@@ -128,7 +128,7 @@
     return out
 
 
-def scan_down(par, z, v, gate, gated, keys, local, gather):
+def scan_down(par, z, v, gated, keys, local, gather):
     zero = jnp.zeros((SUB, LANES), F32)
     terms = len(FIR_TERMS)
 
@@ -171,22 +171,23 @@
             before = keys_of(m - 1)
             keyed = (now, before)
             after = []
-            for (ahead, power, sums), d in zip(state, decay):
+            for (power, sums), d in zip(state, decay):
                 u = [None] * 4
                 for p in reversed(range(4)):
                     u[p] = power * v[at[p], :]
-                    ahead = ahead + u[p] * gate[at[p], :]
                     power = power * d
-                after.append((ahead, power, tuple(correlate(sums, u, keyed))))
+                after.append((power, tuple(correlate(sums, u, keyed))))
             return tuple(after), before
 
-        state = tuple((zero, d, (zero,) * terms) for d in decay)
+        state = tuple((d, (zero,) * terms) for d in decay)
         carry = (state, keys_of(LEN // 4 - 1))
         state, _ = lax.fori_loop(0, LEN // 4, ahead_step, carry, unroll=AHEAD_UNROLL)
-        for (ahead, _, sums), r in zip(state, modes):
+        for (_, sums), r in zip(state, modes):
             half, slot = divmod(r, SUB)
+            taken = moments(sums)
+            ahead = add_in_order(tap_of(par, j) * value for j, value in enumerate(taken))
             gather[tile(half * SUB + slot), :] = ahead
-            for j, value in enumerate(moments(sums)):
+            for j, value in enumerate(taken):
                 gather[tile((ROW_MOMENT + 2 * j + half) * SUB + slot), :] = value
 
     def step(m, carry):
@@ -267,7 +268,7 @@
     lax.fori_loop(0, LEN // 4, prepare, (zero,) * HALO, unroll=2)
     leaving[1].start()
     leaving[2].start()
-    scan_down(par, zt, vt, gate, gated, keys, local, gather)
+    scan_down(par, zt, vt, gated, keys, local, gather)
     leaving[3].start()
     for row in range(ROWS_OUT):
         for s in range(SUB):
@@ -520,8 +521,9 @@
     leaving.wait()
 
 
-def pole_kernel(near, far, out, x):
-    x[...] = near[...].astype(F32) + far[...].astype(F32)
+def pole_kernel(*refs):
+    *parts, out, x = refs
+    x[...] = add_up([part[...].astype(F32) for part in parts])
     for s in range(SUB):
         for half in range(2):
             block = x[pl.ds(s * SUB * 2 + half, SUB, stride=2), :]
@@ -619,14 +621,14 @@
     poles = returned[:, 2].reshape(2 * count, LANES)
     returned = returned.reshape(count * ROWS_BACK, LANES)
 
-    def other(x, bit):
-        return lax.ppermute(x, "chan", [(i, i ^ bit) for i in range(chans)])
+    others = [
+        lax.ppermute(poles, "chan", [(i, i ^ bits) for i in range(chans)]) for bits in (2, 1, 3)
+    ]
 
     swap = [
         pltpu.VMEM((count * ROWS_BACK, LANES), F32),
         pltpu.VMEM((SUB * POLES, LANES), F32),
     ]
-    near = other(poles, 1)
     query, extra_gate, grad_short = call(
         query_kernel,
         "query",
@@ -636,9 +638,6 @@
         flops=5 * 10**6,
         moved=10**6,
     )
-    near, query = lax.optimization_barrier((near, query))
-    near = (poles.astype(F32) + near.astype(F32)).astype(BF16)
-    far = other(near, 3)
     grad_k, grad_v, grad_q = call(
         key_kernel,
         "key",
@@ -654,12 +653,13 @@
         moved=2 * 10**6,
         last=pltpu.HBM,
     )
+    grad_k, *others = lax.optimization_barrier((grad_k, *others))
     (grad_residues,) = call(
         pole_kernel,
         "poles",
         [shape(POLES, F32, channels)],
         [pltpu.VMEM((2 * count, LANES), F32)],
-        (near, far),
+        (poles, *others),
         flops=10**5,
         moved=10**5,
     )

time: 65.3 us -> 63.5 us (0.972)
  Pallas kernels: 16 us -> 15 us
    pallas_call x6, Pallas kernels: 16 us -> 15 us  [call(): pl.pallas_call(kernel, out_shape=outs, in_specs=[pl.BlockSpec(memory_spac...]
    ppermute x2 -> x3, starting transfers between devices: 4.2 us -> 3.78 us  [per_device(): lax.ppermute(poles, 'chan', [(i, i ^ bits) for i in range(chans)])]
  transfers between devices with their start and end apart: 4 -> 5, of which waited for: 3 -> 3; matrix products, arithmetic and copies ran while one was open for 0% -> 0% of each run, Pallas kernels for 7% -> 7%
where the time goes in v6:
time: 63.5 us; the launch traced here: 63.3 us
  starting transfers between devices  19.3 us (30%)
  blocking collectives  16.6 us (26%)
  Pallas kernels  15 us (24%)
  waiting for transfers between devices  11.5 us (18%)
  between operations  0.8 us (1%)
    all_to_all x1, blocking collectives, exchange(): return lax.all_to_all(x, 'seq', split_axis=0, concat_axis=0, tiled=True)  16.6 us
    pallas_call x6, Pallas kernels, call(): pl.pallas_call(kernel, out_shape=outs, in_specs=[pl.BlockSpec(memory_spac...  15 us
    all_to_all x1, starting transfers between devices, exchange(): return lax.all_to_all(x, 'seq', split_axis=0, concat_axis=0, tiled=True)  13.1 us
    all_to_all x1, waiting for transfers between devices, exchange(): return lax.all_to_all(x, 'seq', split_axis=0, concat_axis=0, tiled=True)  8.49 us
    ppermute x3, starting transfers between devices, per_device(): lax.ppermute(poles, 'chan', [(i, i ^ bits) for i in range(chans)])  3.78 us
    ppermute x1, waiting for transfers between devices, per_device(): head = lax.ppermute(head, 'seq', [(i + 1, i) for i in range(count - 1)])  2.93 us
    ppermute x1, starting transfers between devices, per_device(): head = lax.ppermute(head, 'seq', [(i + 1, i) for i in range(count - 1)])  2.36 us
  transfers between devices with their start and end apart: 5, of which 3 were waited for; matrix products, arithmetic and copies ran while one was open for 0% of the time, Pallas kernels for 7%

profile of v6, /device:TPU:1, one launch (start us, length us, event | category | flops | bytes accessed | tf_op | source)
XLA Modules:
  0.0 63.3 jit_solution(2389280287222218789)
XLA Ops:
  0.6 8.6 %first.1 = (f32[1024,128]{1,0:T(8,128)}, f32[1024,128]{1,0:T(8,128)}, f32[1024,128]{1,0:T(8,128)}, f32[1024,128]{1,0:T(8,128)}, f32[320,128]{1,0:T(8,128)}, /*in...) custom-call(bf16[1024,128]{1,0:T(8,128)(2,1)} %refs_0_.1, bf16[1024,128]{1,0:T(8,128)(2,1)} %refs_1_.1, ...), custom_call_target="tpu_custom_call" | custom-call | flops 48000000 | bytes 4000000 | tf_op jit(solution)/shard_map/first/pallas_call | solution.py:537
  9.3 0.0 copy-start.3
  9.3 0.0 copy-start.9
  9.3 0.0 copy-start.1
  9.3 13.1 %all-to-all-start = ((bf16[64,12,2,128]{3,2,1,0:T(2,128)(2,1)}), bf16[64,12,2,128]{3,2,1,0:T(2,128)(2,1)S(1)}, u32[]{:S(2)}, u32[]{:S(2)}) async-start(bf16[64,12,2,128]{3,2,1,0:T(2,128)(2,1)} %bitcast.25), calls=%async_computation | async-start | bytes 786432 | tf_op jit(solution)/shard_map/all_to_all | solution.py:591
  22.4 0.0 copy-done.9
  22.4 2.4 %collective-permute-start = (f32[128,128]{1,0:T(8,128)S(1)}, f32[128,128]{1,0:T(8,128)S(1)}, u32[]{:S(2)}, u32[]{:S(2)}) collective-permute-start(f32[128,128]{1,0:T(8,128)S(1)} %copy-done.9), channel_id=1, source_target_pairs={{4,0},{8,4},{12,8},{16,12},{20,16},{24,20},{28,24},{32,28},{36,32}... | collective-permute-start | bytes 196616 | tf_op jit(solution)/shard_map/ppermute | solution.py:594
  24.8 0.0 copy-done.3
  24.8 0.0 copy-done.1
  24.8 0.0 copy-start.6
  24.9 0.0 copy-start.7
  24.9 0.0 copy-start.8
  24.9 1.2 %forward.1.own_out = f32[1024,128]{1,0:T(8,128)S(1)} custom-call(f32[1024,128]{1,0:T(8,128)S(1)} %copy-done.3, f32[320,128]{1,0:T(8,128)S(1)} %copy-done.1), custom_call_target="tpu_custom_call" | custom-call | flops 10000000 | bytes 1000000 | tf_op jit(solution)/shard_map/forward/pallas_call | solution.py:537
  26.1 0.0 copy-start
  26.1 2.9 %collective-permute-done.head = f32[128,128]{1,0:T(8,128)S(1)} collective-permute-done((f32[128,128]{1,0:T(8,128)S(1)}, f32[128,128]{1,0:T(8,128)S(1)}, u32[]{:S(2)}, u32[]{:S(2)}) %collective-permute-start) | collective-permute-done | bytes 65568 | tf_op jit(solution)/shard_map/ppermute | solution.py:594
  29.0 8.5 %all-to-all-done = bf16[64,12,2,128]{3,2,1,0:T(2,128)(2,1)S(1)} async-done(((bf16[64,12,2,128]{3,2,1,0:T(2,128)(2,1)}), bf16[64,12,2,128]{3,2,1,0:T(2,128)(2,1)S(1)}, u32[]{:S(2)}, u32[]{:S(2)}) %all-to-all-start) | async-done | bytes 393248 | tf_op jit(solution)/shard_map/all_to_all | solution.py:591
  37.5 0.0 copy-done.6
  37.5 0.0 copy-done.7
  37.5 0.0 copy-done.8
  37.5 0.9 %owner.1 = bf16[512,128]{1,0:T(8,128)(2,1)S(1)} custom-call(s32[1]{0:T(128)} %bitcast.index, bf16[1536,128]{1,0:T(8,128)(2,1)S(1)} %bitcast.11, f32[16,1024]{1,0:T(8,128)S(1)} %bitcast.16, f32[16,1024]{1,0:T(8,128)S(1)} %bitcast.18, f32[7,1024]{1,0:T(8,128)S(1)} %bitcast.20), custom_call_target="tpu_custom_call" | custom-call | flops 2000000 | bytes 1000000 | tf_op jit(solution)/shard_map/owner/pallas_call | solution.py:537
  38.4 0.0 copy-start.2
  38.5 16.6 %all_to_all.10 = bf16[64,4,2,128]{3,2,1,0:T(2,128)(2,1)S(1)} all-to-all(bf16[64,4,2,128]{3,2,1,0:T(2,128)(2,1)S(1)} %bitcast.14), channel_id=1, replica_groups=mesh['seq'=64,'chan'=4] {'seq'}, dimensions={0} | all-to-all | bytes 262144 | tf_op jit(solution)/shard_map/all_to_all | solution.py:591
  55.1 3.0 %collective-permute-start.1 = (bf16[128,128]{1,0:T(8,128)(2,1)S(1)}, bf16[128,128]{1,0:T(8,128)(2,1)S(1)}, u32[]{:S(2)}, u32[]{:S(2)}) collective-permute-start(bf16[128,128]{1,0:T(8,128)(2,1)S(1)} %bitcast.21), channel_id=1, source_target_pairs={{0,2},{1,3},{2,0},{3,1},{4,6},{5,7},{6,4},{7,5},{8,10},{9,11},{10,... | collective-permute-start | bytes 98312 | tf_op jit(solution)/shard_map/ppermute | solution.py:625
  58.1 0.4 collective-permute-start.2
  58.5 0.4 collective-permute-start.3
  58.9 0.0 copy-done
  58.9 0.0 copy-done.2
  58.9 0.0 copy-start.4
  58.9 0.0 copy-start.5
  58.9 1.3 %query.1 = (bf16[1024,128]{1,0:T(8,128)(2,1)S(1)}, f32[48,128]{1,0:T(8,128)S(1)}, f32[7,1024]{1,0:T(8,128)}) custom-call(bf16[512,128]{1,0:T(8,128)(2,1)S(1)} %bitcast.12, f32[1024,128]{1,0:T(8,128)S(1)} %forward.1.own_out, f32[1024,128]{1,0:T(8,128)S(1)} %copy-done, f32[320,128]{1,0:T(8,128)S(1)} %copy-done.1, bf16[1024,128]{1,0:T(8,128)(2,1)S(1)} %copy-done.2), custom_call_target="tpu_custom_call" | custom-call | flops 5000000 | bytes 1000000 | tf_op jit(solution)/shard_map/query/pallas_call | solution.py:537
  60.2 0.0 copy-done.4
  60.2 0.0 copy-done.5
  60.2 2.1 %key.1 = (bf16[1024,128]{1,0:T(8,128)(2,1)}, bf16[1024,128]{1,0:T(8,128)(2,1)}, bf16[1024,128]{1,0:T(8,128)(2,1)}) custom-call(bf16[512,128]{1,0:T(8,128)(2,1)S(1)} %bitcast.13, f32[1024,128]{1,0:T(8,128)S(1)} %copy-done.4, f32[1024,128]{1,0:T(8,128)S(1)} %copy-done.5, f32[1024,128]{1,0:T(8,128)S(1)} %copy-done, f32[48,128]{1,0:T(8,128)S(1)} %get-tuple-element.34.extra_gate, ...), custom_call_target="tpu_custom_call" | custom-call | flops 8000000 | bytes 2000000 | tf_op jit(solution)/shard_map/key/pallas_call | solution.py:537
  62.4 0.0 collective-permute-done.1.refs_1_
  62.4 0.0 collective-permute-done.2.refs_2_
  62.4 0.1 collective-permute-done.3.refs_3_
  62.5 0.8 %poles.1 = f32[16,1024]{1,0:T(8,128)} custom-call(bf16[128,128]{1,0:T(8,128)(2,1)S(1)} %bitcast.24, bf16[128,128]{1,0:T(8,128)(2,1)S(1)} %collective-permute-done.1.refs_1_, bf16[128,128]{1,0:T(8,128)(2,1)S(1)} %collective-permute-done.2.refs_2_, bf16[128,128]{1,0:T(8,128)(2,1)S(1)} %collective-permute-done.3.refs_3_), custom_call_target="tpu_custom_call" | custom-call | flops 100000 | bytes 100000 | tf_op jit(solution)/shard_map/poles/pallas_call | solution.py:537
  (1 shorter events, 0.0 us)
Async XLA Ops:
  9.3 15.6 %copy-start.3 = (f32[1024,128]{1,0:T(8,128)S(1)}, f32[1024,128]{1,0:T(8,128)}, u32[]{:S(2)}) copy-start(f32[1024,128]{1,0:T(8,128)} %get-tuple-element.26.gated) | copy-start | bytes 1572868
  9.3 13.2 %copy-start.9 = (f32[128,128]{1,0:T(8,128)S(1)}, f32[128,128]{1,0:T(8,128)}, u32[]{:S(2)}) copy-start(f32[128,128]{1,0:T(8,128)} %get-tuple-element.28) | copy-start | bytes 196612
  9.3 15.5 %copy-start.1 = (f32[320,128]{1,0:T(8,128)S(1)}, f32[320,128]{1,0:T(8,128)}, u32[]{:S(2)}) copy-start(f32[320,128]{1,0:T(8,128)} %get-tuple-element.27.par) | copy-start | bytes 491524
  9.3 28.2 %all-to-all-start = ((bf16[64,12,2,128]{3,2,1,0:T(2,128)(2,1)}), bf16[64,12,2,128]{3,2,1,0:T(2,128)(2,1)S(1)}, u32[]{:S(2)}, u32[]{:S(2)}) async-start(bf16[64,12,2,128]{3,2,1,0:T(2,128)(2,1)} %bitcast.25), calls=%async_computation | async-start | bytes 786432 | tf_op jit(solution)/shard_map/all_to_all | solution.py:591
  22.4 6.6 %collective-permute-start = (f32[128,128]{1,0:T(8,128)S(1)}, f32[128,128]{1,0:T(8,128)S(1)}, u32[]{:S(2)}, u32[]{:S(2)}) collective-permute-start(f32[128,128]{1,0:T(8,128)S(1)} %copy-done.9), channel_id=1, source_target_pairs={{4,0},{8,4},{12,8},{16,12},{20,16},{24,20},{28,24},{32,28},{36,32}... | collective-permute-start | bytes 196616 | tf_op jit(solution)/shard_map/ppermute | solution.py:594
  24.8 12.7 %copy-start.6 = (f32[1024,16]{0,1:T(8,128)S(1)}, f32[1024,16]{0,1:T(8,128)}, u32[]{:S(2)}) copy-start(f32[1024,16]{0,1:T(8,128)} %param.13) | copy-start | bytes 196612
  24.9 12.6 %copy-start.7 = (f32[1024,16]{0,1:T(8,128)S(1)}, f32[1024,16]{0,1:T(8,128)}, u32[]{:S(2)}) copy-start(f32[1024,16]{0,1:T(8,128)} %param.12) | copy-start | bytes 196612
  24.9 12.6 %copy-start.8 = (f32[1024,7]{0,1:T(8,128)S(1)}, f32[1024,7]{0,1:T(8,128)}, u32[]{:S(2)}) copy-start(f32[1024,7]{0,1:T(8,128)} %param.11) | copy-start | bytes 86020
  26.1 32.8 %copy-start = (f32[1024,128]{1,0:T(8,128)S(1)}, f32[1024,128]{1,0:T(8,128)}, u32[]{:S(2)}) copy-start(f32[1024,128]{1,0:T(8,128)} %get-tuple-element.32.vt) | copy-start | bytes 1572868
  38.4 20.5 %copy-start.2 = (bf16[1024,128]{1,0:T(8,128)(2,1)S(1)}, bf16[1024,128]{1,0:T(8,128)(2,1)}, u32[]{:S(2)}) copy-start(bf16[1024,128]{1,0:T(8,128)(2,1)} %cot.1) | copy-start | bytes 786436
  55.1 7.2 %collective-permute-start.1 = (bf16[128,128]{1,0:T(8,128)(2,1)S(1)}, bf16[128,128]{1,0:T(8,128)(2,1)S(1)}, u32[]{:S(2)}, u32[]{:S(2)}) collective-permute-start(bf16[128,128]{1,0:T(8,128)(2,1)S(1)} %bitcast.21), channel_id=1, source_target_pairs={{0,2},{1,3},{2,0},{3,1},{4,6},{5,7},{6,4},{7,5},{8,10},{9,11},{10,... | collective-permute-start | bytes 98312 | tf_op jit(solution)/shard_map/ppermute | solution.py:625
  58.1 4.3 %collective-permute-start.2 = (bf16[128,128]{1,0:T(8,128)(2,1)S(1)}, bf16[128,128]{1,0:T(8,128)(2,1)S(1)}, u32[]{:S(2)}, u32[]{:S(2)}) collective-permute-start(bf16[128,128]{1,0:T(8,128)(2,1)S(1)} %bitcast.22), channel_id=1, source_target_pairs={{0,1},{1,0},{2,3},{3,2},{4,5},{5,4},{6,7},{7,6},{8,9},{9,8},{10,11... | collective-permute-start | bytes 98312 | tf_op jit(solution)/shard_map/ppermute | solution.py:625
  58.5 4.0 %collective-permute-start.3 = (bf16[128,128]{1,0:T(8,128)(2,1)S(1)}, bf16[128,128]{1,0:T(8,128)(2,1)S(1)}, u32[]{:S(2)}, u32[]{:S(2)}) collective-permute-start(bf16[128,128]{1,0:T(8,128)(2,1)S(1)} %bitcast.23), channel_id=1, source_target_pairs={{0,3},{1,2},{2,1},{3,0},{4,7},{5,6},{6,5},{7,4},{8,11},{9,10},{10,... | collective-permute-start | bytes 98312 | tf_op jit(solution)/shard_map/ppermute | solution.py:625
  58.9 1.3 %copy-start.4 = (f32[1024,128]{1,0:T(8,128)S(1)}, f32[1024,128]{1,0:T(8,128)}, u32[]{:S(2)}) copy-start(f32[1024,128]{1,0:T(8,128)} %get-tuple-element.30.gate) | copy-start | bytes 1572868
  58.9 1.3 %copy-start.5 = (f32[1024,128]{1,0:T(8,128)S(1)}, f32[1024,128]{1,0:T(8,128)}, u32[]{:S(2)}) copy-start(f32[1024,128]{1,0:T(8,128)} %get-tuple-element.31.local) | copy-start | bytes 1572868

commit v7 on v6

--- a/solution.py
+++ b/solution.py
@@ -440,18 +440,15 @@
     ]
 
 
-def unpack(arrived, x, state, first):
-    x[...] = arrived[...].astype(F32)
+def unpack(x, state, first):
     for s in range(SUB):
         for row in range(2):
             block = x[pl.ds(s * SUB * ROWS_BACK + first + row, SUB, stride=ROWS_BACK), :]
             state[pl.ds(row * SUB * SUB + s, SUB, stride=SUB), :] = from_owner(block)
 
 
-def query_kernel(
-    arrived, own_out, vt, par, cot, grad_q, extra_gate, grad_short, x, state, long_out, last
-):
-    unpack(arrived, x, state, 0)
+def query_part(own_out, vt, par, cot, grad_q, extra_gate, grad_short, x, state, long_out, last):
+    unpack(x, state, 0)
     for s in range(SUB):
         short = x[pl.ds(s * SUB * ROWS_BACK + 6, SUB, stride=ROWS_BACK), :]
         grad_short[:, s * LANES : (s + 1) * LANES] = from_owner(short)[0:TAPS, :]
@@ -477,13 +474,8 @@
         grad_q[rows, :] = (cot[rows, :].astype(F32) * long_out[across(s), :].T).astype(BF16)
 
 
-def key_kernel(
-    arrived, gate, local, vt, extra_gate, head, par, query,
-    grad_k, grad_v, grad_q, x, state, slope, vals, gone,
-):
-    leaving = pltpu.make_async_copy(query, grad_q, gone)
-    leaving.start()
-    unpack(arrived, x, state, 2)
+def key_part(gate, local, vt, extra_gate, head, par, grad_k, grad_v, x, state, slope, vals):
+    unpack(x, state, 2)
     decay = [decay_of(par, r) for r in range(POLES)]
     back = [state[tile(r), :] for r in range(POLES)]
     growth = [1.0 / d for d in decay]
@@ -518,6 +510,17 @@
         rows = slice(s * LANES, (s + 1) * LANES)
         grad_k[rows, :] = slope[across(s), :].T.astype(BF16)
         grad_v[rows, :] = vals[across(s), :].T.astype(BF16)
+
+
+def leave_kernel(
+    arrived, own_out, gate, local, vt, head, par, cot, grad_k, grad_v, grad_short, grad_q,
+    x, state, long_out, last, extra_gate, slope, vals, query, gone,
+):
+    x[...] = arrived[...].astype(F32)
+    query_part(own_out, vt, par, cot, query, extra_gate, grad_short, x, state, long_out, last)
+    leaving = pltpu.make_async_copy(query, grad_q, gone)
+    leaving.start()
+    key_part(gate, local, vt, extra_gate, head, par, grad_k, grad_v, x, state, slope, vals)
     leaving.wait()
 
 
@@ -622,35 +625,27 @@
     returned = returned.reshape(count * ROWS_BACK, LANES)
 
     others = [
-        lax.ppermute(poles, "chan", [(i, i ^ bits) for i in range(chans)]) for bits in (2, 1, 3)
+        lax.ppermute(poles, "chan", [(i, i ^ bits) for i in range(chans)]) for bits in (3, 1, 2)
     ]
 
-    swap = [
-        pltpu.VMEM((count * ROWS_BACK, LANES), F32),
-        pltpu.VMEM((SUB * POLES, LANES), F32),
-    ]
-    query, extra_gate, grad_short = call(
-        query_kernel,
-        "query",
-        [shape(channels, BF16), shape(halo), shape(TAPS, F32, channels)],
-        [*swap, pltpu.VMEM((full, LANES), F32), pltpu.VMEM((edge, LANES), F32)],
-        (returned, own_out, vt, par, cotangent),
-        flops=5 * 10**6,
-        moved=10**6,
-    )
-    grad_k, grad_v, grad_q = call(
-        key_kernel,
-        "key",
-        [shape(channels, BF16)] * 3,
+    grad_k, grad_v, grad_short, grad_q = call(
+        leave_kernel,
+        "leave",
+        [shape(channels, BF16)] * 2 + [shape(TAPS, F32, channels), shape(channels, BF16)],
         [
-            *swap,
+            pltpu.VMEM((count * ROWS_BACK, LANES), F32),
+            pltpu.VMEM((SUB * POLES, LANES), F32),
+            pltpu.VMEM((full, LANES), F32),
+            pltpu.VMEM((edge, LANES), F32),
+            pltpu.VMEM((halo, LANES), F32),
             pltpu.VMEM((full, LANES), F32),
             pltpu.VMEM((full, LANES), F32),
+            pltpu.VMEM((channels, LANES), BF16),
             pltpu.SemaphoreType.DMA,
         ],
-        (returned, gate, local, vt, extra_gate, head, par, query),
-        flops=8 * 10**6,
-        moved=2 * 10**6,
+        (returned, own_out, gate, local, vt, head, par, cotangent),
+        flops=13 * 10**6,
+        moved=3 * 10**6,
         last=pltpu.HBM,
     )
     grad_k, *others = lax.optimization_barrier((grad_k, *others))

time: 63.5 us -> 63.5 us (level)
    pallas_call x6 -> x5, Pallas kernels: 15 us -> 14.6 us  [call(): pl.pallas_call(kernel, out_shape=outs, in_specs=[pl.BlockSpec(memory_spac...]
where the time goes in v7:
time: 63.5 us; the launch traced here: 63.3 us
  starting transfers between devices  19.3 us (30%)
  blocking collectives  16.6 us (26%)
  Pallas kernels  14.6 us (23%)
  waiting for transfers between devices  11.9 us (19%)
  between operations  0.82 us (1%)
    all_to_all x1, blocking collectives, exchange(): return lax.all_to_all(x, 'seq', split_axis=0, concat_axis=0, tiled=True)  16.6 us
    pallas_call x5, Pallas kernels, call(): pl.pallas_call(kernel, out_shape=outs, in_specs=[pl.BlockSpec(memory_spac...  14.6 us
    all_to_all x1, starting transfers between devices, exchange(): return lax.all_to_all(x, 'seq', split_axis=0, concat_axis=0, tiled=True)  13.1 us
    all_to_all x1, waiting for transfers between devices, exchange(): return lax.all_to_all(x, 'seq', split_axis=0, concat_axis=0, tiled=True)  8.49 us
    ppermute x3, starting transfers between devices, per_device(): lax.ppermute(poles, 'chan', [(i, i ^ bits) for i in range(chans)])  3.78 us
    ppermute x1, waiting for transfers between devices, per_device(): head = lax.ppermute(head, 'seq', [(i + 1, i) for i in range(count - 1)])  2.91 us
    ppermute x1, starting transfers between devices, per_device(): head = lax.ppermute(head, 'seq', [(i + 1, i) for i in range(count - 1)])  2.36 us
  transfers between devices with their start and end apart: 5, of which 3 were waited for; matrix products, arithmetic and copies ran while one was open for 0% of the time, Pallas kernels for 7%

profile of v7, /device:TPU:1, one launch (start us, length us, event | category | flops | bytes accessed | tf_op | source)
XLA Modules:
  0.0 63.3 jit_solution(4053092166436745476)
XLA Ops:
  0.6 8.6 %first.1 = (f32[1024,128]{1,0:T(8,128)}, f32[1024,128]{1,0:T(8,128)}, f32[1024,128]{1,0:T(8,128)}, f32[1024,128]{1,0:T(8,128)}, f32[320,128]{1,0:T(8,128)}, /*in...) custom-call(bf16[1024,128]{1,0:T(8,128)(2,1)} %refs_0_.1, bf16[1024,128]{1,0:T(8,128)(2,1)} %refs_1_.1, ...), custom_call_target="tpu_custom_call" | custom-call | flops 48000000 | bytes 4000000 | tf_op jit(solution)/shard_map/first/pallas_call | solution.py:540
  9.3 0.0 copy-start.2
  9.3 0.0 copy-start.9
  9.3 0.0 copy-start.1
  9.3 13.1 %all-to-all-start = ((bf16[64,12,2,128]{3,2,1,0:T(2,128)(2,1)}), bf16[64,12,2,128]{3,2,1,0:T(2,128)(2,1)S(1)}, u32[]{:S(2)}, u32[]{:S(2)}) async-start(bf16[64,12,2,128]{3,2,1,0:T(2,128)(2,1)} %bitcast.24), calls=%async_computation | async-start | bytes 786432 | tf_op jit(solution)/shard_map/all_to_all | solution.py:594
  22.4 0.0 copy-done.9
  22.4 2.4 %collective-permute-start = (f32[128,128]{1,0:T(8,128)S(1)}, f32[128,128]{1,0:T(8,128)S(1)}, u32[]{:S(2)}, u32[]{:S(2)}) collective-permute-start(f32[128,128]{1,0:T(8,128)S(1)} %copy-done.9), channel_id=1, source_target_pairs={{4,0},{8,4},{12,8},{16,12},{20,16},{24,20},{28,24},{32,28},{36,32}... | collective-permute-start | bytes 196616 | tf_op jit(solution)/shard_map/ppermute | solution.py:597
  24.8 0.0 copy-done.2
  24.8 0.0 copy-done.1
  24.8 0.0 copy-start.6
  24.8 0.0 copy-start.7
  24.9 0.0 copy-start.8
  24.9 0.0 copy-start.4
  24.9 0.0 copy-start.5
  24.9 1.2 %forward.1.own_out = f32[1024,128]{1,0:T(8,128)S(1)} custom-call(f32[1024,128]{1,0:T(8,128)S(1)} %copy-done.2, f32[320,128]{1,0:T(8,128)S(1)} %copy-done.1), custom_call_target="tpu_custom_call" | custom-call | flops 10000000 | bytes 1000000 | tf_op jit(solution)/shard_map/forward/pallas_call | solution.py:540
  26.1 0.0 copy-start.3
  26.1 2.9 %collective-permute-done.head = f32[128,128]{1,0:T(8,128)S(1)} collective-permute-done((f32[128,128]{1,0:T(8,128)S(1)}, f32[128,128]{1,0:T(8,128)S(1)}, u32[]{:S(2)}, u32[]{:S(2)}) %collective-permute-start) | collective-permute-done | bytes 65568 | tf_op jit(solution)/shard_map/ppermute | solution.py:597
  29.0 8.5 %all-to-all-done = bf16[64,12,2,128]{3,2,1,0:T(2,128)(2,1)S(1)} async-done(((bf16[64,12,2,128]{3,2,1,0:T(2,128)(2,1)}), bf16[64,12,2,128]{3,2,1,0:T(2,128)(2,1)S(1)}, u32[]{:S(2)}, u32[]{:S(2)}) %all-to-all-start) | async-done | bytes 393248 | tf_op jit(solution)/shard_map/all_to_all | solution.py:594
  37.5 0.0 copy-done.6
  37.5 0.0 copy-done.7
  37.5 0.0 copy-done.8
  37.5 0.9 %owner.1 = bf16[512,128]{1,0:T(8,128)(2,1)S(1)} custom-call(s32[1]{0:T(128)} %bitcast.index, bf16[1536,128]{1,0:T(8,128)(2,1)S(1)} %bitcast.11, f32[16,1024]{1,0:T(8,128)S(1)} %bitcast.15, f32[16,1024]{1,0:T(8,128)S(1)} %bitcast.17, f32[7,1024]{1,0:T(8,128)S(1)} %bitcast.19), custom_call_target="tpu_custom_call" | custom-call | flops 2000000 | bytes 1000000 | tf_op jit(solution)/shard_map/owner/pallas_call | solution.py:540
  38.4 0.0 copy-start
  38.4 16.6 %all_to_all.10 = bf16[64,4,2,128]{3,2,1,0:T(2,128)(2,1)S(1)} all-to-all(bf16[64,4,2,128]{3,2,1,0:T(2,128)(2,1)S(1)} %bitcast.13), channel_id=1, replica_groups=mesh['seq'=64,'chan'=4] {'seq'}, dimensions={0} | all-to-all | bytes 262144 | tf_op jit(solution)/shard_map/all_to_all | solution.py:594
  55.1 3.0 %collective-permute-start.3 = (bf16[128,128]{1,0:T(8,128)(2,1)S(1)}, bf16[128,128]{1,0:T(8,128)(2,1)S(1)}, u32[]{:S(2)}, u32[]{:S(2)}) collective-permute-start(bf16[128,128]{1,0:T(8,128)(2,1)S(1)} %bitcast.20), channel_id=1, source_target_pairs={{0,2},{1,3},{2,0},{3,1},{4,6},{5,7},{6,4},{7,5},{8,10},{9,11},{10,... | collective-permute-start | bytes 98312 | tf_op jit(solution)/shard_map/ppermute | solution.py:628
  58.1 0.4 collective-permute-start.2
  58.5 0.4 collective-permute-start.1
  58.9 0.0 copy-done.4
  58.9 0.0 copy-done.5
  58.9 0.0 copy-done.3
  58.9 0.0 copy-done
  58.9 3.1 %leave.1 = (bf16[1024,128]{1,0:T(8,128)(2,1)}, bf16[1024,128]{1,0:T(8,128)(2,1)}, f32[7,1024]{1,0:T(8,128)}, bf16[1024,128]{1,0:T(8,128)(2,1)}) custom-call(bf16[512,128]{1,0:T(8,128)(2,1)S(1)} %bitcast.12, f32[1024,128]{1,0:T(8,128)S(1)} %forward.1.own_out, f32[1024,128]{1,0:T(8,128)S(1)} %copy-done.4, f32[1024,128]{1,0:T(8,128)S(1)} %copy-done.5, ...), custom_call_target="tpu_custom_call" | custom-call | flops 13000000 | bytes 3000000 | tf_op jit(solution)/shard_map/leave/pallas_call | solution.py:540
  62.0 0.0 collective-permute-done.3.refs_3_
  62.0 0.0 collective-permute-done.2.refs_2_
  62.0 0.5 collective-permute-done.1.refs_1_
  62.5 0.8 %poles.1 = f32[16,1024]{1,0:T(8,128)} custom-call(bf16[128,128]{1,0:T(8,128)(2,1)S(1)} %bitcast.23, bf16[128,128]{1,0:T(8,128)(2,1)S(1)} %collective-permute-done.1.refs_1_, bf16[128,128]{1,0:T(8,128)(2,1)S(1)} %collective-permute-done.2.refs_2_, bf16[128,128]{1,0:T(8,128)(2,1)S(1)} %collective-permute-done.3.refs_3_), custom_call_target="tpu_custom_call" | custom-call | flops 100000 | bytes 100000 | tf_op jit(solution)/shard_map/poles/pallas_call | solution.py:540
  (1 shorter events, 0.0 us)
Async XLA Ops:
  9.3 15.6 %copy-start.2 = (f32[1024,128]{1,0:T(8,128)S(1)}, f32[1024,128]{1,0:T(8,128)}, u32[]{:S(2)}) copy-start(f32[1024,128]{1,0:T(8,128)} %get-tuple-element.24.gated) | copy-start | bytes 1572868
  9.3 13.2 %copy-start.9 = (f32[128,128]{1,0:T(8,128)S(1)}, f32[128,128]{1,0:T(8,128)}, u32[]{:S(2)}) copy-start(f32[128,128]{1,0:T(8,128)} %get-tuple-element.26) | copy-start | bytes 196612
  9.3 15.5 %copy-start.1 = (f32[320,128]{1,0:T(8,128)S(1)}, f32[320,128]{1,0:T(8,128)}, u32[]{:S(2)}) copy-start(f32[320,128]{1,0:T(8,128)} %get-tuple-element.25.par) | copy-start | bytes 491524
  9.3 28.2 %all-to-all-start = ((bf16[64,12,2,128]{3,2,1,0:T(2,128)(2,1)}), bf16[64,12,2,128]{3,2,1,0:T(2,128)(2,1)S(1)}, u32[]{:S(2)}, u32[]{:S(2)}) async-start(bf16[64,12,2,128]{3,2,1,0:T(2,128)(2,1)} %bitcast.24), calls=%async_computation | async-start | bytes 786432 | tf_op jit(solution)/shard_map/all_to_all | solution.py:594
  22.4 6.6 %collective-permute-start = (f32[128,128]{1,0:T(8,128)S(1)}, f32[128,128]{1,0:T(8,128)S(1)}, u32[]{:S(2)}, u32[]{:S(2)}) collective-permute-start(f32[128,128]{1,0:T(8,128)S(1)} %copy-done.9), channel_id=1, source_target_pairs={{4,0},{8,4},{12,8},{16,12},{20,16},{24,20},{28,24},{32,28},{36,32}... | collective-permute-start | bytes 196616 | tf_op jit(solution)/shard_map/ppermute | solution.py:597
  24.8 12.7 %copy-start.6 = (f32[1024,16]{0,1:T(8,128)S(1)}, f32[1024,16]{0,1:T(8,128)}, u32[]{:S(2)}) copy-start(f32[1024,16]{0,1:T(8,128)} %param.13) | copy-start | bytes 196612
  24.8 12.6 %copy-start.7 = (f32[1024,16]{0,1:T(8,128)S(1)}, f32[1024,16]{0,1:T(8,128)}, u32[]{:S(2)}) copy-start(f32[1024,16]{0,1:T(8,128)} %param.12) | copy-start | bytes 196612
  24.9 12.6 %copy-start.8 = (f32[1024,7]{0,1:T(8,128)S(1)}, f32[1024,7]{0,1:T(8,128)}, u32[]{:S(2)}) copy-start(f32[1024,7]{0,1:T(8,128)} %param.11) | copy-start | bytes 86020
  24.9 34.0 %copy-start.4 = (f32[1024,128]{1,0:T(8,128)S(1)}, f32[1024,128]{1,0:T(8,128)}, u32[]{:S(2)}) copy-start(f32[1024,128]{1,0:T(8,128)} %get-tuple-element.29.gate) | copy-start | bytes 1572868
  24.9 34.0 %copy-start.5 = (f32[1024,128]{1,0:T(8,128)S(1)}, f32[1024,128]{1,0:T(8,128)}, u32[]{:S(2)}) copy-start(f32[1024,128]{1,0:T(8,128)} %get-tuple-element.30.local) | copy-start | bytes 1572868
  26.1 32.8 %copy-start.3 = (f32[1024,128]{1,0:T(8,128)S(1)}, f32[1024,128]{1,0:T(8,128)}, u32[]{:S(2)}) copy-start(f32[1024,128]{1,0:T(8,128)} %get-tuple-element.31.vt) | copy-start | bytes 1572868
  38.4 20.5 %copy-start = (bf16[1024,128]{1,0:T(8,128)(2,1)S(1)}, bf16[1024,128]{1,0:T(8,128)(2,1)}, u32[]{:S(2)}) copy-start(bf16[1024,128]{1,0:T(8,128)(2,1)} %cot.1) | copy-start | bytes 786436
  55.1 6.9 %collective-permute-start.3 = (bf16[128,128]{1,0:T(8,128)(2,1)S(1)}, bf16[128,128]{1,0:T(8,128)(2,1)S(1)}, u32[]{:S(2)}, u32[]{:S(2)}) collective-permute-start(bf16[128,128]{1,0:T(8,128)(2,1)S(1)} %bitcast.20), channel_id=1, source_target_pairs={{0,2},{1,3},{2,0},{3,1},{4,6},{5,7},{6,4},{7,5},{8,10},{9,11},{10,... | collective-permute-start | bytes 98312 | tf_op jit(solution)/shard_map/ppermute | solution.py:628
  58.1 3.9 %collective-permute-start.2 = (bf16[128,128]{1,0:T(8,128)(2,1)S(1)}, bf16[128,128]{1,0:T(8,128)(2,1)S(1)}, u32[]{:S(2)}, u32[]{:S(2)}) collective-permute-start(bf16[128,128]{1,0:T(8,128)(2,1)S(1)} %bitcast.21), channel_id=1, source_target_pairs={{0,1},{1,0},{2,3},{3,2},{4,5},{5,4},{6,7},{7,6},{8,9},{9,8},{10,11... | collective-permute-start | bytes 98312 | tf_op jit(solution)/shard_map/ppermute | solution.py:628
  58.5 4.0 %collective-permute-start.1 = (bf16[128,128]{1,0:T(8,128)(2,1)S(1)}, bf16[128,128]{1,0:T(8,128)(2,1)S(1)}, u32[]{:S(2)}, u32[]{:S(2)}) collective-permute-start(bf16[128,128]{1,0:T(8,128)(2,1)S(1)} %bitcast.22), channel_id=1, source_target_pairs={{0,3},{1,2},{2,1},{3,0},{4,7},{5,6},{6,5},{7,4},{8,11},{9,10},{10,... | collective-permute-start | bytes 98312 | tf_op jit(solution)/shard_map/ppermute | solution.py:628

commit v8 on v7

--- a/solution.py
+++ b/solution.py
@@ -270,12 +270,20 @@
     leaving[2].start()
     scan_down(par, zt, vt, gated, keys, local, gather)
     leaving[3].start()
-    for row in range(ROWS_OUT):
-        for s in range(SUB):
-            block = to_owner(gather[pl.ds(row * SUB * SUB + s, SUB, stride=SUB), :])
-            spread[pl.ds(s * SUB * ROWS_OUT + row, SUB, stride=ROWS_OUT), :] = block
-    message[...] = spread[...].astype(BF16)
-    leaving[6].start()
+    size = message.shape[0] // 2
+    halves = []
+    for n in range(2):
+        for s in range(n * SUB // 2, (n + 1) * SUB // 2):
+            for row in range(ROWS_OUT):
+                block = to_owner(gather[pl.ds(row * SUB * SUB + s, SUB, stride=SUB), :])
+                spread[pl.ds(s * SUB * ROWS_OUT + row, SUB, stride=ROWS_OUT), :] = block
+        part = pl.ds(n * size, size)
+        message[part, :] = spread[part, :].astype(BF16)
+        halves.append(
+            pltpu.make_async_copy(message.at[part, :], targets[-1].at[part, :], went.at[6 + n])
+        )
+        halves[-1].start()
+    leaving = [*leaving[:-1], *halves]
     for copy in leaving:
         copy.wait()
 
@@ -580,7 +588,7 @@
             pltpu.VMEM((SUB * SUB * ROWS_OUT, LANES), F32),
             pltpu.VMEM((count * ROWS_OUT, LANES), F32),
             pltpu.SemaphoreType.DMA((len(operands),)),
-            pltpu.SemaphoreType.DMA((len(outs),)),
+            pltpu.SemaphoreType.DMA((len(outs) + 1,)),
         ],
         operands,
         flops=48 * 10**6,

time: 63.5 us -> 63.5 us (level)
  no operation moved by 1% of the time
where the time goes in v8:
time: 63.5 us; the launch traced here: 63.2 us
  starting transfers between devices  19.3 us (30%)
  blocking collectives  16.6 us (26%)
  Pallas kernels  14.5 us (23%)
  waiting for transfers between devices  11.9 us (19%)
  between operations  0.82 us (1%)
    all_to_all x1, blocking collectives, exchange(): return lax.all_to_all(x, 'seq', split_axis=0, concat_axis=0, tiled=True)  16.6 us
    pallas_call x5, Pallas kernels, call(): pl.pallas_call(kernel, out_shape=outs, in_specs=[pl.BlockSpec(memory_spac...  14.5 us
    all_to_all x1, starting transfers between devices, exchange(): return lax.all_to_all(x, 'seq', split_axis=0, concat_axis=0, tiled=True)  13.1 us
    all_to_all x1, waiting for transfers between devices, exchange(): return lax.all_to_all(x, 'seq', split_axis=0, concat_axis=0, tiled=True)  8.49 us
    ppermute x3, starting transfers between devices, per_device(): lax.ppermute(poles, 'chan', [(i, i ^ bits) for i in range(chans)])  3.78 us
    ppermute x1, waiting for transfers between devices, per_device(): head = lax.ppermute(head, 'seq', [(i + 1, i) for i in range(count - 1)])  2.91 us
    ppermute x1, starting transfers between devices, per_device(): head = lax.ppermute(head, 'seq', [(i + 1, i) for i in range(count - 1)])  2.36 us
  transfers between devices with their start and end apart: 5, of which 3 were waited for; matrix products, arithmetic and copies ran while one was open for 0% of the time, Pallas kernels for 7%

profile of v8, /device:TPU:1, one launch (start us, length us, event | category | flops | bytes accessed | tf_op | source)
XLA Modules:
  0.0 63.2 jit_solution(5330629728741998042)
XLA Ops:
  0.6 8.6 %first.1 = (f32[1024,128]{1,0:T(8,128)}, f32[1024,128]{1,0:T(8,128)}, f32[1024,128]{1,0:T(8,128)}, f32[1024,128]{1,0:T(8,128)}, f32[320,128]{1,0:T(8,128)}, /*in...) custom-call(bf16[1024,128]{1,0:T(8,128)(2,1)} %refs_0_.1, bf16[1024,128]{1,0:T(8,128)(2,1)} %refs_1_.1, ...), custom_call_target="tpu_custom_call" | custom-call | flops 48000000 | bytes 4000000 | tf_op jit(solution)/shard_map/first/pallas_call | solution.py:548
  9.2 0.0 copy-start.2
  9.2 0.0 copy-start.9
  9.2 0.0 copy-start.1
  9.2 13.1 %all-to-all-start = ((bf16[64,12,2,128]{3,2,1,0:T(2,128)(2,1)}), bf16[64,12,2,128]{3,2,1,0:T(2,128)(2,1)S(1)}, u32[]{:S(2)}, u32[]{:S(2)}) async-start(bf16[64,12,2,128]{3,2,1,0:T(2,128)(2,1)} %bitcast.24), calls=%async_computation | async-start | bytes 786432 | tf_op jit(solution)/shard_map/all_to_all | solution.py:602
  22.4 0.0 copy-done.9
  22.4 2.4 %collective-permute-start = (f32[128,128]{1,0:T(8,128)S(1)}, f32[128,128]{1,0:T(8,128)S(1)}, u32[]{:S(2)}, u32[]{:S(2)}) collective-permute-start(f32[128,128]{1,0:T(8,128)S(1)} %copy-done.9), channel_id=1, source_target_pairs={{4,0},{8,4},{12,8},{16,12},{20,16},{24,20},{28,24},{32,28},{36,32}... | collective-permute-start | bytes 196616 | tf_op jit(solution)/shard_map/ppermute | solution.py:605
  24.8 0.0 copy-done.2
  24.8 0.0 copy-done.1
  24.8 0.0 copy-start.6
  24.8 0.0 copy-start.7
  24.8 0.0 copy-start.8
  24.8 0.0 copy-start.4
  24.8 0.0 copy-start.5
  24.8 1.2 %forward.1.own_out = f32[1024,128]{1,0:T(8,128)S(1)} custom-call(f32[1024,128]{1,0:T(8,128)S(1)} %copy-done.2, f32[320,128]{1,0:T(8,128)S(1)} %copy-done.1), custom_call_target="tpu_custom_call" | custom-call | flops 10000000 | bytes 1000000 | tf_op jit(solution)/shard_map/forward/pallas_call | solution.py:548
  26.0 0.0 copy-start.3
  26.0 2.9 %collective-permute-done.head = f32[128,128]{1,0:T(8,128)S(1)} collective-permute-done((f32[128,128]{1,0:T(8,128)S(1)}, f32[128,128]{1,0:T(8,128)S(1)}, u32[]{:S(2)}, u32[]{:S(2)}) %collective-permute-start) | collective-permute-done | bytes 65568 | tf_op jit(solution)/shard_map/ppermute | solution.py:605
  29.0 8.5 %all-to-all-done = bf16[64,12,2,128]{3,2,1,0:T(2,128)(2,1)S(1)} async-done(((bf16[64,12,2,128]{3,2,1,0:T(2,128)(2,1)}), bf16[64,12,2,128]{3,2,1,0:T(2,128)(2,1)S(1)}, u32[]{:S(2)}, u32[]{:S(2)}) %all-to-all-start) | async-done | bytes 393248 | tf_op jit(solution)/shard_map/all_to_all | solution.py:602
  37.4 0.0 copy-done.6
  37.4 0.0 copy-done.7
  37.4 0.0 copy-done.8
  37.5 0.9 %owner.1 = bf16[512,128]{1,0:T(8,128)(2,1)S(1)} custom-call(s32[1]{0:T(128)} %bitcast.index, bf16[1536,128]{1,0:T(8,128)(2,1)S(1)} %bitcast.11, f32[16,1024]{1,0:T(8,128)S(1)} %bitcast.15, f32[16,1024]{1,0:T(8,128)S(1)} %bitcast.17, f32[7,1024]{1,0:T(8,128)S(1)} %bitcast.19), custom_call_target="tpu_custom_call" | custom-call | flops 2000000 | bytes 1000000 | tf_op jit(solution)/shard_map/owner/pallas_call | solution.py:548
  38.4 0.0 copy-start
  38.4 16.6 %all_to_all.10 = bf16[64,4,2,128]{3,2,1,0:T(2,128)(2,1)S(1)} all-to-all(bf16[64,4,2,128]{3,2,1,0:T(2,128)(2,1)S(1)} %bitcast.13), channel_id=1, replica_groups=mesh['seq'=64,'chan'=4] {'seq'}, dimensions={0} | all-to-all | bytes 262144 | tf_op jit(solution)/shard_map/all_to_all | solution.py:602
  55.1 3.0 %collective-permute-start.3 = (bf16[128,128]{1,0:T(8,128)(2,1)S(1)}, bf16[128,128]{1,0:T(8,128)(2,1)S(1)}, u32[]{:S(2)}, u32[]{:S(2)}) collective-permute-start(bf16[128,128]{1,0:T(8,128)(2,1)S(1)} %bitcast.20), channel_id=1, source_target_pairs={{0,2},{1,3},{2,0},{3,1},{4,6},{5,7},{6,4},{7,5},{8,10},{9,11},{10,... | collective-permute-start | bytes 98312 | tf_op jit(solution)/shard_map/ppermute | solution.py:636
  58.1 0.4 collective-permute-start.2
  58.5 0.4 collective-permute-start.1
  58.8 0.0 copy-done.4
  58.8 0.0 copy-done.5
  58.8 0.0 copy-done.3
  58.9 0.0 copy-done
  58.9 3.1 %leave.1 = (bf16[1024,128]{1,0:T(8,128)(2,1)}, bf16[1024,128]{1,0:T(8,128)(2,1)}, f32[7,1024]{1,0:T(8,128)}, bf16[1024,128]{1,0:T(8,128)(2,1)}) custom-call(bf16[512,128]{1,0:T(8,128)(2,1)S(1)} %bitcast.12, f32[1024,128]{1,0:T(8,128)S(1)} %forward.1.own_out, f32[1024,128]{1,0:T(8,128)S(1)} %copy-done.4, f32[1024,128]{1,0:T(8,128)S(1)} %copy-done.5, ...), custom_call_target="tpu_custom_call" | custom-call | flops 13000000 | bytes 3000000 | tf_op jit(solution)/shard_map/leave/pallas_call | solution.py:548
  61.9 0.0 collective-permute-done.3.refs_3_
  61.9 0.0 collective-permute-done.2.refs_2_
  62.0 0.5 collective-permute-done.1.refs_1_
  62.4 0.8 %poles.1 = f32[16,1024]{1,0:T(8,128)} custom-call(bf16[128,128]{1,0:T(8,128)(2,1)S(1)} %bitcast.23, bf16[128,128]{1,0:T(8,128)(2,1)S(1)} %collective-permute-done.1.refs_1_, bf16[128,128]{1,0:T(8,128)(2,1)S(1)} %collective-permute-done.2.refs_2_, bf16[128,128]{1,0:T(8,128)(2,1)S(1)} %collective-permute-done.3.refs_3_), custom_call_target="tpu_custom_call" | custom-call | flops 100000 | bytes 100000 | tf_op jit(solution)/shard_map/poles/pallas_call | solution.py:548
  (1 shorter events, 0.0 us)
Async XLA Ops:
  9.2 15.6 %copy-start.2 = (f32[1024,128]{1,0:T(8,128)S(1)}, f32[1024,128]{1,0:T(8,128)}, u32[]{:S(2)}) copy-start(f32[1024,128]{1,0:T(8,128)} %get-tuple-element.24.gated) | copy-start | bytes 1572868
  9.2 13.2 %copy-start.9 = (f32[128,128]{1,0:T(8,128)S(1)}, f32[128,128]{1,0:T(8,128)}, u32[]{:S(2)}) copy-start(f32[128,128]{1,0:T(8,128)} %get-tuple-element.26) | copy-start | bytes 196612
  9.2 15.5 %copy-start.1 = (f32[320,128]{1,0:T(8,128)S(1)}, f32[320,128]{1,0:T(8,128)}, u32[]{:S(2)}) copy-start(f32[320,128]{1,0:T(8,128)} %get-tuple-element.25.par) | copy-start | bytes 491524
  9.2 28.2 %all-to-all-start = ((bf16[64,12,2,128]{3,2,1,0:T(2,128)(2,1)}), bf16[64,12,2,128]{3,2,1,0:T(2,128)(2,1)S(1)}, u32[]{:S(2)}, u32[]{:S(2)}) async-start(bf16[64,12,2,128]{3,2,1,0:T(2,128)(2,1)} %bitcast.24), calls=%async_computation | async-start | bytes 786432 | tf_op jit(solution)/shard_map/all_to_all | solution.py:602
  22.4 6.6 %collective-permute-start = (f32[128,128]{1,0:T(8,128)S(1)}, f32[128,128]{1,0:T(8,128)S(1)}, u32[]{:S(2)}, u32[]{:S(2)}) collective-permute-start(f32[128,128]{1,0:T(8,128)S(1)} %copy-done.9), channel_id=1, source_target_pairs={{4,0},{8,4},{12,8},{16,12},{20,16},{24,20},{28,24},{32,28},{36,32}... | collective-permute-start | bytes 196616 | tf_op jit(solution)/shard_map/ppermute | solution.py:605
  24.8 12.7 %copy-start.6 = (f32[1024,16]{0,1:T(8,128)S(1)}, f32[1024,16]{0,1:T(8,128)}, u32[]{:S(2)}) copy-start(f32[1024,16]{0,1:T(8,128)} %param.13) | copy-start | bytes 196612
  24.8 12.6 %copy-start.7 = (f32[1024,16]{0,1:T(8,128)S(1)}, f32[1024,16]{0,1:T(8,128)}, u32[]{:S(2)}) copy-start(f32[1024,16]{0,1:T(8,128)} %param.12) | copy-start | bytes 196612
  24.8 12.6 %copy-start.8 = (f32[1024,7]{0,1:T(8,128)S(1)}, f32[1024,7]{0,1:T(8,128)}, u32[]{:S(2)}) copy-start(f32[1024,7]{0,1:T(8,128)} %param.11) | copy-start | bytes 86020
  24.8 34.0 %copy-start.4 = (f32[1024,128]{1,0:T(8,128)S(1)}, f32[1024,128]{1,0:T(8,128)}, u32[]{:S(2)}) copy-start(f32[1024,128]{1,0:T(8,128)} %get-tuple-element.29.gate) | copy-start | bytes 1572868
  24.8 34.0 %copy-start.5 = (f32[1024,128]{1,0:T(8,128)S(1)}, f32[1024,128]{1,0:T(8,128)}, u32[]{:S(2)}) copy-start(f32[1024,128]{1,0:T(8,128)} %get-tuple-element.30.local) | copy-start | bytes 1572868
  26.0 32.8 %copy-start.3 = (f32[1024,128]{1,0:T(8,128)S(1)}, f32[1024,128]{1,0:T(8,128)}, u32[]{:S(2)}) copy-start(f32[1024,128]{1,0:T(8,128)} %get-tuple-element.31.vt) | copy-start | bytes 1572868
  38.4 20.5 %copy-start = (bf16[1024,128]{1,0:T(8,128)(2,1)S(1)}, bf16[1024,128]{1,0:T(8,128)(2,1)}, u32[]{:S(2)}) copy-start(bf16[1024,128]{1,0:T(8,128)(2,1)} %cot.1) | copy-start | bytes 786436
  55.1 6.9 %collective-permute-start.3 = (bf16[128,128]{1,0:T(8,128)(2,1)S(1)}, bf16[128,128]{1,0:T(8,128)(2,1)S(1)}, u32[]{:S(2)}, u32[]{:S(2)}) collective-permute-start(bf16[128,128]{1,0:T(8,128)(2,1)S(1)} %bitcast.20), channel_id=1, source_target_pairs={{0,2},{1,3},{2,0},{3,1},{4,6},{5,7},{6,4},{7,5},{8,10},{9,11},{10,... | collective-permute-start | bytes 98312 | tf_op jit(solution)/shard_map/ppermute | solution.py:636
  58.1 3.9 %collective-permute-start.2 = (bf16[128,128]{1,0:T(8,128)(2,1)S(1)}, bf16[128,128]{1,0:T(8,128)(2,1)S(1)}, u32[]{:S(2)}, u32[]{:S(2)}) collective-permute-start(bf16[128,128]{1,0:T(8,128)(2,1)S(1)} %bitcast.21), channel_id=1, source_target_pairs={{0,1},{1,0},{2,3},{3,2},{4,5},{5,4},{6,7},{7,6},{8,9},{9,8},{10,11... | collective-permute-start | bytes 98312 | tf_op jit(solution)/shard_map/ppermute | solution.py:636
  58.5 4.0 %collective-permute-start.1 = (bf16[128,128]{1,0:T(8,128)(2,1)S(1)}, bf16[128,128]{1,0:T(8,128)(2,1)S(1)}, u32[]{:S(2)}, u32[]{:S(2)}) collective-permute-start(bf16[128,128]{1,0:T(8,128)(2,1)S(1)} %bitcast.22), channel_id=1, source_target_pairs={{0,3},{1,2},{2,1},{3,0},{4,7},{5,6},{6,5},{7,4},{8,11},{9,10},{10,... | collective-permute-start | bytes 98312 | tf_op jit(solution)/shard_map/ppermute | solution.py:636
